TPU v7x, 128 devices: a whole 4x4x4 slice. The times are simulated.
128 devices in a mesh: seq: 64 (over x, z, y_hi, core), batch: 2 (over y_lo).
Axes of the slice: x: 4, y: 4 (y_hi: 2, y_lo: 2; y = y_hi * 2 + y_lo), z: 4, core: 2. Of those that a mesh axis runs over, the one named last changes fastest.
Arguments:
- inputs: bfloat16 [8, 16384, 768], P('batch', 'seq'), may hold values from -6 to 6
- cotangent: bfloat16 [8, 16384, 768], P('batch', 'seq'), may hold values from -16 to 16
- conv_weight: bfloat16 [2, 3, 768, 384], replicated, may hold values from -0.125 to 0.125
- proj_weight: bfloat16 [2, 384, 768], replicated, may hold values from -0.3125 to 0.3125
Outputs:
- outputs: bfloat16 [8, 16384, 768], P('batch', 'seq')
- input_grad: bfloat16 [8, 16384, 768], P('batch', 'seq')
- conv_grad: float32 [2, 3, 768, 384], P(None, None, ('seq', 'batch'))
- proj_grad: float32 [2, 384, 768], P(None, None, ('seq', 'batch'))
All inputs are finite; a program needn't handle non-finite values.
Results may differ from a plain program's by a relative error of at most 0.015.
Values may be sent and summed in bfloat16 or wider, within the bound.
No kernel may reach another device: no remote copies, remote signals or barrier semaphores. Data moves between devices by JAX's collectives and lax.ppermute only.
A program may use at most 128 MiB of HBM per device.

v0:
```python
import functools
import math

import jax
import jax.numpy as jnp
from jax import lax
from jax.experimental import pallas as pl
from jax.experimental.pallas import tpu as pltpu
from jax.sharding import Mesh
from jax.sharding import PartitionSpec as P

RING = ("x", "z")
COLUMN = ("yh", "yl")
SEQ = ("x", "z", "yh", "c")
BF = jnp.bfloat16
F32 = jnp.float32
BLOCK = 256
VMEM_BYTES = 56 * 1024 * 1024


def gelu_parts(value):
    cdf = 0.5 * (1.0 + lax.erf(value * (1.0 / math.sqrt(2.0))))
    density = jnp.exp(-0.5 * value * value) * (1.0 / math.sqrt(2.0 * math.pi))
    return (value * cdf).astype(BF), (cdf + value * density).astype(BF)


def dot(left, right):
    return jnp.dot(left, right, preferred_element_type=F32)


def dot_t(left, right):
    return lax.dot_general(left, right, (((1,), (1,)), ((), ())), preferred_element_type=F32)


def dot_rows(left, right):
    return lax.dot_general(left, right, (((0,), (0,)), ((), ())), preferred_element_type=F32)


def ring_rows(ref, start, count):
    total = ref.shape[0]
    start %= total
    if start + count <= total:
        return ref[start : start + count, :]
    first = total - start
    return jnp.concatenate([ref[start:total, :], ref[: count - first, :]], axis=0)


def forward_kernel(step, x_ref, conv_ref, proj_ref, *refs):
    out_ref, saved, mid_ref = refs[0], (refs[1:5], refs[5:9]), refs[9]
    total = x_ref.shape[0]
    starts = range(0, total, BLOCK)

    def enter(b, start, value):
        rows = slice(start, start + BLOCK)
        feature, slope = gelu_parts(value)
        saved[b][0][rows, :] = feature
        saved[b][1][rows, :] = slope

    for start in starts:
        enter(0, start, x_ref[start : start + BLOCK, :].astype(F32))
    for b in range(2):
        feature_ref, _, activ_ref, slope_ref = saved[b]
        source = x_ref if b == 0 else mid_ref
        shift = step * 2**b
        for start in starts:
            rows = slice(start, start + BLOCK)
            pre = (
                dot(ring_rows(feature_ref, start - shift, BLOCK), conv_ref[b, 0])
                + dot(feature_ref[rows, :], conv_ref[b, 1])
                + dot(ring_rows(feature_ref, start + shift, BLOCK), conv_ref[b, 2])
            )
            activ, slope = gelu_parts(pre)
            activ_ref[rows, :] = activ
            slope_ref[rows, :] = slope
            after = (source[rows, :].astype(F32) + dot(activ, proj_ref[b])).astype(BF)
            if b == 0:
                mid_ref[rows, :] = after
                enter(1, start, after.astype(F32))
            else:
                out_ref[rows, :] = after


def forward(state, conv, proj, step):
    total, chans = state.shape
    mids = conv.shape[-1]
    wide = jax.ShapeDtypeStruct((total, chans), BF)
    thin = jax.ShapeDtypeStruct((total, mids), BF)
    outs = pl.pallas_call(
        functools.partial(forward_kernel, step),
        out_shape=[wide] + [wide, wide, thin, thin] * 2,
        scratch_shapes=[pltpu.VMEM((total, chans), BF)],
        compiler_params=pltpu.CompilerParams(vmem_limit_bytes=VMEM_BYTES),
        name="forward",
    )(state, conv, proj)
    return outs[0], (outs[1:5], outs[5:9])


def backward_kernel(
    b, step, place_ref, grad_ref, feature_ref, slope_in_ref, activ_ref, slope_ref,
    conv_ref, proj_ref, out_ref, part_ref, e_ref, taps_ref, sum_ref, order_ref,
):
    total, mids = e_ref.shape
    chans = grad_ref.shape[1]
    shift = step * 2**b
    starts = range(0, total, BLOCK)
    for start in starts:
        rows = slice(start, start + BLOCK)
        back = dot_t(grad_ref[rows, :], proj_ref[b])
        e_ref[rows, :] = (back * slope_ref[rows, :].astype(F32)).astype(BF)
    for start in starts:
        rows = slice(start, start + BLOCK)
        taps_ref[rows, :mids] = ring_rows(e_ref, start + shift, BLOCK)
        taps_ref[rows, mids : 2 * mids] = e_ref[rows, :]
        taps_ref[rows, 2 * mids :] = ring_rows(e_ref, start - shift, BLOCK)
    for first in range(0, chans, BLOCK):
        some = slice(first, first + BLOCK)
        sum_ref[some, : 3 * mids] = dot_rows(feature_ref[:, some], taps_ref[...])
        sum_ref[some, 3 * mids :] = dot_rows(grad_ref[:, some], activ_ref[...])
    for start in starts:
        rows = slice(start, start + BLOCK)
        summed = sum(
            dot_t(taps_ref[rows, k * mids : (k + 1) * mids], conv_ref[b, k]) for k in range(3)
        )
        grown = grad_ref[rows, :].astype(F32) + summed * slope_in_ref[rows, :].astype(F32)
        out_ref[rows, :] = grown.astype(BF)
    share = chans // 128
    for c in range(2):
        for y in range(4):
            for ring in range(16):
                owner = ((ring * 2 + y // 2) * 2 + c) * 2 + y % 2
                order_ref[ring * share : (ring + 1) * share, :] = sum_ref[
                    owner * share : (owner + 1) * share, :
                ]
            half = (c + place_ref[0]) % 2
            part_ref[half, (y + 4 - place_ref[1]) % 4] = order_ref[...].astype(BF)


def backward(b, grad, saved, conv, proj, step, place):
    total, chans = grad.shape
    mids = conv.shape[-1]
    vmem = pl.BlockSpec(memory_space=pltpu.VMEM)
    rows = 16 * (chans // 128)
    return pl.pallas_call(
        functools.partial(backward_kernel, b, step),
        out_shape=[
            jax.ShapeDtypeStruct((total, chans), BF),
            jax.ShapeDtypeStruct((2, 4, rows, 4 * mids), BF),
        ],
        in_specs=[pl.BlockSpec(memory_space=pltpu.SMEM)] + [vmem] * 7,
        scratch_shapes=[
            pltpu.VMEM((total, mids), BF),
            pltpu.VMEM((total, 3 * mids), BF),
            pltpu.VMEM((chans, 4 * mids), F32),
            pltpu.VMEM((rows, 4 * mids), F32),
        ],
        compiler_params=pltpu.CompilerParams(vmem_limit_bytes=VMEM_BYTES),
        name="backward%d" % b,
    )(place, grad, *saved, conv, proj)


def to_rings(block):
    return lax.all_to_all(block, RING, 0, 0, tiled=True)


def passed(block, axis, distance):
    size = lax.axis_size(axis)
    return lax.ppermute(block, axis, [(i, (i + distance) % size) for i in range(size)])


def total_of(parts):
    out = parts[0].astype(F32)
    for part in parts[1:]:
        out = out + part.astype(F32)
    return out


def share_of(part):
    both = total_of([part[0], passed(part[1], "c", 1)]).astype(BF)
    both = total_of([both[0]] + [passed(both[k], COLUMN, k) for k in (1, 3, 2)]).astype(BF)
    for axis in RING:
        pieces = both.reshape(4, -1, both.shape[-1])
        me = lax.axis_index(axis)

        def piece(k):
            return lax.dynamic_index_in_dim(pieces, (me + k) % 4, 0, keepdims=False)

        both = total_of([piece(0)] + [passed(piece(k), axis, k) for k in (1, 3, 2)])
        if axis == "x":
            both = both.astype(BF)
    return both


def local(inputs, cotangent, conv, proj):
    genomes, bins, chans = inputs.shape
    total = genomes * bins
    step = total // 16
    mids = conv.shape[-1]

    def rings(block):
        return to_rings(block.reshape(16, step, chans)).reshape(total, chans)

    def unring(block):
        return to_rings(block.reshape(16, step, chans)).reshape(genomes, bins, chans)

    place = jnp.stack([lax.axis_index("c"), lax.axis_index(COLUMN)]).astype(jnp.int32)
    state = rings(inputs)
    grad = rings(cotangent)
    out, saved = forward(state, conv, proj, step)
    outputs = unring(out)
    shares = [None, None]
    for b in (1, 0):
        grad, part = backward(b, grad, saved[b], conv, proj, step, place)
        shares[b] = share_of(part)
    input_grad = unring(grad)
    factor = jnp.float32(1.0 / math.sqrt(total * 128))
    share = jnp.stack(shares) * factor
    conv_out = share[:, :, : 3 * mids].reshape(2, -1, 3, mids).transpose(0, 2, 1, 3)
    proj_out = share[:, :, 3 * mids :].transpose(0, 2, 1)
    return outputs, input_grad, conv_out, proj_out


def solution(mesh):
    fine = Mesh(mesh.devices.reshape(4, 4, 2, 2, 2), ("x", "z", "yh", "c", "yl"))
    rows = P("yl", SEQ, None)
    in_specs = (rows, rows, P(), P())
    out_specs = (rows, rows, P(None, None, SEQ + ("yl",), None), P(None, None, SEQ + ("yl",)))
    return jax.shard_map(local, mesh=fine, in_specs=in_specs, out_specs=out_specs, check_vma=False)
```

profile of v0, /device:TPU:0, one launch (start us, length us, event | category | flops | bytes accessed | tf_op | source)
XLA Modules:
  0.0 171.9 jit_solution(18101294054754639262)
XLA Ops:
  0.6 30.6 %all_to_all.20 = bf16[16,64,768]{2,1,0:T(8,128)(2,1)} all-to-all(bf16[16,64,768]{2,1,0:T(8,128)(2,1)} %bitcast.93), channel_id=1, replica_groups=mesh['x'=4,'z'=4,'yh'=2,'c'=2,'yl'=2] {'x','z'}, dimensions={0} | all-to-all | bytes 3145728 | tf_op jit(solution)/shard_map/all_to_all | solution.py:162
  31.3 3.8 %all-to-all-start.2 = ((bf16[16,64,768]{2,1,0:T(8,128)(2,1)}), bf16[16,64,768]{2,1,0:T(8,128)(2,1)S(1)}, u32[]{:S(2)}, u32[]{:S(2)}) async-start(bf16[16,64,768]{2,1,0:T(8,128)(2,1)} %bitcast.6), calls=%async_computation.2 | async-start | bytes 3145728 | tf_op jit(solution)/shard_map/all_to_all | solution.py:162
  35.1 0.6 pad_add_fusion.place_ref
  35.7 13.6 %forward.1 = (bf16[1024,768]{1,0:T(8,128)(2,1)}, bf16[1024,768]{1,0:T(8,128)(2,1)}, bf16[1024,768]{1,0:T(8,128)(2,1)}, bf16[1024,384]{1,0:T(8,128)(2,1)}, bf16[1...) custom-call(bf16[1024,768]{1,0:T(8,128)(2,1)} %bitcast.91, ...), custom_call_target="tpu_custom_call" | custom-call | tf_op jit(solution)/shard_map/forward/pallas_call | solution.py:88
  49.3 8.3 %all-to-all-done.2 = bf16[16,64,768]{2,1,0:T(8,128)(2,1)S(1)} async-done(((bf16[16,64,768]{2,1,0:T(8,128)(2,1)}), bf16[16,64,768]{2,1,0:T(8,128)(2,1)S(1)}, u32[]{:S(2)}, u32[]{:S(2)}) %all-to-all-start.2) | async-done | bytes 1572896 | tf_op jit(solution)/shard_map/all_to_all | solution.py:162
  57.6 1.1 copy-done
  58.8 13.8 %backward1.1 = (bf16[1024,768]{1,0:T(8,128)(2,1)}, bf16[2,4,96,1536]{3,2,1,0:T(8,128)(2,1)}) custom-call(s32[2]{0:T(128)} %pad_add_fusion.place_ref, bf16[1024,768]{1,0:T(8,128)(2,1)} %bitcast.92, bf16[1024,768]{1,0:T(8,128)(2,1)} %get-tuple-element.18.feature_ref, bf16[1024,768]{1,0:T(8,128)(2,1)} %get-tuple-element.19.slope_in_ref, ...), custom_call_target="tpu_custom_call" | custom-call | tf_op jit(solution)/shard_map/backward1/pallas_call | solution.py:143
  72.6 13.7 %backward0.1 = (bf16[1024,768]{1,0:T(8,128)(2,1)}, bf16[2,4,96,1536]{3,2,1,0:T(8,128)(2,1)}) custom-call(s32[2]{0:T(128)} %pad_add_fusion.place_ref, bf16[1024,768]{1,0:T(8,128)(2,1)} %get-tuple-element.22.grad_ref, bf16[1024,768]{1,0:T(8,128)(2,1)} %get-tuple-element.23.feature_ref, bf16[1024,768]{1,0:T(8,128)(2,1)} %get-tuple-element.24.slope_in_ref, ...), custom_call_target="tpu_custom_call" | custom-call | tf_op jit(solution)/shard_map/backward0/pallas_call | solution.py:143
  86.3 2.6 %slice_bitcast_fusion.1 = bf16[4,96,1536]{2,1,0:T(8,128)(2,1)} fusion(bf16[2,4,96,1536]{3,2,1,0:T(8,128)(2,1)} %get-tuple-element.28), kind=kLoop, calls=%fused_computation.5 | loop fusion | bytes 2359296 | tf_op jit(solution)/shard_map/squeeze | solution.py:178
  88.8 1.1 slice_bitcast_fusion
  89.9 0.5 collective-permute-start.10
  90.5 3.7 %all-to-all-start.3 = ((bf16[16,64,768]{2,1,0:T(8,128)(2,1)}), bf16[16,64,768]{2,1,0:T(8,128)(2,1)S(1)}, u32[]{:S(2)}, u32[]{:S(2)}) async-start(bf16[16,64,768]{2,1,0:T(8,128)(2,1)} %bitcast.8), calls=%async_computation.3 | async-start | bytes 3145728 | tf_op jit(solution)/shard_map/all_to_all | solution.py:162
  94.2 2.1 %fusion.1 = bf16[4,96,1536]{2,1,0:T(8,128)(2,1)S(1)} fusion(bf16[4,96,1536]{2,1,0:T(8,128)(2,1)} %collective-permute-done, bf16[2,4,96,1536]{3,2,1,0:T(8,128)(2,1)} %get-tuple-element.28), kind=kLoop, calls=%fused_computation.3 | loop fusion | flops 2359296 | bytes 3538944 | tf_op jit(solution)/shard_map/convert_element_type | solution.py:178
  96.3 1.0 slice_bitcast_fusion.8
  97.2 1.6 collective-permute-start.1
  98.8 1.7 collective-permute-start.2
  100.5 2.0 %collective-permute-start.3 = (bf16[96,1536]{1,0:T(8,128)(2,1)S(1)}, bf16[96,1536]{1,0:T(8,128)(2,1)}, u32[]{:S(2)}, u32[]{:S(2)}) collective-permute-start(bf16[96,1536]{1,0:T(8,128)(2,1)S(1)} %get-tuple-element.35), channel_id=1, source_target_pairs={{0,4},{1,5},{4,0},{5,1},{2,6},{3,7},{6,2},{7,3},{8,12},{9,13},{12,... | collective-permute-start | bytes 884744 | tf_op jit(solution)/shard_map/ppermute | solution.py:167
  102.5 0.0 collective-permute-done.10
  102.5 0.3 fusion
  102.8 0.0 copy-start.1
  102.8 1.0 slice_bitcast_fusion.4
  103.8 0.7 collective-permute-start.11
  104.5 2.6 %collective-permute-start.12 = (bf16[96,1536]{1,0:T(8,128)(2,1)}, bf16[96,1536]{1,0:T(8,128)(2,1)}, u32[]{:S(2)}, u32[]{:S(2)}) collective-permute-start(bf16[96,1536]{1,0:T(8,128)(2,1)} %get-tuple-element.39), channel_id=1, source_target_pairs={{0,5},{1,0},{4,1},{5,4},{2,7},{3,2},{6,3},{7,6},{8,13},{9,8},{12,9... | collective-permute-start | bytes 884744 | tf_op jit(solution)/shard_map/ppermute | solution.py:167
  107.1 11.7 %all-to-all-done.3 = bf16[16,64,768]{2,1,0:T(8,128)(2,1)S(1)} async-done(((bf16[16,64,768]{2,1,0:T(8,128)(2,1)}), bf16[16,64,768]{2,1,0:T(8,128)(2,1)S(1)}, u32[]{:S(2)}, u32[]{:S(2)}) %all-to-all-start.3) | async-done | bytes 1572896 | tf_op jit(solution)/shard_map/all_to_all | solution.py:162
  118.7 3.7 %all-to-all-start.1 = ((bf16[16,64,768]{2,1,0:T(8,128)(2,1)}), bf16[16,64,768]{2,1,0:T(8,128)(2,1)S(1)}, u32[]{:S(2)}, u32[]{:S(2)}) async-start(bf16[16,64,768]{2,1,0:T(8,128)(2,1)} %bitcast.94), calls=%async_computation.1 | async-start | bytes 3145728 | tf_op jit(solution)/shard_map/all_to_all | solution.py:162
  122.4 0.0 collective-permute-done.1
  122.4 3.3 %collective-permute-start.13 = (bf16[96,1536]{1,0:T(8,128)(2,1)}, bf16[96,1536]{1,0:T(8,128)(2,1)S(1)}, u32[]{:S(2)}, u32[]{:S(2)}) collective-permute-start(bf16[96,1536]{1,0:T(8,128)(2,1)} %get-tuple-element.38), channel_id=1, source_target_pairs={{0,4},{1,5},{4,0},{5,1},{2,6},{3,7},{6,2},{7,3},{8,12},{9,13},{12,... | collective-permute-start | bytes 884744 | tf_op jit(solution)/shard_map/ppermute | solution.py:167
  125.7 0.0 collective-permute-done.2
  125.7 0.0 collective-permute-done.3
  125.7 1.4 fusion.7
  127.1 0.7 dynamic-slice_bitcast_fusion.5
  127.8 1.8 %collective-permute-start.4 = (bf16[24,1536]{1,0:T(8,128)(2,1)S(1)}, bf16[24,1536]{1,0:T(8,128)(2,1)}, u32[]{:S(2)}, u32[]{:S(2)}) collective-permute-start(bf16[24,1536]{1,0:T(8,128)(2,1)S(1)} %get-tuple-element.40), channel_id=1, source_target_pairs={{0,32},{32,64},{64,96},{96,0},{1,33},{33,65},{65,97},{97,1},{2,34}... | collective-permute-start | bytes 221192 | tf_op jit(solution)/shard_map/ppermute | solution.py:167
  129.6 1.4 collective-permute-start.5
  131.0 0.0 collective-permute-done.11
  131.0 2.1 %collective-permute-start.6 = (bf16[24,1536]{1,0:T(8,128)(2,1)}, bf16[24,1536]{1,0:T(8,128)(2,1)}, u32[]{:S(2)}, u32[]{:S(2)}) collective-permute-start(bf16[24,1536]{1,0:T(8,128)(2,1)} %get-tuple-element.41), channel_id=1, source_target_pairs={{0,64},{32,96},{64,0},{96,32},{1,65},{33,97},{65,1},{97,33},{2,66}... | collective-permute-start | bytes 221192 | tf_op jit(solution)/shard_map/ppermute | solution.py:167
  133.2 0.0 collective-permute-done.13
  133.2 1.3 fusion.4
  134.5 0.0 copy-start.5
  134.5 0.7 copy-done.5
  135.2 0.7 dynamic-slice_bitcast_fusion.2
  135.9 0.6 collective-permute-start.14
  136.5 2.6 %collective-permute-start.15 = (bf16[24,1536]{1,0:T(8,128)(2,1)}, bf16[24,1536]{1,0:T(8,128)(2,1)}, u32[]{:S(2)}, u32[]{:S(2)}) collective-permute-start(bf16[24,1536]{1,0:T(8,128)(2,1)} %get-tuple-element.45), channel_id=1, source_target_pairs={{0,96},{32,0},{64,32},{96,64},{1,97},{33,1},{65,33},{97,65},{2,98}... | collective-permute-start | bytes 221192 | tf_op jit(solution)/shard_map/ppermute | solution.py:167
  139.1 6.5 %collective-permute-done.4 = bf16[24,1536]{1,0:T(8,128)(2,1)} collective-permute-done((bf16[24,1536]{1,0:T(8,128)(2,1)S(1)}, bf16[24,1536]{1,0:T(8,128)(2,1)}, u32[]{:S(2)}, u32[]{:S(2)}) %collective-permute-start.4) | collective-permute-done | bytes 73760 | tf_op jit(solution)/shard_map/ppermute | solution.py:167
  145.6 1.6 collective-permute-start.16
  147.3 0.0 all-to-all-done.1
  147.3 0.0 collective-permute-done.15
  147.3 0.6 copy-done.6
  147.9 3.9 %collective-permute-done.16 = bf16[24,1536]{1,0:T(8,128)(2,1)} collective-permute-done((bf16[24,1536]{1,0:T(8,128)(2,1)}, bf16[24,1536]{1,0:T(8,128)(2,1)}, u32[]{:S(2)}, u32[]{:S(2)}) %collective-permute-start.16) | collective-permute-done | bytes 73760 | tf_op jit(solution)/shard_map/ppermute | solution.py:167
  151.8 1.8 %fusion.10 = (bf16[24,1536]{1,0:T(8,128)(2,1)S(1)}, bf16[24,1536]{1,0:T(8,128)(2,1)}) fusion(bf16[24,1536]{1,0:T(8,128)(2,1)} %collective-permute-done.16, bf16[24,1536]{1,0:T(8,128)(2,1)} %collective-permute-done.15, bf16[24,1536]{1,0:T(8,128)(2,1)} %collective-permute-done.14, bf16[4,24,1536]{2,1,0:T(8,128)(2,1)} %bitcast.98, s32[]{:T(128)S(6)} %select_n.86, ...), kind=kLoop, calls=%fused_computation.25 | loop fusion | flops 589824 | bytes 737284 | tf_op jit(solution)/shard_map/convert_element_type | solution.py:189
  153.6 0.9 reshape.72
  154.5 0.6 dynamic-slice_bitcast_fusion.11
  155.1 1.4 collective-permute-start.7
  156.5 1.8 %collective-permute-start.8 = (bf16[6,1536]{1,0:T(8,128)(2,1)S(1)}, bf16[6,1536]{1,0:T(8,128)(2,1)S(1)}, u32[]{:S(2)}, u32[]{:S(2)}) collective-permute-start(bf16[6,1536]{1,0:T(8,128)(2,1)S(1)} %get-tuple-element.48), channel_id=1, source_target_pairs={{0,24},{8,0},{16,8},{24,16},{1,25},{9,1},{17,9},{25,17},{2,26},{10... | collective-permute-start | bytes 55304 | tf_op jit(solution)/shard_map/ppermute | solution.py:167
  158.4 1.0 collective-permute-start.9
  159.5 0.6 collective-permute-start.17
  160.1 2.7 %collective-permute-start.18 = (bf16[6,1536]{1,0:T(8,128)(2,1)S(1)}, bf16[6,1536]{1,0:T(8,128)(2,1)S(1)}, u32[]{:S(2)}, u32[]{:S(2)}) collective-permute-start(bf16[6,1536]{1,0:T(8,128)(2,1)S(1)} %get-tuple-element.51), channel_id=1, source_target_pairs={{0,24},{8,0},{16,8},{24,16},{1,25},{9,1},{17,9},{25,17},{2,26},{10... | collective-permute-start | bytes 55304 | tf_op jit(solution)/shard_map/ppermute | solution.py:167
  162.8 1.3 collective-permute-start.19
  164.1 0.5 collective-permute-done.17
  164.6 3.5 %collective-permute-done.19 = bf16[6,1536]{1,0:T(8,128)(2,1)S(1)} collective-permute-done((bf16[6,1536]{1,0:T(8,128)(2,1)S(1)}, bf16[6,1536]{1,0:T(8,128)(2,1)S(1)}, u32[]{:S(2)}, u32[]{:S(2)}) %collective-permute-start.19) | collective-permute-done | bytes 18464 | tf_op jit(solution)/shard_map/ppermute | solution.py:167
  168.2 0.1 reshape.75
  168.3 0.7 copy.10
  169.0 0.6 copy.11
  169.6 1.1 copy.14
  170.7 1.1 copy.15
  (27 shorter events, 0.2 us)
Async XLA Ops:
  31.3 26.4 %all-to-all-start.2 = ((bf16[16,64,768]{2,1,0:T(8,128)(2,1)}), bf16[16,64,768]{2,1,0:T(8,128)(2,1)S(1)}, u32[]{:S(2)}, u32[]{:S(2)}) async-start(bf16[16,64,768]{2,1,0:T(8,128)(2,1)} %bitcast.6), calls=%async_computation.2 | async-start | bytes 3145728 | tf_op jit(solution)/shard_map/all_to_all | solution.py:162
  57.6 1.1 copy-start
  86.3 2.6 %copy-start.3 = (bf16[2,4,96,1536]{3,2,1,0:T(8,128)(2,1)S(1)}, bf16[2,4,96,1536]{3,2,1,0:T(8,128)(2,1)}, u32[]{:S(2)}) copy-start(bf16[2,4,96,1536]{3,2,1,0:T(8,128)(2,1)} %get-tuple-element.29) | copy-start | bytes 7077892
  88.8 5.3 %collective-permute-start = (bf16[4,96,1536]{2,1,0:T(8,128)(2,1)}, bf16[4,96,1536]{2,1,0:T(8,128)(2,1)}, u32[]{:S(2)}, u32[]{:S(2)}) collective-permute-start(bf16[4,96,1536]{2,1,0:T(8,128)(2,1)} %slice_bitcast_fusion.1), channel_id=1, source_target_pairs={{0,2},{2,0},{1,3},{3,1},{4,6},{6,4},{5,7},{7,5},{8,10},{10,8},{9,1... | collective-permute-start | bytes 3538952 | tf_op jit(solution)/shard_map/ppermute | solution.py:167
  89.9 12.5 %collective-permute-start.10 = (bf16[4,96,1536]{2,1,0:T(8,128)(2,1)}, bf16[4,96,1536]{2,1,0:T(8,128)(2,1)S(1)}, u32[]{:S(2)}, u32[]{:S(2)}) collective-permute-start(bf16[4,96,1536]{2,1,0:T(8,128)(2,1)} %slice_bitcast_fusion), channel_id=1, source_target_pairs={{0,2},{2,0},{1,3},{3,1},{4,6},{6,4},{5,7},{7,5},{8,10},{10,8},{9,1... | collective-permute-start | bytes 3538952 | tf_op jit(solution)/shard_map/ppermute | solution.py:167
  90.5 28.3 %all-to-all-start.3 = ((bf16[16,64,768]{2,1,0:T(8,128)(2,1)}), bf16[16,64,768]{2,1,0:T(8,128)(2,1)S(1)}, u32[]{:S(2)}, u32[]{:S(2)}) async-start(bf16[16,64,768]{2,1,0:T(8,128)(2,1)} %bitcast.8), calls=%async_computation.3 | async-start | bytes 3145728 | tf_op jit(solution)/shard_map/all_to_all | solution.py:162
  94.2 8.3 %copy-start.4 = (bf16[2,4,96,1536]{3,2,1,0:T(8,128)(2,1)S(1)}, bf16[2,4,96,1536]{3,2,1,0:T(8,128)(2,1)}, u32[]{:S(2)}) copy-start(bf16[2,4,96,1536]{3,2,1,0:T(8,128)(2,1)} %get-tuple-element.29) | copy-start | bytes 7077892
  96.2 6.2 %copy-start.2 = (bf16[4,96,1536]{2,1,0:T(8,128)(2,1)}, bf16[4,96,1536]{2,1,0:T(8,128)(2,1)S(1)}, u32[]{:S(2)}) copy-start(bf16[4,96,1536]{2,1,0:T(8,128)(2,1)S(1)} %fusion.1) | copy-start | bytes 3538948
  97.2 25.2 %collective-permute-start.1 = (bf16[96,1536]{1,0:T(8,128)(2,1)}, bf16[96,1536]{1,0:T(8,128)(2,1)}, u32[]{:S(2)}, u32[]{:S(2)}) collective-permute-start(bf16[96,1536]{1,0:T(8,128)(2,1)} %get-tuple-element.34), channel_id=1, source_target_pairs={{0,1},{1,4},{4,5},{5,0},{2,3},{3,6},{6,7},{7,2},{8,9},{9,12},{12,1... | collective-permute-start | bytes 884744 | tf_op jit(solution)/shard_map/ppermute | solution.py:167
  98.8 26.9 %collective-permute-start.2 = (bf16[96,1536]{1,0:T(8,128)(2,1)}, bf16[96,1536]{1,0:T(8,128)(2,1)}, u32[]{:S(2)}, u32[]{:S(2)}) collective-permute-start(bf16[96,1536]{1,0:T(8,128)(2,1)} %get-tuple-element.36), channel_id=1, source_target_pairs={{0,5},{1,0},{4,1},{5,4},{2,7},{3,2},{6,3},{7,6},{8,13},{9,8},{12,9... | collective-permute-start | bytes 884744 | tf_op jit(solution)/shard_map/ppermute | solution.py:167
  100.5 25.3 %collective-permute-start.3 = (bf16[96,1536]{1,0:T(8,128)(2,1)S(1)}, bf16[96,1536]{1,0:T(8,128)(2,1)}, u32[]{:S(2)}, u32[]{:S(2)}) collective-permute-start(bf16[96,1536]{1,0:T(8,128)(2,1)S(1)} %get-tuple-element.35), channel_id=1, source_target_pairs={{0,4},{1,5},{4,0},{5,1},{2,6},{3,7},{6,2},{7,3},{8,12},{9,13},{12,... | collective-permute-start | bytes 884744 | tf_op jit(solution)/shard_map/ppermute | solution.py:167
  102.8 1.7 copy-start.1
  103.8 27.2 %collective-permute-start.11 = (bf16[96,1536]{1,0:T(8,128)(2,1)}, bf16[96,1536]{1,0:T(8,128)(2,1)}, u32[]{:S(2)}, u32[]{:S(2)}) collective-permute-start(bf16[96,1536]{1,0:T(8,128)(2,1)} %get-tuple-element.37), channel_id=1, source_target_pairs={{0,1},{1,4},{4,5},{5,0},{2,3},{3,6},{6,7},{7,2},{8,9},{9,12},{12,1... | collective-permute-start | bytes 884744 | tf_op jit(solution)/shard_map/ppermute | solution.py:167
  104.5 28.7 %collective-permute-start.12 = (bf16[96,1536]{1,0:T(8,128)(2,1)}, bf16[96,1536]{1,0:T(8,128)(2,1)}, u32[]{:S(2)}, u32[]{:S(2)}) collective-permute-start(bf16[96,1536]{1,0:T(8,128)(2,1)} %get-tuple-element.39), channel_id=1, source_target_pairs={{0,5},{1,0},{4,1},{5,4},{2,7},{3,2},{6,3},{7,6},{8,13},{9,8},{12,9... | collective-permute-start | bytes 884744 | tf_op jit(solution)/shard_map/ppermute | solution.py:167
  118.7 28.6 %all-to-all-start.1 = ((bf16[16,64,768]{2,1,0:T(8,128)(2,1)}), bf16[16,64,768]{2,1,0:T(8,128)(2,1)S(1)}, u32[]{:S(2)}, u32[]{:S(2)}) async-start(bf16[16,64,768]{2,1,0:T(8,128)(2,1)} %bitcast.94), calls=%async_computation.1 | async-start | bytes 3145728 | tf_op jit(solution)/shard_map/all_to_all | solution.py:162
  122.4 10.8 %collective-permute-start.13 = (bf16[96,1536]{1,0:T(8,128)(2,1)}, bf16[96,1536]{1,0:T(8,128)(2,1)S(1)}, u32[]{:S(2)}, u32[]{:S(2)}) collective-permute-start(bf16[96,1536]{1,0:T(8,128)(2,1)} %get-tuple-element.38), channel_id=1, source_target_pairs={{0,4},{1,5},{4,0},{5,1},{2,6},{3,7},{6,2},{7,3},{8,12},{9,13},{12,... | collective-permute-start | bytes 884744 | tf_op jit(solution)/shard_map/ppermute | solution.py:167
  127.8 17.8 %collective-permute-start.4 = (bf16[24,1536]{1,0:T(8,128)(2,1)S(1)}, bf16[24,1536]{1,0:T(8,128)(2,1)}, u32[]{:S(2)}, u32[]{:S(2)}) collective-permute-start(bf16[24,1536]{1,0:T(8,128)(2,1)S(1)} %get-tuple-element.40), channel_id=1, source_target_pairs={{0,32},{32,64},{64,96},{96,0},{1,33},{33,65},{65,97},{97,1},{2,34}... | collective-permute-start | bytes 221192 | tf_op jit(solution)/shard_map/ppermute | solution.py:167
  129.6 17.7 %collective-permute-start.5 = (bf16[24,1536]{1,0:T(8,128)(2,1)}, bf16[24,1536]{1,0:T(8,128)(2,1)S(1)}, u32[]{:S(2)}, u32[]{:S(2)}) collective-permute-start(bf16[24,1536]{1,0:T(8,128)(2,1)} %get-tuple-element.42), channel_id=1, source_target_pairs={{0,96},{32,0},{64,32},{96,64},{1,97},{33,1},{65,33},{97,65},{2,98}... | collective-permute-start | bytes 221192 | tf_op jit(solution)/shard_map/ppermute | solution.py:167
  131.0 16.2 %collective-permute-start.6 = (bf16[24,1536]{1,0:T(8,128)(2,1)}, bf16[24,1536]{1,0:T(8,128)(2,1)}, u32[]{:S(2)}, u32[]{:S(2)}) collective-permute-start(bf16[24,1536]{1,0:T(8,128)(2,1)} %get-tuple-element.41), channel_id=1, source_target_pairs={{0,64},{32,96},{64,0},{96,32},{1,65},{33,97},{65,1},{97,33},{2,66}... | collective-permute-start | bytes 221192 | tf_op jit(solution)/shard_map/ppermute | solution.py:167
  134.5 0.7 copy-start.5
  135.9 11.4 %collective-permute-start.14 = (bf16[24,1536]{1,0:T(8,128)(2,1)}, bf16[24,1536]{1,0:T(8,128)(2,1)}, u32[]{:S(2)}, u32[]{:S(2)}) collective-permute-start(bf16[24,1536]{1,0:T(8,128)(2,1)} %get-tuple-element.43), channel_id=1, source_target_pairs={{0,32},{32,64},{64,96},{96,0},{1,33},{33,65},{65,97},{97,1},{2,34}... | collective-permute-start | bytes 221192 | tf_op jit(solution)/shard_map/ppermute | solution.py:167
  136.5 10.8 %collective-permute-start.15 = (bf16[24,1536]{1,0:T(8,128)(2,1)}, bf16[24,1536]{1,0:T(8,128)(2,1)}, u32[]{:S(2)}, u32[]{:S(2)}) collective-permute-start(bf16[24,1536]{1,0:T(8,128)(2,1)} %get-tuple-element.45), channel_id=1, source_target_pairs={{0,96},{32,0},{64,32},{96,64},{1,97},{33,1},{65,33},{97,65},{2,98}... | collective-permute-start | bytes 221192 | tf_op jit(solution)/shard_map/ppermute | solution.py:167
  145.6 6.2 %collective-permute-start.16 = (bf16[24,1536]{1,0:T(8,128)(2,1)}, bf16[24,1536]{1,0:T(8,128)(2,1)}, u32[]{:S(2)}, u32[]{:S(2)}) collective-permute-start(bf16[24,1536]{1,0:T(8,128)(2,1)} %get-tuple-element.44), channel_id=1, source_target_pairs={{0,64},{32,96},{64,0},{96,32},{1,65},{33,97},{65,1},{97,33},{2,66}... | collective-permute-start | bytes 221192 | tf_op jit(solution)/shard_map/ppermute | solution.py:167
  147.3 0.6 copy-start.6
  155.1 7.6 %collective-permute-start.7 = (bf16[6,1536]{1,0:T(8,128)(2,1)}, bf16[6,1536]{1,0:T(8,128)(2,1)S(1)}, u32[]{:S(2)}, u32[]{:S(2)}) collective-permute-start(bf16[6,1536]{1,0:T(8,128)(2,1)} %get-tuple-element.46), channel_id=1, source_target_pairs={{0,8},{8,16},{16,24},{24,0},{1,9},{9,17},{17,25},{25,1},{2,10},{10... | collective-permute-start | bytes 55304 | tf_op jit(solution)/shard_map/ppermute | solution.py:167
  156.5 7.5 %collective-permute-start.8 = (bf16[6,1536]{1,0:T(8,128)(2,1)S(1)}, bf16[6,1536]{1,0:T(8,128)(2,1)S(1)}, u32[]{:S(2)}, u32[]{:S(2)}) collective-permute-start(bf16[6,1536]{1,0:T(8,128)(2,1)S(1)} %get-tuple-element.48), channel_id=1, source_target_pairs={{0,24},{8,0},{16,8},{24,16},{1,25},{9,1},{17,9},{25,17},{2,26},{10... | collective-permute-start | bytes 55304 | tf_op jit(solution)/shard_map/ppermute | solution.py:167
  158.4 5.7 %collective-permute-start.9 = (bf16[6,1536]{1,0:T(8,128)(2,1)S(1)}, bf16[6,1536]{1,0:T(8,128)(2,1)S(1)}, u32[]{:S(2)}, u32[]{:S(2)}) collective-permute-start(bf16[6,1536]{1,0:T(8,128)(2,1)S(1)} %get-tuple-element.47), channel_id=1, source_target_pairs={{0,16},{8,24},{16,0},{24,8},{1,17},{9,25},{17,1},{25,9},{2,18},{10... | collective-permute-start | bytes 55304 | tf_op jit(solution)/shard_map/ppermute | solution.py:167
  159.5 5.1 %collective-permute-start.17 = (bf16[6,1536]{1,0:T(8,128)(2,1)S(1)}, bf16[6,1536]{1,0:T(8,128)(2,1)S(1)}, u32[]{:S(2)}, u32[]{:S(2)}) collective-permute-start(bf16[6,1536]{1,0:T(8,128)(2,1)S(1)} %get-tuple-element.49), channel_id=1, source_target_pairs={{0,8},{8,16},{16,24},{24,0},{1,9},{9,17},{17,25},{25,1},{2,10},{10... | collective-permute-start | bytes 55304 | tf_op jit(solution)/shard_map/ppermute | solution.py:167
  160.1 4.5 %collective-permute-start.18 = (bf16[6,1536]{1,0:T(8,128)(2,1)S(1)}, bf16[6,1536]{1,0:T(8,128)(2,1)S(1)}, u32[]{:S(2)}, u32[]{:S(2)}) collective-permute-start(bf16[6,1536]{1,0:T(8,128)(2,1)S(1)} %get-tuple-element.51), channel_id=1, source_target_pairs={{0,24},{8,0},{16,8},{24,16},{1,25},{9,1},{17,9},{25,17},{2,26},{10... | collective-permute-start | bytes 55304 | tf_op jit(solution)/shard_map/ppermute | solution.py:167
  162.8 5.3 %collective-permute-start.19 = (bf16[6,1536]{1,0:T(8,128)(2,1)S(1)}, bf16[6,1536]{1,0:T(8,128)(2,1)S(1)}, u32[]{:S(2)}, u32[]{:S(2)}) collective-permute-start(bf16[6,1536]{1,0:T(8,128)(2,1)S(1)} %get-tuple-element.50), channel_id=1, source_target_pairs={{0,16},{8,24},{16,0},{24,8},{1,17},{9,25},{17,1},{25,9},{2,18},{10... | collective-permute-start | bytes 55304 | tf_op jit(solution)/shard_map/ppermute | solution.py:167
where the time goes:
time: 172 us
  starting transfers between devices  42.6 us (25%)
  Pallas kernels  41.1 us (24%)
  waiting for transfers between devices  34.4 us (20%)
  blocking collectives  30.6 us (18%)
  local copies, waits for them, and re-layouts  14.8 us (9%)
  other arithmetic  7.49 us (4%)
    ppermute x20, starting transfers between devices, passed(): lax.ppermute(block, axis, [(i, (i + distance) % size) for i in range(size)])  31.4 us
    all_to_all x1, blocking collectives, to_rings(): return lax.all_to_all(block, RING, 0, 0, tiled=True)  30.6 us
    pallas_call x2, Pallas kernels, backward(): pl.pallas_call(functools.partial(backward_kernel, b, step), out_shape=[ja...  27.5 us
    all_to_all x3, waiting for transfers between devices, to_rings(): return lax.all_to_all(block, RING, 0, 0, tiled=True)  20 us
    ppermute x20, waiting for transfers between devices, passed(): lax.ppermute(block, axis, [(i, (i + distance) % size) for i in range(size)])  14.4 us
    pallas_call x1, Pallas kernels, forward(): pl.pallas_call(functools.partial(forward_kernel, step), out_shape=[wide]...  13.6 us
    all_to_all x3, starting transfers between devices, to_rings(): return lax.all_to_all(block, RING, 0, 0, tiled=True)  11.3 us
    unnamed x18, local copies, waits for them, and re-layouts  6.02 us
  transfers between devices with their start and end apart: 23, of which 6 were waited for; matrix products, arithmetic and copies ran while one was open for 6% of the time, Pallas kernels for 8%

commit v1 on v0

v1 whole, which is shorter than its diff:
```python
import functools
import math

import jax
import jax.numpy as jnp
from jax import lax
from jax.experimental import pallas as pl
from jax.experimental.pallas import tpu as pltpu
from jax.sharding import Mesh
from jax.sharding import PartitionSpec as P

RING = ("x", "z")
COLUMN = ("yh", "yl")
SEQ = ("x", "z", "yh", "c")
BF = jnp.bfloat16
F32 = jnp.float32
BLOCK = 256
VMEM_BYTES = 40 * 1024 * 1024


def gelu_parts(value):
    cdf = 0.5 * (1.0 + lax.erf(value * (1.0 / math.sqrt(2.0))))
    density = jnp.exp(-0.5 * value * value) * (1.0 / math.sqrt(2.0 * math.pi))
    return (value * cdf).astype(BF), (cdf + value * density).astype(BF)


def dot(left, right):
    return jnp.dot(left, right, preferred_element_type=F32)


def dot_t(left, right):
    return lax.dot_general(left, right, (((1,), (1,)), ((), ())), preferred_element_type=F32)


def dot_rows(left, right):
    return lax.dot_general(left, right, (((0,), (0,)), ((), ())), preferred_element_type=F32)


def ring_rows(ref, start, count):
    total = ref.shape[0]
    start %= total
    if start + count <= total:
        return ref[start : start + count, :]
    first = total - start
    return jnp.concatenate([ref[start:total, :], ref[: count - first, :]], axis=0)


class Fetched:
    def __init__(self, copy):
        self.copy, self.here = copy, False
        copy.start()

    def get(self):
        if not self.here:
            self.copy.wait()
            self.here = True
        return self.copy.dst_ref


class Sent:
    def __init__(self, source, target, sem):
        self.source = source
        self.copy = pltpu.make_async_copy(source, target, sem)

    def send(self):
        self.copy.start()

    def finish(self):
        self.copy.wait()


def staged_call(body, name, ins, outs, scratch, work, place=None):
    blocks = [x[1] if isinstance(x, tuple) else None for x in ins]
    arrays = [x[0] if isinstance(x, tuple) else x for x in ins]
    shapes = [x.shape if b is None else x.shape[1:] for x, b in zip(arrays, blocks)]
    held = [pltpu.VMEM(shape, BF) for shape in shapes] + [pltpu.VMEM(x.shape, BF) for x in outs]
    n, m, k = len(arrays), len(outs), len(held)
    extra = [] if place is None else [place]

    def kernel(*refs):
        head, refs = refs[: len(extra)], refs[len(extra) :]
        sources, targets, kept = refs[:n], refs[n : n + m], refs[n + m : n + m + k]
        in_sems, out_sems = refs[n + m + k], refs[n + m + k + 1]
        rest = refs[n + m + k + 2 :]
        sources = [ref if b is None else ref.at[b] for ref, b in zip(sources, blocks)]
        fetched = [
            Fetched(pltpu.make_async_copy(sources[i], kept[i], in_sems.at[i])) for i in range(n)
        ]
        sent = [Sent(kept[n + i], targets[i], out_sems.at[i]) for i in range(m)]
        body(fetched, sent, *head, *rest)
        for result in sent:
            result.finish()

    return pl.pallas_call(
        kernel,
        out_shape=[pltpu.HBM(x.shape, x.dtype) for x in outs],
        in_specs=[pl.BlockSpec(memory_space=pltpu.SMEM)] * len(extra)
        + [pl.BlockSpec(memory_space=pltpu.HBM)] * n,
        out_specs=[pl.BlockSpec(memory_space=pltpu.HBM)] * m,
        scratch_shapes=held
        + [pltpu.SemaphoreType.DMA((n,)), pltpu.SemaphoreType.DMA((m,))]
        + list(scratch),
        compiler_params=pltpu.CompilerParams(vmem_limit_bytes=VMEM_BYTES),
        cost_estimate=pl.CostEstimate(flops=1, bytes_accessed=1, transcendentals=0),
        name=name,
    )(*extra, *[pltpu.with_memory_space_constraint(x, pltpu.HBM) for x in arrays])


def forward(state, conv, proj, step):
    total, chans = state.shape
    mids = conv.shape[-1]
    wide = jax.ShapeDtypeStruct((total, chans), BF)
    thin = jax.ShapeDtypeStruct((total, mids), BF)
    starts = range(0, total, BLOCK)

    def body(fetched, sent, mid_ref):
        out, saved = sent[0], (sent[1:5], sent[5:9])

        def enter(b, start, value):
            rows = slice(start, start + BLOCK)
            feature, slope = gelu_parts(value)
            saved[b][0].source[rows, :] = feature
            saved[b][1].source[rows, :] = slope

        x_ref = fetched[0].get()
        for start in starts:
            enter(0, start, x_ref[start : start + BLOCK, :].astype(F32))
        saved[0][0].send()
        saved[0][1].send()
        for b in range(2):
            feature_ref, activ_ref, slope_ref = (saved[b][i].source for i in (0, 2, 3))
            conv_ref, proj_ref = fetched[1 + 2 * b].get(), fetched[2 + 2 * b].get()
            source = x_ref if b == 0 else mid_ref
            shift = step * 2**b
            for start in starts:
                rows = slice(start, start + BLOCK)
                pre = (
                    dot(ring_rows(feature_ref, start - shift, BLOCK), conv_ref[0])
                    + dot(feature_ref[rows, :], conv_ref[1])
                    + dot(ring_rows(feature_ref, start + shift, BLOCK), conv_ref[2])
                )
                activ, slope = gelu_parts(pre)
                activ_ref[rows, :] = activ
                slope_ref[rows, :] = slope
                after = source[rows, :].astype(F32) + dot(activ, proj_ref[...])
                after = after.astype(BF)
                if b == 0:
                    mid_ref[rows, :] = after
                    enter(1, start, after.astype(F32))
                else:
                    out.source[rows, :] = after
            for result in saved[0][2:] + saved[1][:2] if b == 0 else [*saved[1][2:], out]:
                result.send()

    outs = staged_call(
        body, "forward", [state, (conv, 0), (proj, 0), (conv, 1), (proj, 1)],
        [wide] + [wide, wide, thin, thin] * 2, [pltpu.VMEM((total, chans), BF)],
        16 * total * chans * mids,
    )
    return outs[0], (outs[1:5], outs[5:9])


def put_taps(e_ref, taps_ref, shift):
    total, mids = e_ref.shape
    for start in range(0, total, BLOCK):
        rows = slice(start, start + BLOCK)
        taps_ref[rows, :mids] = ring_rows(e_ref, start + shift, BLOCK)
        taps_ref[rows, mids : 2 * mids] = e_ref[rows, :]
        taps_ref[rows, 2 * mids :] = ring_rows(e_ref, start - shift, BLOCK)


def spread(e_ref, conv_ref, start, shift):
    return (
        dot_t(ring_rows(e_ref, start + shift, BLOCK), conv_ref[0])
        + dot_t(e_ref[start : start + BLOCK, :], conv_ref[1])
        + dot_t(ring_rows(e_ref, start - shift, BLOCK), conv_ref[2])
    )


def weight_terms(left_ref, right_ref, sum_ref, at):
    chans, wide = left_ref.shape[1], right_ref.shape[1]
    for first in range(0, chans, BLOCK):
        some = slice(first, first + BLOCK)
        sum_ref[some, at : at + wide] = dot_rows(left_ref[:, some], right_ref[...])


def put_in_order(place_ref, sum_ref, order_ref, mine, away):
    share = sum_ref.shape[0] // 128
    for c in range(2):
        for y in range(4):
            for ring in range(16):
                owner = ((ring * 2 + y // 2) * 2 + c) * 2 + y % 2
                order_ref[ring * share : (ring + 1) * share, :] = sum_ref[
                    owner * share : (owner + 1) * share, :
                ]
            slot = (y + 4 - place_ref[1]) % 4

            @pl.when(place_ref[0] == c)
            def _():
                mine.source[slot] = order_ref[...].astype(BF)

            @pl.when(place_ref[0] != c)
            def _():
                away.source[slot] = order_ref[...].astype(BF)

    away.send()
    mine.send()


def term_scratch(chans, wide):
    return [pltpu.VMEM((chans, wide), F32), pltpu.VMEM((16 * (chans // 128), wide), F32)]


def term_outs(chans, wide):
    return [jax.ShapeDtypeStruct((4, 16 * (chans // 128), wide), BF)] * 2


def later(grad_parts, slope1, feature1, activ1, slope_in1, activ0, conv, proj, step, place):
    total, chans = feature1.shape
    mids = slope1.shape[1]
    starts = range(0, total, BLOCK)

    def body(fetched, sent, place_ref, e_ref, taps_ref, sum_ref, order_ref):
        mid, mine, away = sent
        grad_ref, proj_ref, slope_ref = (f.get() for f in fetched[:3])
        for start in starts:
            rows = slice(start, start + BLOCK)
            pulled = dot_t(grad_ref[rows, :], proj_ref[...])
            e_ref[rows, :] = (pulled * slope_ref[rows, :].astype(F32)).astype(BF)
        put_taps(e_ref, taps_ref, 2 * step)
        conv_ref, slope_in_ref, feature_ref, activ_ref, before_ref = (f.get() for f in fetched[3:])
        for start in starts:
            rows = slice(start, start + BLOCK)
            summed = spread(e_ref, conv_ref, start, 2 * step)
            grown = grad_ref[rows, :].astype(F32) + summed * slope_in_ref[rows, :].astype(F32)
            mid.source[rows, :] = grown.astype(BF)
        mid.send()
        weight_terms(feature_ref, taps_ref, sum_ref, 0)
        weight_terms(grad_ref, activ_ref, sum_ref, 3 * mids)
        weight_terms(mid.source, before_ref, sum_ref, 4 * mids)
        put_in_order(place_ref, sum_ref, order_ref, mine, away)

    return staged_call(
        body, "later",
        [grad_parts, (proj, 1), slope1, (conv, 1), slope_in1, feature1, activ1, activ0],
        [jax.ShapeDtypeStruct((total, chans), BF)] + term_outs(chans, 5 * mids),
        [pltpu.VMEM((total, mids), BF), pltpu.VMEM((total, 3 * mids), BF)]
        + term_scratch(chans, 5 * mids),
        18 * total * chans * mids, place,
    )


def first(mid, slope0, feature0, slope_in0, conv, proj, step, place):
    total, chans = mid.shape
    mids = slope0.shape[1]
    starts = range(0, total, BLOCK)

    def body(fetched, sent, place_ref, e_ref, taps_ref, sum_ref, order_ref):
        out, mine, away = sent
        mid_ref, proj_ref, slope_ref = (f.get() for f in fetched[:3])
        for start in starts:
            rows = slice(start, start + BLOCK)
            pulled = dot_t(mid_ref[rows, :], proj_ref[...])
            e_ref[rows, :] = (pulled * slope_ref[rows, :].astype(F32)).astype(BF)
        put_taps(e_ref, taps_ref, step)
        feature_ref, conv_ref, slope_in_ref = (f.get() for f in fetched[3:])
        weight_terms(feature_ref, taps_ref, sum_ref, 0)
        put_in_order(place_ref, sum_ref, order_ref, mine, away)
        for start in starts:
            rows = slice(start, start + BLOCK)
            summed = spread(e_ref, conv_ref, start, step)
            grown = mid_ref[rows, :].astype(F32) + summed * slope_in_ref[rows, :].astype(F32)
            out.source[rows, :] = grown.astype(BF)
        out.send()

    return staged_call(
        body, "first", [mid, (proj, 0), slope0, feature0, (conv, 0), slope_in0],
        [jax.ShapeDtypeStruct((total, chans), BF)] + term_outs(chans, 3 * mids),
        [pltpu.VMEM((total, mids), BF), pltpu.VMEM((total, 3 * mids), BF)]
        + term_scratch(chans, 3 * mids),
        14 * total * chans * mids, place,
    )


def to_rings(block):
    return lax.all_to_all(block, RING, 0, 0, tiled=True)


def passed(block, axis, distance):
    size = lax.axis_size(axis)
    return lax.ppermute(block, axis, [(i, (i + distance) % size) for i in range(size)])


def total_of(parts):
    out = parts[0].astype(F32)
    for part in parts[1:]:
        out = out + part.astype(F32)
    return out


def column_share(mine, came):
    both = [total_of([mine[k], came[k]]).astype(BF) for k in range(4)]
    return total_of([both[0]] + [passed(both[k], COLUMN, k) for k in (1, 3, 2)]).astype(BF)


def ring_share(both):
    rows, wide = both.shape
    got = lax.all_to_all(both.reshape(16, -1, 128), RING, 0, 0, tiled=True)
    return got.astype(F32).sum(0).reshape(rows // 16, wide)


def local(inputs, cotangent, conv, proj):
    genomes, bins, chans = inputs.shape
    total = genomes * bins
    step = total // 16
    mids = conv.shape[-1]

    def rings(block):
        return to_rings(block.reshape(16, step, chans)).reshape(total, chans)

    def unring(block):
        return to_rings(block.reshape(16, step, chans)).reshape(genomes, bins, chans)

    place = [lax.axis_index("c"), lax.axis_index(COLUMN)]
    place = jnp.stack(place).astype(jnp.int32)
    state = rings(inputs)
    grad = rings(cotangent)
    out, saved = forward(state, conv, proj, step)
    (feature0, slope_in0, activ0, slope0), (feature1, slope_in1, activ1, slope1) = saved
    outputs = unring(out)
    mid, mine1, away1 = later(
        grad, slope1, feature1, activ1, slope_in1, activ0, conv, proj, step, place
    )
    out, mine0, away0 = first(mid, slope0, feature0, slope_in0, conv, proj, step, place)
    input_grad = unring(out)
    came1, came0 = passed(away1, "c", 1), passed(away0, "c", 1)
    came1, came0, outputs = lax.optimization_barrier((came1, came0, outputs))
    both = [column_share(mine0, came0), column_share(mine1, came1)]
    share = ring_share(jnp.concatenate(both, axis=1))
    share = share * jnp.float32(1.0 / math.sqrt(total * 128))
    wide = 3 * mids
    conv_out = jnp.stack([share[:, :wide], share[:, wide : 2 * wide]])
    conv_out = conv_out.reshape(2, -1, 3, mids).transpose(0, 2, 1, 3)
    proj_out = jnp.stack([share[:, 2 * wide + mids :].T, share[:, 2 * wide : 2 * wide + mids].T])
    return outputs, input_grad, conv_out, proj_out


def solution(mesh):
    fine = Mesh(mesh.devices.reshape(4, 4, 2, 2, 2), ("x", "z", "yh", "c", "yl"))
    rows = P("yl", SEQ, None)
    in_specs = (rows, rows, P(), P())
    out_specs = (rows, rows, P(None, None, SEQ + ("yl",), None), P(None, None, SEQ + ("yl",)))
    return jax.shard_map(local, mesh=fine, in_specs=in_specs, out_specs=out_specs, check_vma=False)
```

time: 172 us -> 156 us (0.907)
  starting transfers between devices: 42.6 us -> 32.3 us
  local copies, waits for them, and re-layouts: 14.8 us -> 6.88 us
  waiting for transfers between devices: 34.4 us -> 37.4 us
  Pallas kernels: 41.1 us -> 39.1 us
    ppermute x20 -> x8, starting transfers between devices: 31.4 us -> 10.6 us  [passed(): lax.ppermute(block, axis, [(i, (i + distance) % size) for i in range(size)])]
    all_to_all x3, waiting for transfers between devices: 20 us -> 8.83 us  [to_rings(): return lax.all_to_all(block, RING, 0, 0, tiled=True)]
    all_to_all x0 -> x1, waiting for transfers between devices: none -> 11 us  [ring_share(): got = lax.all_to_all(both.reshape(16, -1, 128), RING, 0, 0, tiled=True)]
    squeeze x8 -> x0, local copies, waits for them, and re-layouts: 7.71 us -> none  [the longest x2 3.68 us: share_of(): both = total_of([part[0], passed(part[1], 'c', 1)]).astype(BF)]
    all_to_all x0 -> x1, starting transfers between devices: none -> 6.98 us  [ring_share(): got = lax.all_to_all(both.reshape(16, -1, 128), RING, 0, 0, tiled=True)]
    all_to_all x3, starting transfers between devices: 11.3 us -> 14.7 us  [to_rings(): return lax.all_to_all(block, RING, 0, 0, tiled=True)]
    ppermute x20 -> x8, waiting for transfers between devices: 14.4 us -> 17.6 us  [passed(): lax.ppermute(block, axis, [(i, (i + distance) % size) for i in range(size)])]
    pallas_call x3, Pallas kernels: 41.1 us -> 39.1 us  [staged_call(): pl.pallas_call(kernel, out_shape=[pltpu.HBM(x.shape, x.dtype) for x in ou...]
  transfers between devices with their start and end apart: 23 -> 12, of which waited for: 6 -> 5; matrix products, arithmetic and copies ran while one was open for 6% -> 6% of each run, Pallas kernels for 8% -> 25%
where the time goes in v1:
time: 156 us; the launch traced here: 155 us
  Pallas kernels  39.1 us (25%)
  waiting for transfers between devices  37.4 us (24%)
  starting transfers between devices  32.3 us (21%)
  blocking collectives  30.6 us (20%)
  other arithmetic  7.73 us (5%)
  local copies, waits for them, and re-layouts  6.88 us (4%)
    pallas_call x3, Pallas kernels, staged_call(): pl.pallas_call(kernel, out_shape=[pltpu.HBM(x.shape, x.dtype) for x in ou...  39.1 us
    all_to_all x1, blocking collectives, to_rings(): return lax.all_to_all(block, RING, 0, 0, tiled=True)  30.6 us
    ppermute x8, waiting for transfers between devices, passed(): lax.ppermute(block, axis, [(i, (i + distance) % size) for i in range(size)])  17.6 us
    all_to_all x3, starting transfers between devices, to_rings(): return lax.all_to_all(block, RING, 0, 0, tiled=True)  14.7 us
    all_to_all x1, waiting for transfers between devices, ring_share(): got = lax.all_to_all(both.reshape(16, -1, 128), RING, 0, 0, tiled=True)  11 us
    ppermute x8, starting transfers between devices, passed(): lax.ppermute(block, axis, [(i, (i + distance) % size) for i in range(size)])  10.6 us
    all_to_all x3, waiting for transfers between devices, to_rings(): return lax.all_to_all(block, RING, 0, 0, tiled=True)  8.83 us
    all_to_all x1, starting transfers between devices, ring_share(): got = lax.all_to_all(both.reshape(16, -1, 128), RING, 0, 0, tiled=True)  6.98 us
  transfers between devices with their start and end apart: 12, of which 5 were waited for; matrix products, arithmetic and copies ran while one was open for 6% of the time, Pallas kernels for 25%

profile of v1, /device:TPU:0, one launch (start us, length us, event | category | flops | bytes accessed | tf_op | source)
XLA Modules:
  0.0 154.8 jit_solution(14703898059899822896)
XLA Ops:
  0.6 30.6 %all_to_all.25 = bf16[16,64,768]{2,1,0:T(8,128)(2,1)} all-to-all(bf16[16,64,768]{2,1,0:T(8,128)(2,1)} %bitcast.46), channel_id=1, replica_groups=mesh['x'=4,'z'=4,'yh'=2,'c'=2,'yl'=2] {'x','z'}, dimensions={0} | all-to-all | bytes 3145728 | tf_op jit(solution)/shard_map/all_to_all | solution.py:286
  31.3 3.8 %all-to-all-start = ((bf16[16,64,768]{2,1,0:T(8,128)(2,1)}), bf16[16,64,768]{2,1,0:T(8,128)(2,1)S(1)}, u32[]{:S(2)}, u32[]{:S(2)}) async-start(bf16[16,64,768]{2,1,0:T(8,128)(2,1)} %bitcast.2), calls=%async_computation | async-start | bytes 3145728 | tf_op jit(solution)/shard_map/all_to_all | solution.py:286
  35.1 0.1 pad_add_fusion.refs_0_
  35.2 13.6 %forward.1 = (bf16[1024,768]{1,0:T(8,128)(2,1)}, bf16[1024,768]{1,0:T(8,128)(2,1)}, bf16[1024,768]{1,0:T(8,128)(2,1)}, bf16[1024,384]{1,0:T(8,128)(2,1)}, bf16[1...) custom-call(bf16[1024,768]{1,0:T(8,128)(2,1)} %bitcast.45, ...), custom_call_target="tpu_custom_call" | custom-call | flops 1 | bytes 1 | tf_op jit(solution)/shard_map/forward/pallas_call | solution.py:94
  48.8 8.8 %all-to-all-done = bf16[16,64,768]{2,1,0:T(8,128)(2,1)S(1)} async-done(((bf16[16,64,768]{2,1,0:T(8,128)(2,1)}), bf16[16,64,768]{2,1,0:T(8,128)(2,1)S(1)}, u32[]{:S(2)}, u32[]{:S(2)}) %all-to-all-start) | async-done | bytes 1572896 | tf_op jit(solution)/shard_map/all_to_all | solution.py:286
  57.6 0.0 copy-start
  57.6 1.2 copy-done
  58.8 3.9 %all-to-all-start.2 = ((bf16[16,64,768]{2,1,0:T(8,128)(2,1)}), bf16[16,64,768]{2,1,0:T(8,128)(2,1)S(1)}, u32[]{:S(2)}, u32[]{:S(2)}) async-start(bf16[16,64,768]{2,1,0:T(8,128)(2,1)} %bitcast.48), calls=%async_computation.2 | async-start | bytes 3145728 | tf_op jit(solution)/shard_map/all_to_all | solution.py:286
  62.7 13.9 %later.1 = (bf16[1024,768]{1,0:T(8,128)(2,1)}, bf16[4,96,1920]{2,1,0:T(8,128)(2,1)}, bf16[4,96,1920]{2,1,0:T(8,128)(2,1)}) custom-call(s32[2]{0:T(128)S(1)} %pad_add_fusion.refs_0_, bf16[1024,768]{1,0:T(8,128)(2,1)} %bitcast.44, bf16[2,384,768]{2,1,0:T(8,128)(2,1)} %refs_2_.5, bf16[1024,384]{1,0:T(8,128)(2,1)} %get-tuple-element.22.refs_3_, ...), custom_call_target="tpu_custom_call" | custom-call | flops 1 | bytes 1 | tf_op jit(solution)/shard_map/later/pallas_call | solution.py:94
  76.5 0.1 collective-permute-start
  76.6 11.6 %first.1 = (bf16[1024,768]{1,0:T(8,128)(2,1)}, bf16[4,96,1152]{2,1,0:T(8,128)(2,1)}, bf16[4,96,1152]{2,1,0:T(8,128)(2,1)}) custom-call(s32[2]{0:T(128)S(1)} %pad_add_fusion.refs_0_, bf16[1024,768]{1,0:T(8,128)(2,1)} %get-tuple-element.28.refs_1_, bf16[2,384,768]{2,1,0:T(8,128)(2,1)} %refs_2_.5, bf16[1024,384]{1,0:T(8,128)(2,1)} %get-tuple-element.29.refs_3_, ...), custom_call_target="tpu_custom_call" | custom-call | flops 1 | bytes 1 | tf_op jit(solution)/shard_map/first/pallas_call | solution.py:94
  88.3 0.6 collective-permute-start.1
  88.9 0.0 all-to-all-done.2
  88.9 7.0 %all-to-all-start.3 = ((bf16[16,64,768]{2,1,0:T(8,128)(2,1)}), bf16[16,64,768]{2,1,0:T(8,128)(2,1)S(1)}, u32[]{:S(2)}, u32[]{:S(2)}) async-start(bf16[16,64,768]{2,1,0:T(8,128)(2,1)} %bitcast.47), calls=%async_computation.3 | async-start | bytes 3145728 | tf_op jit(solution)/shard_map/all_to_all | solution.py:286
  95.9 0.0 copy-start.1
  95.9 0.0 collective-permute-done.1
  95.9 0.0 collective-permute-done
  95.9 1.7 %fusion.11 = (bf16[96,1152]{1,0:T(8,128)(2,1)S(1)}, bf16[96,1152]{1,0:T(8,128)(2,1)S(1)}, bf16[96,1152]{1,0:T(8,128)(2,1)S(1)}) fusion(bf16[4,96,1152]{2,1,0:T(8,128)(2,1)} %collective-permute-done.1, bf16[4,96,1152]{2,1,0:T(8,128)(2,1)} %get-tuple-element.36), kind=kLoop, calls=%fused_computation.23 | loop fusion | flops 1327104 | bytes 1990656 | tf_op jit(solution)/shard_map/convert_element_type | solution.py:302
  97.6 1.6 %collective-permute-start.2 = (bf16[96,1152]{1,0:T(8,128)(2,1)S(1)}, bf16[96,1152]{1,0:T(8,128)(2,1)S(1)}, u32[]{:S(2)}, u32[]{:S(2)}) collective-permute-start(bf16[96,1152]{1,0:T(8,128)(2,1)S(1)} %get-tuple-element.47), channel_id=1, source_target_pairs={{0,1},{1,4},{4,5},{5,0},{2,3},{3,6},{6,7},{7,2},{8,9},{9,12},{12,1... | collective-permute-start | bytes 663560 | tf_op jit(solution)/shard_map/ppermute | solution.py:291
  99.2 2.9 %collective-permute-start.4 = (bf16[96,1152]{1,0:T(8,128)(2,1)S(1)}, bf16[96,1152]{1,0:T(8,128)(2,1)S(1)}, u32[]{:S(2)}, u32[]{:S(2)}) collective-permute-start(bf16[96,1152]{1,0:T(8,128)(2,1)S(1)} %get-tuple-element.48), channel_id=1, source_target_pairs={{0,4},{1,5},{4,0},{5,1},{2,6},{3,7},{6,2},{7,3},{8,12},{9,13},{12,... | collective-permute-start | bytes 663560 | tf_op jit(solution)/shard_map/ppermute | solution.py:291
  102.1 1.3 collective-permute-start.3
  103.5 0.0 copy-done.1
  103.5 1.5 fusion.7
  105.0 0.7 collective-permute-start.5
  105.7 0.8 collective-permute-start.7
  106.5 0.0 collective-permute-done.2
  106.5 2.5 %collective-permute-start.6 = (bf16[96,1920]{1,0:T(8,128)(2,1)S(1)}, bf16[96,1920]{1,0:T(8,128)(2,1)S(1)}, u32[]{:S(2)}, u32[]{:S(2)}) collective-permute-start(bf16[96,1920]{1,0:T(8,128)(2,1)S(1)} %get-tuple-element.46), channel_id=1, source_target_pairs={{0,5},{1,0},{4,1},{5,4},{2,7},{3,2},{6,3},{7,6},{8,13},{9,8},{12,9... | collective-permute-start | bytes 1105928 | tf_op jit(solution)/shard_map/ppermute | solution.py:291
  109.0 4.2 %collective-permute-done.4 = bf16[96,1152]{1,0:T(8,128)(2,1)S(1)} collective-permute-done((bf16[96,1152]{1,0:T(8,128)(2,1)S(1)}, bf16[96,1152]{1,0:T(8,128)(2,1)S(1)}, u32[]{:S(2)}, u32[]{:S(2)}) %collective-permute-start.4) | collective-permute-done | bytes 221216 | tf_op jit(solution)/shard_map/ppermute | solution.py:291
  113.2 0.0 collective-permute-done.3
  113.2 1.2 fusion.5
  114.4 5.9 %collective-permute-done.5 = bf16[96,1920]{1,0:T(8,128)(2,1)S(1)} collective-permute-done((bf16[96,1920]{1,0:T(8,128)(2,1)S(1)}, bf16[96,1920]{1,0:T(8,128)(2,1)S(1)}, u32[]{:S(2)}, u32[]{:S(2)}) %collective-permute-start.5) | collective-permute-done | bytes 368672 | tf_op jit(solution)/shard_map/ppermute | solution.py:291
  120.3 7.4 %collective-permute-done.7 = bf16[96,1920]{1,0:T(8,128)(2,1)S(1)} collective-permute-done((bf16[96,1920]{1,0:T(8,128)(2,1)S(1)}, bf16[96,1920]{1,0:T(8,128)(2,1)S(1)}, u32[]{:S(2)}, u32[]{:S(2)}) %collective-permute-start.7) | collective-permute-done | bytes 368672 | tf_op jit(solution)/shard_map/ppermute | solution.py:291
  127.8 0.0 collective-permute-done.6
  127.8 1.2 fusion.2
  129.0 0.9 pad_maximum_fusion
  129.9 2.1 %reshape.87 = bf16[16,144,128]{2,1,0:T(8,128)(2,1)} reshape(bf16[96,3072]{1,0:T(8,128)(2,1)} %pad_maximum_fusion) | data formatting | bytes 1179648 | tf_op jit(solution)/shard_map/reshape | solution.py:308
  132.0 0.0 all-to-all-done.3
  132.0 7.0 %all-to-all-start.4 = ((bf16[16,144,128]{2,1,0:T(8,128)(2,1)}), bf16[16,144,128]{2,1,0:T(8,128)(2,1)}, u32[]{:S(2)}, u32[]{:S(2)}) async-start(bf16[16,144,128]{2,1,0:T(8,128)(2,1)} %reshape.87), calls=%async_computation.4 | async-start | bytes 1179648 | tf_op jit(solution)/shard_map/all_to_all | solution.py:308
  139.0 11.0 %all-to-all-done.4 = bf16[16,144,128]{2,1,0:T(8,128)(2,1)} async-done(((bf16[16,144,128]{2,1,0:T(8,128)(2,1)}), bf16[16,144,128]{2,1,0:T(8,128)(2,1)}, u32[]{:S(2)}, u32[]{:S(2)}) %all-to-all-start.4) | async-done | bytes 589856 | tf_op jit(solution)/shard_map/all_to_all | solution.py:308
  149.9 1.2 convert_reduce_fusion
  151.2 0.6 copy.12
  151.8 0.7 copy.11
  152.5 1.1 copy.15
  153.6 1.1 copy.16
  (8 shorter events, 0.1 us)
Async XLA Ops:
  31.3 26.4 %all-to-all-start = ((bf16[16,64,768]{2,1,0:T(8,128)(2,1)}), bf16[16,64,768]{2,1,0:T(8,128)(2,1)S(1)}, u32[]{:S(2)}, u32[]{:S(2)}) async-start(bf16[16,64,768]{2,1,0:T(8,128)(2,1)} %bitcast.2), calls=%async_computation | async-start | bytes 3145728 | tf_op jit(solution)/shard_map/all_to_all | solution.py:286
  57.6 1.2 copy-start
  58.8 30.1 %all-to-all-start.2 = ((bf16[16,64,768]{2,1,0:T(8,128)(2,1)}), bf16[16,64,768]{2,1,0:T(8,128)(2,1)S(1)}, u32[]{:S(2)}, u32[]{:S(2)}) async-start(bf16[16,64,768]{2,1,0:T(8,128)(2,1)} %bitcast.48), calls=%async_computation.2 | async-start | bytes 3145728 | tf_op jit(solution)/shard_map/all_to_all | solution.py:286
  76.5 19.3 %collective-permute-start = (bf16[4,96,1920]{2,1,0:T(8,128)(2,1)}, bf16[4,96,1920]{2,1,0:T(8,128)(2,1)}, u32[]{:S(2)}, u32[]{:S(2)}) collective-permute-start(bf16[4,96,1920]{2,1,0:T(8,128)(2,1)} %get-tuple-element.27), channel_id=1, source_target_pairs={{0,2},{2,0},{1,3},{3,1},{4,6},{6,4},{5,7},{7,5},{8,10},{10,8},{9,1... | collective-permute-start | bytes 4423688 | tf_op jit(solution)/shard_map/ppermute | solution.py:291
  88.3 7.6 %collective-permute-start.1 = (bf16[4,96,1152]{2,1,0:T(8,128)(2,1)}, bf16[4,96,1152]{2,1,0:T(8,128)(2,1)}, u32[]{:S(2)}, u32[]{:S(2)}) collective-permute-start(bf16[4,96,1152]{2,1,0:T(8,128)(2,1)} %get-tuple-element.32), channel_id=1, source_target_pairs={{0,2},{2,0},{1,3},{3,1},{4,6},{6,4},{5,7},{7,5},{8,10},{10,8},{9,1... | collective-permute-start | bytes 2654216 | tf_op jit(solution)/shard_map/ppermute | solution.py:291
  88.9 43.1 %all-to-all-start.3 = ((bf16[16,64,768]{2,1,0:T(8,128)(2,1)}), bf16[16,64,768]{2,1,0:T(8,128)(2,1)S(1)}, u32[]{:S(2)}, u32[]{:S(2)}) async-start(bf16[16,64,768]{2,1,0:T(8,128)(2,1)} %bitcast.47), calls=%async_computation.3 | async-start | bytes 3145728 | tf_op jit(solution)/shard_map/all_to_all | solution.py:286
  95.9 7.6 %copy-start.1 = (bf16[4,96,1920]{2,1,0:T(8,128)(2,1)S(1)}, bf16[4,96,1920]{2,1,0:T(8,128)(2,1)}, u32[]{:S(2)}) copy-start(bf16[4,96,1920]{2,1,0:T(8,128)(2,1)} %get-tuple-element.38) | copy-start | bytes 4423684
  97.6 8.9 %collective-permute-start.2 = (bf16[96,1152]{1,0:T(8,128)(2,1)S(1)}, bf16[96,1152]{1,0:T(8,128)(2,1)S(1)}, u32[]{:S(2)}, u32[]{:S(2)}) collective-permute-start(bf16[96,1152]{1,0:T(8,128)(2,1)S(1)} %get-tuple-element.47), channel_id=1, source_target_pairs={{0,1},{1,4},{4,5},{5,0},{2,3},{3,6},{6,7},{7,2},{8,9},{9,12},{12,1... | collective-permute-start | bytes 663560 | tf_op jit(solution)/shard_map/ppermute | solution.py:291
  99.2 14.0 %collective-permute-start.4 = (bf16[96,1152]{1,0:T(8,128)(2,1)S(1)}, bf16[96,1152]{1,0:T(8,128)(2,1)S(1)}, u32[]{:S(2)}, u32[]{:S(2)}) collective-permute-start(bf16[96,1152]{1,0:T(8,128)(2,1)S(1)} %get-tuple-element.48), channel_id=1, source_target_pairs={{0,4},{1,5},{4,0},{5,1},{2,6},{3,7},{6,2},{7,3},{8,12},{9,13},{12,... | collective-permute-start | bytes 663560 | tf_op jit(solution)/shard_map/ppermute | solution.py:291
  102.1 11.1 %collective-permute-start.3 = (bf16[96,1152]{1,0:T(8,128)(2,1)S(1)}, bf16[96,1152]{1,0:T(8,128)(2,1)S(1)}, u32[]{:S(2)}, u32[]{:S(2)}) collective-permute-start(bf16[96,1152]{1,0:T(8,128)(2,1)S(1)} %get-tuple-element.49), channel_id=1, source_target_pairs={{0,5},{1,0},{4,1},{5,4},{2,7},{3,2},{6,3},{7,6},{8,13},{9,8},{12,9... | collective-permute-start | bytes 663560 | tf_op jit(solution)/shard_map/ppermute | solution.py:291
  105.0 15.4 %collective-permute-start.5 = (bf16[96,1920]{1,0:T(8,128)(2,1)S(1)}, bf16[96,1920]{1,0:T(8,128)(2,1)S(1)}, u32[]{:S(2)}, u32[]{:S(2)}) collective-permute-start(bf16[96,1920]{1,0:T(8,128)(2,1)S(1)} %get-tuple-element.44), channel_id=1, source_target_pairs={{0,1},{1,4},{4,5},{5,0},{2,3},{3,6},{6,7},{7,2},{8,9},{9,12},{12,1... | collective-permute-start | bytes 1105928 | tf_op jit(solution)/shard_map/ppermute | solution.py:291
  105.7 22.0 %collective-permute-start.7 = (bf16[96,1920]{1,0:T(8,128)(2,1)S(1)}, bf16[96,1920]{1,0:T(8,128)(2,1)S(1)}, u32[]{:S(2)}, u32[]{:S(2)}) collective-permute-start(bf16[96,1920]{1,0:T(8,128)(2,1)S(1)} %get-tuple-element.45), channel_id=1, source_target_pairs={{0,4},{1,5},{4,0},{5,1},{2,6},{3,7},{6,2},{7,3},{8,12},{9,13},{12,... | collective-permute-start | bytes 1105928 | tf_op jit(solution)/shard_map/ppermute | solution.py:291
  106.5 21.3 %collective-permute-start.6 = (bf16[96,1920]{1,0:T(8,128)(2,1)S(1)}, bf16[96,1920]{1,0:T(8,128)(2,1)S(1)}, u32[]{:S(2)}, u32[]{:S(2)}) collective-permute-start(bf16[96,1920]{1,0:T(8,128)(2,1)S(1)} %get-tuple-element.46), channel_id=1, source_target_pairs={{0,5},{1,0},{4,1},{5,4},{2,7},{3,2},{6,3},{7,6},{8,13},{9,8},{12,9... | collective-permute-start | bytes 1105928 | tf_op jit(solution)/shard_map/ppermute | solution.py:291
  132.0 18.0 %all-to-all-start.4 = ((bf16[16,144,128]{2,1,0:T(8,128)(2,1)}), bf16[16,144,128]{2,1,0:T(8,128)(2,1)}, u32[]{:S(2)}, u32[]{:S(2)}) async-start(bf16[16,144,128]{2,1,0:T(8,128)(2,1)} %reshape.87), calls=%async_computation.4 | async-start | bytes 1179648 | tf_op jit(solution)/shard_map/all_to_all | solution.py:308

commit v2 on v1

v2 whole, which is shorter than its diff:
```python
import functools
import math

import jax
import jax.numpy as jnp
from jax import lax
from jax.experimental import pallas as pl
from jax.experimental.pallas import tpu as pltpu
from jax.sharding import Mesh
from jax.sharding import PartitionSpec as P

RING = ("x", "z")
COLUMN = ("yh", "yl")
SEQ = ("x", "z", "yh", "c")
BF = jnp.bfloat16
F32 = jnp.float32
BLOCK = 256
VMEM_BYTES = 52 * 1024 * 1024


def gelu_parts(value):
    cdf = 0.5 * (1.0 + lax.erf(value * (1.0 / math.sqrt(2.0))))
    density = jnp.exp(-0.5 * value * value) * (1.0 / math.sqrt(2.0 * math.pi))
    return (value * cdf).astype(BF), (cdf + value * density).astype(BF)


def dot(left, right):
    return jnp.dot(left, right, preferred_element_type=F32)


def dot_t(left, right):
    return lax.dot_general(left, right, (((1,), (1,)), ((), ())), preferred_element_type=F32)


def dot_rows(left, right):
    return lax.dot_general(left, right, (((0,), (0,)), ((), ())), preferred_element_type=F32)


def ring_rows(ref, start, count):
    total = ref.shape[0]
    start %= total
    if start + count <= total:
        return ref[start : start + count, :]
    first = total - start
    return jnp.concatenate([ref[start:total, :], ref[: count - first, :]], axis=0)


class Fetched:
    def __init__(self, copies, target):
        self.copies, self.target, self.here = copies, target, False

    def start(self):
        for copy in self.copies:
            copy.start()

    def get(self):
        if not self.here:
            for copy in self.copies:
                copy.wait()
            self.here = True
        return self.target


class Sent:
    def __init__(self, source, copies):
        self.source, self.copies = source, copies

    def send(self):
        for copy in self.copies:
            copy.start()

    def finish(self):
        for copy in self.copies:
            copy.wait()


def get_then(wanted, following):
    refs = [f.get() for f in wanted]
    for f in following:
        f.start()
    return refs


class Flat:
    def __init__(self, array, b):
        self.array, self.b = array, b
        taps, chans, mids = array.shape[1:]
        self.shape = (chans, taps * mids)

    def copies(self, source, target, sems):
        mids = self.array.shape[-1]
        return [
            pltpu.make_async_copy(
                source.at[self.b, k], target.at[:, k * mids : (k + 1) * mids], sems.at[k]
            )
            for k in range(3)
        ]


class Plain:
    def __init__(self, array, b=None, anywhere=False):
        self.array, self.b, self.anywhere = array, b, anywhere
        self.shape = array.shape if b is None else array.shape[1:]

    def copies(self, source, target, sems):
        source = source if self.b is None else source.at[self.b]
        return [pltpu.make_async_copy(source, target, sems.at[0])]


def staged_call(body, name, ins, outs, scratch, urgent, place=None):
    kept_outs = [pltpu.VMEM(shape, BF) for shape, _ in outs]
    held = [pltpu.VMEM(x.shape, BF) for x in ins] + kept_outs
    results = [(i, k) for i, (_, count) in enumerate(outs) for k in range(count or 1)]
    n, m, held_n = len(ins), len(results), len(held)
    extra = [] if place is None else [place]

    def kernel(*refs):
        head, refs = refs[: len(extra)], refs[len(extra) :]
        sources, targets, kept = refs[:n], refs[n : n + m], refs[n + m : n + m + held_n]
        in_sems, out_sems = refs[n + m + held_n], refs[n + m + held_n + 1]
        rest = refs[n + m + held_n + 2 :]
        fetched = [
            Fetched(x.copies(sources[i], kept[i], in_sems.at[i]), kept[i])
            for i, x in enumerate(ins)
        ]
        for f in fetched[:urgent]:
            f.start()
        sent = [Sent(kept[n + i], []) for i in range(len(outs))]
        for j, (i, k) in enumerate(results):
            source = kept[n + i] if outs[i][1] is None else kept[n + i].at[k]
            sent[i].copies.append(pltpu.make_async_copy(source, targets[j], out_sems.at[j]))
        body(fetched, sent, *head, *rest)
        for result in sent:
            result.finish()

    def out_shape(i):
        shape, count = outs[i]
        return pltpu.HBM(shape if count is None else shape[1:], BF)

    return pl.pallas_call(
        kernel,
        out_shape=[out_shape(i) for i, _ in results],
        in_specs=[pl.BlockSpec(memory_space=pltpu.SMEM)] * len(extra)
        + [pl.BlockSpec(memory_space=pl.ANY if anywhere(x) else pltpu.HBM) for x in ins],
        out_specs=[pl.BlockSpec(memory_space=pltpu.HBM)] * m,
        scratch_shapes=held
        + [pltpu.SemaphoreType.DMA((n, 3)), pltpu.SemaphoreType.DMA((m,))]
        + list(scratch),
        compiler_params=pltpu.CompilerParams(vmem_limit_bytes=VMEM_BYTES),
        cost_estimate=pl.CostEstimate(flops=1, bytes_accessed=1, transcendentals=0),
        name=name,
    )(
        *extra,
        *[
            x.array if anywhere(x) else pltpu.with_memory_space_constraint(x.array, pltpu.HBM)
            for x in ins
        ],
    )


def anywhere(operand):
    return getattr(operand, "anywhere", False)


def settled(array):
    return array * lax.optimization_barrier(jnp.ones((), array.dtype))


def forward(state, conv, proj, step):
    total, chans = state.shape
    mids = conv.shape[-1]
    wide, thin = ((total, chans), None), ((total, mids), None)
    starts = range(0, total, BLOCK)

    def body(fetched, sent, mid_ref):
        out, saved = sent[0], (sent[1:5], sent[5:9])

        def enter(b, start, value):
            rows = slice(start, start + BLOCK)
            feature, slope = gelu_parts(value)
            saved[b][0].source[rows, :] = feature
            saved[b][1].source[rows, :] = slope

        (x_ref,) = get_then(fetched[:1], fetched[1:])
        for start in starts:
            enter(0, start, x_ref[start : start + BLOCK, :].astype(F32))
        saved[0][0].send()
        saved[0][1].send()
        for b in range(2):
            feature_ref, activ_ref, slope_ref = (saved[b][i].source for i in (0, 2, 3))
            conv_ref, proj_ref = fetched[1 + 2 * b].get(), fetched[2 + 2 * b].get()
            source = x_ref if b == 0 else mid_ref
            shift = step * 2**b
            for start in starts:
                rows = slice(start, start + BLOCK)
                pre = (
                    dot(ring_rows(feature_ref, start - shift, BLOCK), conv_ref[0])
                    + dot(feature_ref[rows, :], conv_ref[1])
                    + dot(ring_rows(feature_ref, start + shift, BLOCK), conv_ref[2])
                )
                activ, slope = gelu_parts(pre)
                activ_ref[rows, :] = activ
                slope_ref[rows, :] = slope
                after = source[rows, :].astype(F32) + dot(activ, proj_ref[...])
                after = after.astype(BF)
                if b == 0:
                    mid_ref[rows, :] = after
                    enter(1, start, after.astype(F32))
                else:
                    out.source[rows, :] = after
            for result in saved[0][2:] + saved[1][:2] if b == 0 else [*saved[1][2:], out]:
                result.send()

    outs = staged_call(
        body, "forward",
        [Plain(state, anywhere=True)] + [Plain(x, b) for b in range(2) for x in (conv, proj)],
        [wide] + [wide, wide, thin, thin] * 2, [pltpu.VMEM((total, chans), BF)], 1,
    )
    return outs[0], (outs[1:5], outs[5:9])


def put_ring_rows(ref, start, columns, value):
    total, count = ref.shape[0], value.shape[0]
    start %= total
    first = min(count, total - start)
    ref[start : start + first, columns] = value[:first]
    if first < count:
        ref[: count - first, columns] = value[first:]


def pull(from_ref, proj_ref, slope_ref, taps_ref, shift):
    total, mids = slope_ref.shape
    for start in range(0, total, BLOCK):
        rows = slice(start, start + BLOCK)
        pulled = dot_t(from_ref[rows, :], proj_ref[...])
        e = (pulled * slope_ref[rows, :].astype(F32)).astype(BF)
        for k in range(3):
            columns = slice(k * mids, (k + 1) * mids)
            put_ring_rows(taps_ref, start + (k - 1) * shift, columns, e)


def grow(from_ref, taps_ref, flat_ref, slope_ref, out_ref):
    for start in range(0, from_ref.shape[0], BLOCK):
        rows = slice(start, start + BLOCK)
        summed = dot_t(taps_ref[rows, :], flat_ref[...])
        grown = from_ref[rows, :].astype(F32) + summed * slope_ref[rows, :].astype(F32)
        out_ref[rows, :] = grown.astype(BF)


def weight_terms(left_ref, right_ref, sum_ref, at):
    chans, wide = left_ref.shape[1], right_ref.shape[1]
    for first in range(0, chans, BLOCK):
        some = slice(first, first + BLOCK)
        sum_ref[some, at : at + wide] = dot_rows(left_ref[:, some], right_ref[...])


def put_in_order(place_ref, sum_ref, order_ref, part_ref):
    share = sum_ref.shape[0] // 128
    for c in range(2):
        for y in range(4):
            at = order_ref.at[c * 4 + y]
            for ring in range(16):
                owner = ((ring * 2 + y // 2) * 2 + c) * 2 + y % 2
                at[ring * share : (ring + 1) * share, :] = sum_ref[
                    owner * share : (owner + 1) * share, :
                ]
            half, slot = (c + place_ref[0]) % 2, (y + 4 - place_ref[1]) % 4
            part_ref[half, slot] = at[...].astype(BF)


def backward(grad, saved, conv, proj, step, place):
    total, chans = grad.shape
    mids = conv.shape[-1]
    rows, wide = 16 * (chans // 128), 4 * mids
    ins = [Plain(grad, anywhere=True)]
    for b in (1, 0):
        feature, slope_in, activ, slope = saved[b]
        ins += [Plain(proj, b), Plain(slope), Plain(feature), Plain(activ)]
        ins += [Flat(conv, b), Plain(slope_in)]

    def body(fetched, sent, place_ref, grown_ref, taps_ref, sum_ref, order_ref):
        (grad_ref,), queue = get_then(fetched[:1], []), fetched[1:] + [None] * 6
        for b in (1, 0):
            mine, queue = queue[:6], queue[6:]
            ahead = [f for f in queue[:6] if f is not None]
            out_ref = grown_ref if b == 1 else sent[0].source
            proj_ref, slope_ref = get_then(mine[:2], mine[2:] if b == 1 else [])
            pull(grad_ref, proj_ref, slope_ref, taps_ref, step * 2**b)
            feature_ref, activ_ref = get_then(mine[2:4], [])
            weight_terms(feature_ref, taps_ref, sum_ref, 0)
            weight_terms(grad_ref, activ_ref, sum_ref, 3 * mids)
            flat_ref, slope_in_ref = get_then(mine[4:], ahead)
            grow(grad_ref, taps_ref, flat_ref, slope_in_ref, out_ref)
            if b == 0:
                sent[0].send()
            put_in_order(place_ref, sum_ref, order_ref, sent[2 - b].source)
            sent[2 - b].send()
            grad_ref = out_ref

    part = ((2, 4, rows, wide), 2)
    return staged_call(
        body, "backward", ins, [((total, chans), None), part, part],
        [
            pltpu.VMEM((total, chans), BF),
            pltpu.VMEM((total, 3 * mids), BF),
            pltpu.VMEM((chans, wide), F32),
            pltpu.VMEM((8, rows, wide), F32),
        ],
        3, place,
    )


def to_rings(block):
    return lax.all_to_all(block, RING, 0, 0, tiled=True)


def passed(block, axis, distance):
    size = lax.axis_size(axis)
    return lax.ppermute(block, axis, [(i, (i + distance) % size) for i in range(size)])


def total_of(parts):
    out = parts[0].astype(F32)
    for part in parts[1:]:
        out = out + part.astype(F32)
    return out


def column_share(mine, came):
    both = [total_of([mine[k], came[k]]).astype(BF) for k in range(4)]
    return total_of([both[0]] + [passed(both[k], COLUMN, k) for k in (1, 3, 2)]).astype(BF)


def ring_step(both, axis):
    pieces = both.reshape(4, -1, both.shape[-1])
    me = lax.axis_index(axis)

    def piece(k):
        return lax.dynamic_index_in_dim(pieces, (me + k) % 4, 0, keepdims=False)

    return total_of([piece(0)] + [passed(piece(k), axis, k) for k in (2, 1, 3)])


def local(inputs, cotangent, conv, proj):
    genomes, bins, chans = inputs.shape
    total = genomes * bins
    step = total // 16
    mids = conv.shape[-1]

    def rings(block):
        return to_rings(block.reshape(16, step, chans)).reshape(total, chans)

    def unring(block):
        return to_rings(block.reshape(16, step, chans)).reshape(genomes, bins, chans)

    place = [lax.axis_index("c"), lax.axis_index(COLUMN)]
    place = jnp.stack(place).astype(jnp.int32)
    state = rings(inputs)
    grad = rings(cotangent)
    out, saved = forward(state, conv, proj, step)
    outputs = unring(out)
    grad, mine1, away1, mine0, away0 = backward(grad, saved, conv, proj, step, place)
    input_grad = unring(grad)
    came0, came1 = passed(away0, "c", 1), passed(away1, "c", 1)
    came0, came1, outputs = lax.optimization_barrier((came0, came1, outputs))
    early, late = column_share(mine0, came0), column_share(mine1, came1)
    share = ring_step(jnp.concatenate([early, late], axis=1), "x").astype(BF)
    outputs, input_grad = settled(outputs), settled(input_grad)
    share, outputs, input_grad = lax.optimization_barrier((share, outputs, input_grad))
    share = ring_step(share, "z")
    share = share * jnp.float32(1.0 / math.sqrt(total * 128))
    wide = 3 * mids
    share = share.reshape(-1, 2, 4, mids)
    conv_out = share[:, :, :3].transpose(1, 2, 0, 3)
    proj_out = share[:, :, 3].transpose(1, 2, 0)
    return outputs, input_grad, conv_out, proj_out


def solution(mesh):
    fine = Mesh(mesh.devices.reshape(4, 4, 2, 2, 2), ("x", "z", "yh", "c", "yl"))
    rows = P("yl", SEQ, None)
    in_specs = (rows, rows, P(), P())
    out_specs = (rows, rows, P(None, None, SEQ + ("yl",), None), P(None, None, SEQ + ("yl",)))
    return jax.shard_map(local, mesh=fine, in_specs=in_specs, out_specs=out_specs, check_vma=False)
```

time: 156 us -> 144 us (0.923)
  starting transfers between devices: 32.3 us -> 42.8 us
  waiting for transfers between devices: 37.4 us -> 27.6 us
  Pallas kernels: 39.1 us -> 32.3 us
  local copies, waits for them, and re-layouts: 6.88 us -> 1.46 us
    ppermute x8 -> x14, starting transfers between devices: 10.6 us -> 28.4 us  [passed(): lax.ppermute(block, axis, [(i, (i + distance) % size) for i in range(size)])]
    all_to_all x1 -> x0, waiting for transfers between devices: 11 us -> none  [ring_share(): got = lax.all_to_all(both.reshape(16, -1, 128), RING, 0, 0, tiled=True)]
    all_to_all x1 -> x0, starting transfers between devices: 6.98 us -> none  [ring_share(): got = lax.all_to_all(both.reshape(16, -1, 128), RING, 0, 0, tiled=True)]
    pallas_call x3 -> x2, Pallas kernels: 39.1 us -> 32.3 us  [staged_call(): pl.pallas_call(kernel, out_shape=[out_shape(i) for i, _ in results], in_s...]
    unnamed x8 -> x4, local copies, waits for them, and re-layouts: 4.72 us -> 1.27 us
    mul x0 -> x2, other arithmetic: none -> 2.49 us  [settled(): return array * lax.optimization_barrier(jnp.ones((), array.dtype))]
    reshape x1 -> x2, local copies, waits for them, and re-layouts: 2.1 us -> 0.1 us  [the longest x1 0.06 us: ring_step(): pieces = both.reshape(4, -1, both.shape[-1])]
    ppermute x8 -> x14, waiting for transfers between devices: 17.6 us -> 17.4 us  [passed(): lax.ppermute(block, axis, [(i, (i + distance) % size) for i in range(size)])]
  transfers between devices with their start and end apart: 12 -> 17, of which waited for: 5 -> 9; matrix products, arithmetic and copies ran while one was open for 6% -> 6% of each run, Pallas kernels for 25% -> 22%
where the time goes in v2:
time: 144 us
  starting transfers between devices  42.8 us (30%)
  Pallas kernels  32.3 us (22%)
  blocking collectives  30.5 us (21%)
  waiting for transfers between devices  27.6 us (19%)
  other arithmetic  8.19 us (6%)
  local copies, waits for them, and re-layouts  1.46 us (1%)
    pallas_call x2, Pallas kernels, staged_call(): pl.pallas_call(kernel, out_shape=[out_shape(i) for i, _ in results], in_s...  32.3 us
    all_to_all x1, blocking collectives, to_rings(): return lax.all_to_all(block, RING, 0, 0, tiled=True)  30.5 us
    ppermute x14, starting transfers between devices, passed(): lax.ppermute(block, axis, [(i, (i + distance) % size) for i in range(size)])  28.4 us
    ppermute x14, waiting for transfers between devices, passed(): lax.ppermute(block, axis, [(i, (i + distance) % size) for i in range(size)])  17.4 us
    all_to_all x3, starting transfers between devices, to_rings(): return lax.all_to_all(block, RING, 0, 0, tiled=True)  14.4 us
    all_to_all x3, waiting for transfers between devices, to_rings(): return lax.all_to_all(block, RING, 0, 0, tiled=True)  10.2 us
    convert_element_type x2, other arithmetic, column_share(): both = [total_of([mine[k], came[k]]).astype(BF) for k in range(4)]  3.08 us
  transfers between devices with their start and end apart: 17, of which 9 were waited for; matrix products, arithmetic and copies ran while one was open for 6% of the time, Pallas kernels for 22%

profile of v2, /device:TPU:0, one launch (start us, length us, event | category | flops | bytes accessed | tf_op | source)
XLA Modules:
  0.0 143.7 jit_solution(10910691622965169938)
XLA Ops:
  0.6 30.5 %all_to_all.20 = bf16[16,64,768]{2,1,0:T(8,128)(2,1)S(1)} all-to-all(bf16[16,64,768]{2,1,0:T(8,128)(2,1)} %bitcast.63), channel_id=1, replica_groups=mesh['x'=4,'z'=4,'yh'=2,'c'=2,'yl'=2] {'x','z'}, dimensions={0} | all-to-all | bytes 3145728 | tf_op jit(solution)/shard_map/all_to_all | solution.py:314
  31.2 3.8 %all-to-all-start = ((bf16[16,64,768]{2,1,0:T(8,128)(2,1)}), bf16[16,64,768]{2,1,0:T(8,128)(2,1)S(1)}, u32[]{:S(2)}, u32[]{:S(2)}) async-start(bf16[16,64,768]{2,1,0:T(8,128)(2,1)} %bitcast.64), calls=%async_computation | async-start | bytes 3145728 | tf_op jit(solution)/shard_map/all_to_all | solution.py:314
  35.0 12.6 %forward.1 = (bf16[1024,768]{1,0:T(8,128)(2,1)}, bf16[1024,768]{1,0:T(8,128)(2,1)}, bf16[1024,768]{1,0:T(8,128)(2,1)}, bf16[1024,384]{1,0:T(8,128)(2,1)}, bf16[1...) custom-call(bf16[1024,768]{1,0:T(8,128)(2,1)S(1)} %bitcast.59, ...), custom_call_target="tpu_custom_call" | custom-call | flops 1 | bytes 1 | tf_op jit(solution)/shard_map/forward/pallas_call | solution.py:140
  47.6 9.9 %all-to-all-done = bf16[16,64,768]{2,1,0:T(8,128)(2,1)S(1)} async-done(((bf16[16,64,768]{2,1,0:T(8,128)(2,1)}), bf16[16,64,768]{2,1,0:T(8,128)(2,1)S(1)}, u32[]{:S(2)}, u32[]{:S(2)}) %all-to-all-start) | async-done | bytes 1572896 | tf_op jit(solution)/shard_map/all_to_all | solution.py:314
  57.5 3.7 %all-to-all-start.2 = ((bf16[16,64,768]{2,1,0:T(8,128)(2,1)}), bf16[16,64,768]{2,1,0:T(8,128)(2,1)S(1)}, u32[]{:S(2)}, u32[]{:S(2)}) async-start(bf16[16,64,768]{2,1,0:T(8,128)(2,1)} %bitcast.66), calls=%async_computation.2 | async-start | bytes 3145728 | tf_op jit(solution)/shard_map/all_to_all | solution.py:314
  61.2 0.1 pad_add_fusion.refs_0_
  61.3 19.7 %backward.1 = (bf16[1024,768]{1,0:T(8,128)(2,1)}, bf16[4,96,1536]{2,1,0:T(8,128)(2,1)}, bf16[4,96,1536]{2,1,0:T(8,128)(2,1)}, bf16[4,96,1536]{2,1,0:T(8,128)(2,1)}, bf16[4,96,1536]{2,1,0:T(8,128)(2,1)}) custom-call(s32[2]{0:T(128)S(1)} %pad_add_fusion.refs_0_, bf16[1024,768]{1,0:T(8,128)(2,1)S(1)} %bitcast.58, bf16[2,384,768]{2,1,0:T(8,128)(2,1)} %refs_8_.1, ...), custom_call_target="tpu_custom_call" | custom-call | flops 1 | bytes 1 | tf_op jit(solution)/shard_map/backward/pallas_call | solution.py:140
  81.0 0.1 collective-permute-start
  81.1 0.5 collective-permute-start.1
  81.6 0.3 all-to-all-done.2
  81.9 6.9 %all-to-all-start.3 = ((bf16[16,64,768]{2,1,0:T(8,128)(2,1)}), bf16[16,64,768]{2,1,0:T(8,128)(2,1)S(1)}, u32[]{:S(2)}, u32[]{:S(2)}) async-start(bf16[16,64,768]{2,1,0:T(8,128)(2,1)} %bitcast.65), calls=%async_computation.3 | async-start | bytes 3145728 | tf_op jit(solution)/shard_map/all_to_all | solution.py:314
  88.8 0.0 copy-start
  88.8 0.0 collective-permute-done
  88.8 0.0 collective-permute-done.1
  88.8 1.7 %fusion.7 = (bf16[96,1536]{1,0:T(8,128)(2,1)S(1)}, bf16[96,1536]{1,0:T(8,128)(2,1)S(1)}, bf16[96,1536]{1,0:T(8,128)(2,1)S(1)}) fusion(bf16[4,96,1536]{2,1,0:T(8,128)(2,1)} %collective-permute-done, bf16[4,96,1536]{2,1,0:T(8,128)(2,1)} %get-tuple-element.32), kind=kLoop, calls=%fused_computation.20 | loop fusion | flops 1769472 | bytes 2654208 | tf_op jit(solution)/shard_map/convert_element_type | solution.py:330
  90.6 1.6 %collective-permute-start.2 = (bf16[96,1536]{1,0:T(8,128)(2,1)S(1)}, bf16[96,1536]{1,0:T(8,128)(2,1)S(1)}, u32[]{:S(2)}, u32[]{:S(2)}) collective-permute-start(bf16[96,1536]{1,0:T(8,128)(2,1)S(1)} %get-tuple-element.48), channel_id=1, source_target_pairs={{0,1},{1,4},{4,5},{5,0},{2,3},{3,6},{6,7},{7,2},{8,9},{9,12},{12,1... | collective-permute-start | bytes 884744 | tf_op jit(solution)/shard_map/ppermute | solution.py:319
  92.2 1.7 %collective-permute-start.3 = (bf16[96,1536]{1,0:T(8,128)(2,1)S(1)}, bf16[96,1536]{1,0:T(8,128)(2,1)S(1)}, u32[]{:S(2)}, u32[]{:S(2)}) collective-permute-start(bf16[96,1536]{1,0:T(8,128)(2,1)S(1)} %get-tuple-element.50), channel_id=1, source_target_pairs={{0,5},{1,0},{4,1},{5,4},{2,7},{3,2},{6,3},{7,6},{8,13},{9,8},{12,9... | collective-permute-start | bytes 884744 | tf_op jit(solution)/shard_map/ppermute | solution.py:319
  93.9 2.0 %collective-permute-start.4 = (bf16[96,1536]{1,0:T(8,128)(2,1)S(1)}, bf16[96,1536]{1,0:T(8,128)(2,1)S(1)}, u32[]{:S(2)}, u32[]{:S(2)}) collective-permute-start(bf16[96,1536]{1,0:T(8,128)(2,1)S(1)} %get-tuple-element.49), channel_id=1, source_target_pairs={{0,4},{1,5},{4,0},{5,1},{2,6},{3,7},{6,2},{7,3},{8,12},{9,13},{12,... | collective-permute-start | bytes 884744 | tf_op jit(solution)/shard_map/ppermute | solution.py:319
  95.8 0.0 copy-done
  95.8 1.4 fusion.11
  97.2 0.7 collective-permute-start.5
  98.0 2.6 %collective-permute-start.6 = (bf16[96,1536]{1,0:T(8,128)(2,1)S(1)}, bf16[96,1536]{1,0:T(8,128)(2,1)S(1)}, u32[]{:S(2)}, u32[]{:S(2)}) collective-permute-start(bf16[96,1536]{1,0:T(8,128)(2,1)S(1)} %get-tuple-element.53), channel_id=1, source_target_pairs={{0,5},{1,0},{4,1},{5,4},{2,7},{3,2},{6,3},{7,6},{8,13},{9,8},{12,9... | collective-permute-start | bytes 884744 | tf_op jit(solution)/shard_map/ppermute | solution.py:319
  100.5 1.2 broadcast_multiply_fusion.1
  101.8 0.0 collective-permute-done.2
  101.8 8.3 %collective-permute-start.7 = (bf16[96,1536]{1,0:T(8,128)(2,1)S(1)}, bf16[96,1536]{1,0:T(8,128)(2,1)S(1)}, u32[]{:S(2)}, u32[]{:S(2)}) collective-permute-start(bf16[96,1536]{1,0:T(8,128)(2,1)S(1)} %get-tuple-element.52), channel_id=1, source_target_pairs={{0,4},{1,5},{4,0},{5,1},{2,6},{3,7},{6,2},{7,3},{8,12},{9,13},{12,... | collective-permute-start | bytes 884744 | tf_op jit(solution)/shard_map/ppermute | solution.py:319
  110.0 0.0 collective-permute-done.3
  110.0 0.0 collective-permute-done.4
  110.0 1.2 fusion.5
  111.3 2.0 %collective-permute-done.5 = bf16[96,1536]{1,0:T(8,128)(2,1)S(1)} collective-permute-done((bf16[96,1536]{1,0:T(8,128)(2,1)S(1)}, bf16[96,1536]{1,0:T(8,128)(2,1)S(1)}, u32[]{:S(2)}, u32[]{:S(2)}) %collective-permute-start.5) | collective-permute-done | bytes 294944 | tf_op jit(solution)/shard_map/ppermute | solution.py:319
  113.3 5.7 %collective-permute-done.6 = bf16[96,1536]{1,0:T(8,128)(2,1)S(1)} collective-permute-done((bf16[96,1536]{1,0:T(8,128)(2,1)S(1)}, bf16[96,1536]{1,0:T(8,128)(2,1)S(1)}, u32[]{:S(2)}, u32[]{:S(2)}) %collective-permute-start.6) | collective-permute-done | bytes 294944 | tf_op jit(solution)/shard_map/ppermute | solution.py:319
  119.0 1.8 %collective-permute-done.7 = bf16[96,1536]{1,0:T(8,128)(2,1)S(1)} collective-permute-done((bf16[96,1536]{1,0:T(8,128)(2,1)S(1)}, bf16[96,1536]{1,0:T(8,128)(2,1)S(1)}, u32[]{:S(2)}, u32[]{:S(2)}) %collective-permute-start.7) | collective-permute-done | bytes 294944 | tf_op jit(solution)/shard_map/ppermute | solution.py:319
  120.8 1.1 fusion.2
  122.1 2.9 %collective-permute-start.10 = (bf16[24,3072]{1,0:T(8,128)(2,1)S(1)}, bf16[24,3072]{1,0:T(8,128)(2,1)S(1)}, u32[]{:S(2)}, u32[]{:S(2)}) collective-permute-start(bf16[24,3072]{1,0:T(8,128)(2,1)S(1)} %get-tuple-element.55), channel_id=1, source_target_pairs={{0,96},{32,0},{64,32},{96,64},{1,97},{33,1},{65,33},{97,65},{2,98}... | collective-permute-start | bytes 442376 | tf_op jit(solution)/shard_map/ppermute | solution.py:319
  125.0 0.9 collective-permute-start.8
  125.8 0.9 collective-permute-start.9
  126.7 0.0 all-to-all-done.3
  126.7 1.2 broadcast_multiply_fusion
  127.9 2.1 %collective-permute-done.10 = bf16[24,3072]{1,0:T(8,128)(2,1)S(1)} collective-permute-done((bf16[24,3072]{1,0:T(8,128)(2,1)S(1)}, bf16[24,3072]{1,0:T(8,128)(2,1)S(1)}, u32[]{:S(2)}, u32[]{:S(2)}) %collective-permute-start.10) | collective-permute-done | bytes 147488 | tf_op jit(solution)/shard_map/ppermute | solution.py:319
  130.1 2.2 %collective-permute-done.8 = bf16[24,3072]{1,0:T(8,128)(2,1)S(1)} collective-permute-done((bf16[24,3072]{1,0:T(8,128)(2,1)S(1)}, bf16[24,3072]{1,0:T(8,128)(2,1)S(1)}, u32[]{:S(2)}, u32[]{:S(2)}) %collective-permute-start.8) | collective-permute-done | bytes 147488 | tf_op jit(solution)/shard_map/ppermute | solution.py:319
  132.2 1.5 %collective-permute-done.9 = bf16[24,3072]{1,0:T(8,128)(2,1)S(1)} collective-permute-done((bf16[24,3072]{1,0:T(8,128)(2,1)S(1)}, bf16[24,3072]{1,0:T(8,128)(2,1)S(1)}, u32[]{:S(2)}, u32[]{:S(2)}) %collective-permute-start.9) | collective-permute-done | bytes 147488 | tf_op jit(solution)/shard_map/ppermute | solution.py:319
  133.7 0.1 fusion.16
  133.8 0.1 reshape.89
  133.9 3.0 %collective-permute-start.11 = (bf16[6,3072]{1,0:T(8,128)(2,1)S(1)}, bf16[6,3072]{1,0:T(8,128)(2,1)S(1)}, u32[]{:S(2)}, u32[]{:S(2)}) collective-permute-start(bf16[6,3072]{1,0:T(8,128)(2,1)S(1)} %get-tuple-element.57), channel_id=1, source_target_pairs={{0,16},{8,24},{16,0},{24,8},{1,17},{9,25},{17,1},{25,9},{2,18},{10... | collective-permute-start | bytes 110600 | tf_op jit(solution)/shard_map/ppermute | solution.py:319
  137.0 0.6 collective-permute-start.12
  137.5 2.7 %collective-permute-start.13 = (bf16[6,3072]{1,0:T(8,128)(2,1)S(1)}, bf16[6,3072]{1,0:T(8,128)(2,1)S(1)}, u32[]{:S(2)}, u32[]{:S(2)}) collective-permute-start(bf16[6,3072]{1,0:T(8,128)(2,1)S(1)} %get-tuple-element.58), channel_id=1, source_target_pairs={{0,24},{8,0},{16,8},{24,16},{1,25},{9,1},{17,9},{25,17},{2,26},{10... | collective-permute-start | bytes 110600 | tf_op jit(solution)/shard_map/ppermute | solution.py:319
  140.2 0.0 collective-permute-done.11
  140.2 2.1 %collective-permute-done.12 = bf16[6,3072]{1,0:T(8,128)(2,1)S(1)} collective-permute-done((bf16[6,3072]{1,0:T(8,128)(2,1)S(1)}, bf16[6,3072]{1,0:T(8,128)(2,1)S(1)}, u32[]{:S(2)}, u32[]{:S(2)}) %collective-permute-start.12) | collective-permute-done | bytes 36896 | tf_op jit(solution)/shard_map/ppermute | solution.py:319
  142.3 0.0 collective-permute-done.13
  142.4 0.7 copy.8
  143.0 0.6 copy.11
  (7 shorter events, 0.2 us)
Async XLA Ops:
  31.2 26.4 %all-to-all-start = ((bf16[16,64,768]{2,1,0:T(8,128)(2,1)}), bf16[16,64,768]{2,1,0:T(8,128)(2,1)S(1)}, u32[]{:S(2)}, u32[]{:S(2)}) async-start(bf16[16,64,768]{2,1,0:T(8,128)(2,1)} %bitcast.64), calls=%async_computation | async-start | bytes 3145728 | tf_op jit(solution)/shard_map/all_to_all | solution.py:314
  57.5 24.4 %all-to-all-start.2 = ((bf16[16,64,768]{2,1,0:T(8,128)(2,1)}), bf16[16,64,768]{2,1,0:T(8,128)(2,1)S(1)}, u32[]{:S(2)}, u32[]{:S(2)}) async-start(bf16[16,64,768]{2,1,0:T(8,128)(2,1)} %bitcast.66), calls=%async_computation.2 | async-start | bytes 3145728 | tf_op jit(solution)/shard_map/all_to_all | solution.py:314
  81.0 7.8 %collective-permute-start = (bf16[4,96,1536]{2,1,0:T(8,128)(2,1)}, bf16[4,96,1536]{2,1,0:T(8,128)(2,1)}, u32[]{:S(2)}, u32[]{:S(2)}) collective-permute-start(bf16[4,96,1536]{2,1,0:T(8,128)(2,1)} %get-tuple-element.33), channel_id=1, source_target_pairs={{0,2},{2,0},{1,3},{3,1},{4,6},{6,4},{5,7},{7,5},{8,10},{10,8},{9,1... | collective-permute-start | bytes 3538952 | tf_op jit(solution)/shard_map/ppermute | solution.py:319
  81.1 7.7 %collective-permute-start.1 = (bf16[4,96,1536]{2,1,0:T(8,128)(2,1)}, bf16[4,96,1536]{2,1,0:T(8,128)(2,1)}, u32[]{:S(2)}, u32[]{:S(2)}) collective-permute-start(bf16[4,96,1536]{2,1,0:T(8,128)(2,1)} %get-tuple-element.34), channel_id=1, source_target_pairs={{0,2},{2,0},{1,3},{3,1},{4,6},{6,4},{5,7},{7,5},{8,10},{10,8},{9,1... | collective-permute-start | bytes 3538952 | tf_op jit(solution)/shard_map/ppermute | solution.py:319
  81.9 44.8 %all-to-all-start.3 = ((bf16[16,64,768]{2,1,0:T(8,128)(2,1)}), bf16[16,64,768]{2,1,0:T(8,128)(2,1)S(1)}, u32[]{:S(2)}, u32[]{:S(2)}) async-start(bf16[16,64,768]{2,1,0:T(8,128)(2,1)} %bitcast.65), calls=%async_computation.3 | async-start | bytes 3145728 | tf_op jit(solution)/shard_map/all_to_all | solution.py:314
  88.8 7.0 %copy-start = (bf16[4,96,1536]{2,1,0:T(8,128)(2,1)S(1)}, bf16[4,96,1536]{2,1,0:T(8,128)(2,1)}, u32[]{:S(2)}) copy-start(bf16[4,96,1536]{2,1,0:T(8,128)(2,1)} %get-tuple-element.37) | copy-start | bytes 3538948
  90.6 11.2 %collective-permute-start.2 = (bf16[96,1536]{1,0:T(8,128)(2,1)S(1)}, bf16[96,1536]{1,0:T(8,128)(2,1)S(1)}, u32[]{:S(2)}, u32[]{:S(2)}) collective-permute-start(bf16[96,1536]{1,0:T(8,128)(2,1)S(1)} %get-tuple-element.48), channel_id=1, source_target_pairs={{0,1},{1,4},{4,5},{5,0},{2,3},{3,6},{6,7},{7,2},{8,9},{9,12},{12,1... | collective-permute-start | bytes 884744 | tf_op jit(solution)/shard_map/ppermute | solution.py:319
  92.2 17.8 %collective-permute-start.3 = (bf16[96,1536]{1,0:T(8,128)(2,1)S(1)}, bf16[96,1536]{1,0:T(8,128)(2,1)S(1)}, u32[]{:S(2)}, u32[]{:S(2)}) collective-permute-start(bf16[96,1536]{1,0:T(8,128)(2,1)S(1)} %get-tuple-element.50), channel_id=1, source_target_pairs={{0,5},{1,0},{4,1},{5,4},{2,7},{3,2},{6,3},{7,6},{8,13},{9,8},{12,9... | collective-permute-start | bytes 884744 | tf_op jit(solution)/shard_map/ppermute | solution.py:319
  93.9 16.2 %collective-permute-start.4 = (bf16[96,1536]{1,0:T(8,128)(2,1)S(1)}, bf16[96,1536]{1,0:T(8,128)(2,1)S(1)}, u32[]{:S(2)}, u32[]{:S(2)}) collective-permute-start(bf16[96,1536]{1,0:T(8,128)(2,1)S(1)} %get-tuple-element.49), channel_id=1, source_target_pairs={{0,4},{1,5},{4,0},{5,1},{2,6},{3,7},{6,2},{7,3},{8,12},{9,13},{12,... | collective-permute-start | bytes 884744 | tf_op jit(solution)/shard_map/ppermute | solution.py:319
  97.2 16.0 %collective-permute-start.5 = (bf16[96,1536]{1,0:T(8,128)(2,1)S(1)}, bf16[96,1536]{1,0:T(8,128)(2,1)S(1)}, u32[]{:S(2)}, u32[]{:S(2)}) collective-permute-start(bf16[96,1536]{1,0:T(8,128)(2,1)S(1)} %get-tuple-element.51), channel_id=1, source_target_pairs={{0,1},{1,4},{4,5},{5,0},{2,3},{3,6},{6,7},{7,2},{8,9},{9,12},{12,1... | collective-permute-start | bytes 884744 | tf_op jit(solution)/shard_map/ppermute | solution.py:319
  98.0 21.0 %collective-permute-start.6 = (bf16[96,1536]{1,0:T(8,128)(2,1)S(1)}, bf16[96,1536]{1,0:T(8,128)(2,1)S(1)}, u32[]{:S(2)}, u32[]{:S(2)}) collective-permute-start(bf16[96,1536]{1,0:T(8,128)(2,1)S(1)} %get-tuple-element.53), channel_id=1, source_target_pairs={{0,5},{1,0},{4,1},{5,4},{2,7},{3,2},{6,3},{7,6},{8,13},{9,8},{12,9... | collective-permute-start | bytes 884744 | tf_op jit(solution)/shard_map/ppermute | solution.py:319
  101.8 19.0 %collective-permute-start.7 = (bf16[96,1536]{1,0:T(8,128)(2,1)S(1)}, bf16[96,1536]{1,0:T(8,128)(2,1)S(1)}, u32[]{:S(2)}, u32[]{:S(2)}) collective-permute-start(bf16[96,1536]{1,0:T(8,128)(2,1)S(1)} %get-tuple-element.52), channel_id=1, source_target_pairs={{0,4},{1,5},{4,0},{5,1},{2,6},{3,7},{6,2},{7,3},{8,12},{9,13},{12,... | collective-permute-start | bytes 884744 | tf_op jit(solution)/shard_map/ppermute | solution.py:319
  122.1 8.0 %collective-permute-start.10 = (bf16[24,3072]{1,0:T(8,128)(2,1)S(1)}, bf16[24,3072]{1,0:T(8,128)(2,1)S(1)}, u32[]{:S(2)}, u32[]{:S(2)}) collective-permute-start(bf16[24,3072]{1,0:T(8,128)(2,1)S(1)} %get-tuple-element.55), channel_id=1, source_target_pairs={{0,96},{32,0},{64,32},{96,64},{1,97},{33,1},{65,33},{97,65},{2,98}... | collective-permute-start | bytes 442376 | tf_op jit(solution)/shard_map/ppermute | solution.py:319
  125.0 7.2 %collective-permute-start.8 = (bf16[24,3072]{1,0:T(8,128)(2,1)S(1)}, bf16[24,3072]{1,0:T(8,128)(2,1)S(1)}, u32[]{:S(2)}, u32[]{:S(2)}) collective-permute-start(bf16[24,3072]{1,0:T(8,128)(2,1)S(1)} %get-tuple-element.54), channel_id=1, source_target_pairs={{0,64},{32,96},{64,0},{96,32},{1,65},{33,97},{65,1},{97,33},{2,66}... | collective-permute-start | bytes 442376 | tf_op jit(solution)/shard_map/ppermute | solution.py:319
  125.8 7.9 %collective-permute-start.9 = (bf16[24,3072]{1,0:T(8,128)(2,1)S(1)}, bf16[24,3072]{1,0:T(8,128)(2,1)S(1)}, u32[]{:S(2)}, u32[]{:S(2)}) collective-permute-start(bf16[24,3072]{1,0:T(8,128)(2,1)S(1)} %get-tuple-element.56), channel_id=1, source_target_pairs={{0,32},{32,64},{64,96},{96,0},{1,33},{33,65},{65,97},{97,1},{2,34}... | collective-permute-start | bytes 442376 | tf_op jit(solution)/shard_map/ppermute | solution.py:319
  133.9 6.3 %collective-permute-start.11 = (bf16[6,3072]{1,0:T(8,128)(2,1)S(1)}, bf16[6,3072]{1,0:T(8,128)(2,1)S(1)}, u32[]{:S(2)}, u32[]{:S(2)}) collective-permute-start(bf16[6,3072]{1,0:T(8,128)(2,1)S(1)} %get-tuple-element.57), channel_id=1, source_target_pairs={{0,16},{8,24},{16,0},{24,8},{1,17},{9,25},{17,1},{25,9},{2,18},{10... | collective-permute-start | bytes 110600 | tf_op jit(solution)/shard_map/ppermute | solution.py:319
  137.0 5.3 %collective-permute-start.12 = (bf16[6,3072]{1,0:T(8,128)(2,1)S(1)}, bf16[6,3072]{1,0:T(8,128)(2,1)S(1)}, u32[]{:S(2)}, u32[]{:S(2)}) collective-permute-start(bf16[6,3072]{1,0:T(8,128)(2,1)S(1)} %get-tuple-element.59), channel_id=1, source_target_pairs={{0,8},{8,16},{16,24},{24,0},{1,9},{9,17},{17,25},{25,1},{2,10},{10... | collective-permute-start | bytes 110600 | tf_op jit(solution)/shard_map/ppermute | solution.py:319
  137.5 4.7 %collective-permute-start.13 = (bf16[6,3072]{1,0:T(8,128)(2,1)S(1)}, bf16[6,3072]{1,0:T(8,128)(2,1)S(1)}, u32[]{:S(2)}, u32[]{:S(2)}) collective-permute-start(bf16[6,3072]{1,0:T(8,128)(2,1)S(1)} %get-tuple-element.58), channel_id=1, source_target_pairs={{0,24},{8,0},{16,8},{24,16},{1,25},{9,1},{17,9},{25,17},{2,26},{10... | collective-permute-start | bytes 110600 | tf_op jit(solution)/shard_map/ppermute | solution.py:319

commit v3 on v2

--- a/solution.py
+++ b/solution.py
@@ -3,6 +3,7 @@
 
 import jax
 import jax.numpy as jnp
+import numpy as np
 from jax import lax
 from jax.experimental import pallas as pl
 from jax.experimental.pallas import tpu as pltpu
@@ -166,29 +167,43 @@
     return array * lax.optimization_barrier(jnp.ones((), array.dtype))
 
 
+def owner_of(c, y, q):
+    ring = q if c == 0 else q % 4 * 4 + q // 4
+    return ((ring * 2 + y // 2) * 2 + c) * 2 + y % 2
+
+
+def order_of(chans):
+    share = chans // 128
+    owners = [owner_of(c, y, q) for c in range(2) for y in range(4) for q in range(16)]
+    source = np.repeat(np.array(owners) * share, share) + np.tile(np.arange(share), 128)
+    return jnp.asarray(np.arange(chans)[:, None] == source[None, :], BF)
+
+
 def forward(state, conv, proj, step):
     total, chans = state.shape
     mids = conv.shape[-1]
     wide, thin = ((total, chans), None), ((total, mids), None)
     starts = range(0, total, BLOCK)
 
-    def body(fetched, sent, mid_ref):
+    def body(fetched, sent, mid_ref, *feature_refs):
         out, saved = sent[0], (sent[1:5], sent[5:9])
 
         def enter(b, start, value):
             rows = slice(start, start + BLOCK)
             feature, slope = gelu_parts(value)
-            saved[b][0].source[rows, :] = feature
+            feature_refs[b][rows, :] = feature
+            saved[b][0].source[rows, :] = dot(feature, order_ref[...]).astype(BF)
             saved[b][1].source[rows, :] = slope
 
-        (x_ref,) = get_then(fetched[:1], fetched[1:])
+        x_ref, order_ref = get_then(fetched[:2], fetched[2:])
         for start in starts:
             enter(0, start, x_ref[start : start + BLOCK, :].astype(F32))
         saved[0][0].send()
         saved[0][1].send()
         for b in range(2):
-            feature_ref, activ_ref, slope_ref = (saved[b][i].source for i in (0, 2, 3))
-            conv_ref, proj_ref = fetched[1 + 2 * b].get(), fetched[2 + 2 * b].get()
+            feature_ref = feature_refs[b]
+            activ_ref, slope_ref = saved[b][2].source, saved[b][3].source
+            conv_ref, proj_ref = (f.get() for f in fetched[2 + 2 * b : 4 + 2 * b])
             source = x_ref if b == 0 else mid_ref
             shift = step * 2**b
             for start in starts:
@@ -213,8 +228,9 @@
 
     outs = staged_call(
         body, "forward",
-        [Plain(state, anywhere=True)] + [Plain(x, b) for b in range(2) for x in (conv, proj)],
-        [wide] + [wide, wide, thin, thin] * 2, [pltpu.VMEM((total, chans), BF)], 1,
+        [Plain(state, anywhere=True), Plain(order_of(chans))]
+        + [Plain(x, b) for b in range(2) for x in (conv, proj)],
+        [wide] + [wide, wide, thin, thin] * 2, [pltpu.VMEM((total, chans), BF)] * 3, 2,
     )
     return outs[0], (outs[1:5], outs[5:9])
 
@@ -247,31 +263,42 @@
         out_ref[rows, :] = grown.astype(BF)
 
 
-def weight_terms(left_ref, right_ref, sum_ref, at):
-    chans, wide = left_ref.shape[1], right_ref.shape[1]
-    for first in range(0, chans, BLOCK):
-        some = slice(first, first + BLOCK)
-        sum_ref[some, at : at + wide] = dot_rows(left_ref[:, some], right_ref[...])
-
-
-def put_in_order(place_ref, sum_ref, order_ref, part_ref):
-    share = sum_ref.shape[0] // 128
+def slot_of(place_ref, c, y):
+    half, slot = (c + place_ref[0]) % 2, (y + 4 - place_ref[1]) % 4
+    return half * 2 + slot % 2, slot // 2
+
+
+def conv_terms(place_ref, feature_ref, taps_ref, part_ref, at):
+    chans, wide = feature_ref.shape[1], taps_ref.shape[1]
+    rows = chans // 8
+    for c in range(2):
+        half = slice(4 * c * rows, 4 * (c + 1) * rows)
+        terms = dot_rows(feature_ref[:, half], taps_ref[...]).astype(BF)
+        for y in range(4):
+            pair, slot = slot_of(place_ref, c, y)
+            part_ref[pair, slot, :, at : at + wide] = terms[y * rows : (y + 1) * rows]
+
+
+def proj_terms(place_ref, grad_ref, activ_ref, part_ref, at, sum_ref, order_ref):
+    chans, wide = grad_ref.shape[1], activ_ref.shape[1]
+    share = chans // 128
+    sum_ref[...] = dot_rows(grad_ref[...], activ_ref[...])
     for c in range(2):
         for y in range(4):
-            at = order_ref.at[c * 4 + y]
-            for ring in range(16):
-                owner = ((ring * 2 + y // 2) * 2 + c) * 2 + y % 2
-                at[ring * share : (ring + 1) * share, :] = sum_ref[
+            ordered = order_ref.at[c * 4 + y]
+            for q in range(16):
+                owner = owner_of(c, y, q)
+                ordered[q * share : (q + 1) * share, :] = sum_ref[
                     owner * share : (owner + 1) * share, :
                 ]
-            half, slot = (c + place_ref[0]) % 2, (y + 4 - place_ref[1]) % 4
-            part_ref[half, slot] = at[...].astype(BF)
+            pair, slot = slot_of(place_ref, c, y)
+            part_ref[pair, slot, :, at : at + wide] = ordered[...].astype(BF)
 
 
 def backward(grad, saved, conv, proj, step, place):
     total, chans = grad.shape
     mids = conv.shape[-1]
-    rows, wide = 16 * (chans // 128), 4 * mids
+    rows = 16 * (chans // 128)
     ins = [Plain(grad, anywhere=True)]
     for b in (1, 0):
         feature, slope_in, activ, slope = saved[b]
@@ -279,32 +306,33 @@
         ins += [Flat(conv, b), Plain(slope_in)]
 
     def body(fetched, sent, place_ref, grown_ref, taps_ref, sum_ref, order_ref):
-        (grad_ref,), queue = get_then(fetched[:1], []), fetched[1:] + [None] * 6
+        (grad_ref,), queue = get_then(fetched[:1], []), fetched[1:]
+        out, part = sent
         for b in (1, 0):
             mine, queue = queue[:6], queue[6:]
-            ahead = [f for f in queue[:6] if f is not None]
-            out_ref = grown_ref if b == 1 else sent[0].source
+            out_ref = grown_ref if b == 1 else out.source
+            at = 4 * mids * b
             proj_ref, slope_ref = get_then(mine[:2], mine[2:] if b == 1 else [])
             pull(grad_ref, proj_ref, slope_ref, taps_ref, step * 2**b)
             feature_ref, activ_ref = get_then(mine[2:4], [])
-            weight_terms(feature_ref, taps_ref, sum_ref, 0)
-            weight_terms(grad_ref, activ_ref, sum_ref, 3 * mids)
-            flat_ref, slope_in_ref = get_then(mine[4:], ahead)
+            conv_terms(place_ref, feature_ref, taps_ref, part.source, at)
+            proj_terms(
+                place_ref, grad_ref, activ_ref, part.source, at + 3 * mids, sum_ref, order_ref
+            )
+            if b == 0:
+                part.send()
+            flat_ref, slope_in_ref = get_then(mine[4:], queue)
             grow(grad_ref, taps_ref, flat_ref, slope_in_ref, out_ref)
-            if b == 0:
-                sent[0].send()
-            put_in_order(place_ref, sum_ref, order_ref, sent[2 - b].source)
-            sent[2 - b].send()
             grad_ref = out_ref
-
-    part = ((2, 4, rows, wide), 2)
+        out.send()
+
     return staged_call(
-        body, "backward", ins, [((total, chans), None), part, part],
+        body, "backward", ins, [((total, chans), None), ((4, 2, rows, 8 * mids), 4)],
         [
             pltpu.VMEM((total, chans), BF),
             pltpu.VMEM((total, 3 * mids), BF),
-            pltpu.VMEM((chans, wide), F32),
-            pltpu.VMEM((8, rows, wide), F32),
+            pltpu.VMEM((chans, mids), F32),
+            pltpu.VMEM((8, rows, mids), F32),
         ],
         3, place,
     )
@@ -326,19 +354,31 @@
     return out
 
 
-def column_share(mine, came):
-    both = [total_of([mine[k], came[k]]).astype(BF) for k in range(4)]
-    return total_of([both[0]] + [passed(both[k], COLUMN, k) for k in (1, 3, 2)]).astype(BF)
-
-
-def ring_step(both, axis):
-    pieces = both.reshape(4, -1, both.shape[-1])
-    me = lax.axis_index(axis)
+def core_sum(mine, came):
+    return [total_of([mine[k % 2][k // 2], came[k % 2][k // 2]]).astype(BF) for k in range(4)]
+
+
+def column_sum(both):
+    return total_of([both[0]] + [passed(both[k], COLUMN, k) for k in (2, 1, 3)]).astype(BF)
+
+
+def ring_step(rows, second):
+    pieces = rows.reshape(4, -1, rows.shape[-1])
+    x, z, c = (lax.axis_index(axis) for axis in ("x", "z", "c"))
+    me = jnp.where(c == second, x, z)
 
     def piece(k):
         return lax.dynamic_index_in_dim(pieces, (me + k) % 4, 0, keepdims=False)
 
-    return total_of([piece(0)] + [passed(piece(k), axis, k) for k in (2, 1, 3)])
+    def sent(k):
+        route = []
+        for i in range(32):
+            x, z, c = i // 8, i // 2 % 4, i % 2
+            x, z = ((x + k) % 4, z) if c == second else (x, (z + k) % 4)
+            route.append((i, (x * 4 + z) * 2 + c))
+        return lax.ppermute(piece(k), ("x", "z", "c"), route)
+
+    return total_of([piece(0)] + [sent(k) for k in (2, 1, 3)])
 
 
 def local(inputs, cotangent, conv, proj):
@@ -359,15 +399,14 @@
     grad = rings(cotangent)
     out, saved = forward(state, conv, proj, step)
     outputs = unring(out)
-    grad, mine1, away1, mine0, away0 = backward(grad, saved, conv, proj, step, place)
+    grad, *parts = backward(grad, saved, conv, proj, step, place)
     input_grad = unring(grad)
-    came0, came1 = passed(away0, "c", 1), passed(away1, "c", 1)
-    came0, came1, outputs = lax.optimization_barrier((came0, came1, outputs))
-    early, late = column_share(mine0, came0), column_share(mine1, came1)
-    share = ring_step(jnp.concatenate([early, late], axis=1), "x").astype(BF)
+    came = [passed(part, "c", 1) for part in parts[:1:-1]][::-1]
+    *came, outputs = lax.optimization_barrier((*came, outputs))
+    share = ring_step(column_sum(core_sum(parts[:2], came)), 0).astype(BF)
     outputs, input_grad = settled(outputs), settled(input_grad)
     share, outputs, input_grad = lax.optimization_barrier((share, outputs, input_grad))
-    share = ring_step(share, "z")
+    share = ring_step(share, 1)
     share = share * jnp.float32(1.0 / math.sqrt(total * 128))
     wide = 3 * mids
     share = share.reshape(-1, 2, 4, mids)

time: 144 us -> 139 us (0.965)
  starting transfers between devices: 42.8 us -> 32.7 us
  waiting for transfers between devices: 27.6 us -> 30.4 us
    ppermute x14 -> x5, starting transfers between devices: 28.4 us -> 7.01 us  [passed(): lax.ppermute(block, axis, [(i, (i + distance) % size) for i in range(size)])]
    ppermute x0 -> x6, starting transfers between devices: none -> 11 us  [sent(): return lax.ppermute(piece(k), ('x', 'z', 'c'), route)]
    ppermute x0 -> x6, waiting for transfers between devices: none -> 5.37 us  [sent(): return lax.ppermute(piece(k), ('x', 'z', 'c'), route)]
    all_to_all x3, waiting for transfers between devices: 10.2 us -> 7.94 us  [to_rings(): return lax.all_to_all(block, RING, 0, 0, tiled=True)]
    convert_element_type x5 -> x4, other arithmetic: 5.54 us -> 6.79 us  [the longest x2 4.84 us: core_sum(): total_of([mine[k % 2][k // 2], came[k % 2][k // 2]]).astype(BF)]
    ppermute x14 -> x5, waiting for transfers between devices: 17.4 us -> 17.1 us  [passed(): lax.ppermute(block, axis, [(i, (i + distance) % size) for i in range(size)])]
  transfers between devices with their start and end apart: 17 -> 14, of which waited for: 9 -> 10; matrix products, arithmetic and copies ran while one was open for 6% -> 5% of each run, Pallas kernels for 22% -> 24%
where the time goes in v3:
time: 139 us; the launch traced here: 138 us
  Pallas kernels  32.8 us (24%)
  starting transfers between devices  32.7 us (24%)
  blocking collectives  30.5 us (22%)
  waiting for transfers between devices  30.4 us (22%)
  other arithmetic  9.4 us (7%)
  local copies, waits for them, and re-layouts  1.47 us (1%)
    pallas_call x2, Pallas kernels, staged_call(): pl.pallas_call(kernel, out_shape=[out_shape(i) for i, _ in results], in_s...  32.8 us
    all_to_all x1, blocking collectives, to_rings(): return lax.all_to_all(block, RING, 0, 0, tiled=True)  30.5 us
    ppermute x5, waiting for transfers between devices, passed(): lax.ppermute(block, axis, [(i, (i + distance) % size) for i in range(size)])  17.1 us
    all_to_all x3, starting transfers between devices, to_rings(): return lax.all_to_all(block, RING, 0, 0, tiled=True)  14.7 us
    ppermute x6, starting transfers between devices, sent(): return lax.ppermute(piece(k), ('x', 'z', 'c'), route)  11 us
    all_to_all x3, waiting for transfers between devices, to_rings(): return lax.all_to_all(block, RING, 0, 0, tiled=True)  7.94 us
    ppermute x5, starting transfers between devices, passed(): lax.ppermute(block, axis, [(i, (i + distance) % size) for i in range(size)])  7.01 us
    ppermute x6, waiting for transfers between devices, sent(): return lax.ppermute(piece(k), ('x', 'z', 'c'), route)  5.37 us
  transfers between devices with their start and end apart: 14, of which 10 were waited for; matrix products, arithmetic and copies ran while one was open for 5% of the time, Pallas kernels for 24%

profile of v3, /device:TPU:0, one launch (start us, length us, event | category | flops | bytes accessed | tf_op | source)
XLA Modules:
  0.0 138.2 jit_solution(4164443451454483326)
XLA Ops:
  0.6 30.5 %all_to_all.20 = bf16[16,64,768]{2,1,0:T(8,128)(2,1)S(1)} all-to-all(bf16[16,64,768]{2,1,0:T(8,128)(2,1)} %bitcast.52), channel_id=1, replica_groups=mesh['x'=4,'z'=4,'yh'=2,'c'=2,'yl'=2] {'x','z'}, dimensions={0} | all-to-all | bytes 3145728 | tf_op jit(solution)/shard_map/all_to_all | solution.py:342
  31.2 3.8 %all-to-all-start = ((bf16[16,64,768]{2,1,0:T(8,128)(2,1)}), bf16[16,64,768]{2,1,0:T(8,128)(2,1)S(1)}, u32[]{:S(2)}, u32[]{:S(2)}) async-start(bf16[16,64,768]{2,1,0:T(8,128)(2,1)} %bitcast.53), calls=%async_computation | async-start | bytes 3145728 | tf_op jit(solution)/shard_map/all_to_all | solution.py:342
  35.0 15.5 %forward.1 = (bf16[1024,768]{1,0:T(8,128)(2,1)}, bf16[1024,768]{1,0:T(8,128)(2,1)}, bf16[1024,768]{1,0:T(8,128)(2,1)}, bf16[1024,384]{1,0:T(8,128)(2,1)}, bf16[1...) custom-call(bf16[1024,768]{1,0:T(8,128)(2,1)S(1)} %bitcast.48, ...), custom_call_target="tpu_custom_call" | custom-call | flops 1 | bytes 1 | tf_op jit(solution)/shard_map/forward/pallas_call | solution.py:141
  50.5 7.0 %all-to-all-done = bf16[16,64,768]{2,1,0:T(8,128)(2,1)S(1)} async-done(((bf16[16,64,768]{2,1,0:T(8,128)(2,1)}), bf16[16,64,768]{2,1,0:T(8,128)(2,1)S(1)}, u32[]{:S(2)}, u32[]{:S(2)}) %all-to-all-start) | async-done | bytes 1572896 | tf_op jit(solution)/shard_map/all_to_all | solution.py:342
  57.5 3.9 %all-to-all-start.2 = ((bf16[16,64,768]{2,1,0:T(8,128)(2,1)}), bf16[16,64,768]{2,1,0:T(8,128)(2,1)S(1)}, u32[]{:S(2)}, u32[]{:S(2)}) async-start(bf16[16,64,768]{2,1,0:T(8,128)(2,1)} %bitcast.55), calls=%async_computation.2 | async-start | bytes 3145728 | tf_op jit(solution)/shard_map/all_to_all | solution.py:342
  61.4 0.1 pad_add_fusion.refs_0_
  61.5 17.3 %backward.1 = (bf16[1024,768]{1,0:T(8,128)(2,1)}, bf16[2,96,3072]{2,1,0:T(8,128)(2,1)}, bf16[2,96,3072]{2,1,0:T(8,128)(2,1)}, bf16[2,96,3072]{2,1,0:T(8,128)(2,1)}, bf16[2,96,3072]{2,1,0:T(8,128)(2,1)}) custom-call(s32[2]{0:T(128)S(1)} %pad_add_fusion.refs_0_, bf16[1024,768]{1,0:T(8,128)(2,1)S(1)} %bitcast.47, bf16[2,384,768]{2,1,0:T(8,128)(2,1)} %refs_8_.1, ...), custom_call_target="tpu_custom_call" | custom-call | flops 1 | bytes 1 | tf_op jit(solution)/shard_map/backward/pallas_call | solution.py:141
  78.8 0.1 collective-permute-start
  78.9 0.5 collective-permute-start.1
  79.4 3.3 %collective-permute-done = bf16[2,96,3072]{2,1,0:T(8,128)(2,1)S(1)} collective-permute-done((bf16[2,96,3072]{2,1,0:T(8,128)(2,1)}, bf16[2,96,3072]{2,1,0:T(8,128)(2,1)S(1)}, u32[]{:S(2)}, u32[]{:S(2)}) %collective-permute-start) | collective-permute-done | bytes 1179680 | tf_op jit(solution)/shard_map/ppermute | solution.py:347
  82.7 0.0 copy-start.1
  82.7 1.1 collective-permute-done.1
  83.8 0.0 all-to-all-done.2
  83.8 0.0 copy-start.3
  83.8 2.1 %fusion.4 = bf16[96,3072]{1,0:T(8,128)(2,1)} fusion(bf16[2,96,3072]{2,1,0:T(8,128)(2,1)S(1)} %collective-permute-done, bf16[2,96,3072]{2,1,0:T(8,128)(2,1)} %get-tuple-element.32), kind=kLoop, calls=%fused_computation.11 | loop fusion | flops 1179648 | bytes 1769472 | tf_op jit(solution)/shard_map/convert_element_type | solution.py:358
  85.9 3.2 %collective-permute-start.2 = (bf16[96,3072]{1,0:T(8,128)(2,1)}, bf16[96,3072]{1,0:T(8,128)(2,1)}, u32[]{:S(2)}, u32[]{:S(2)}) collective-permute-start(bf16[96,3072]{1,0:T(8,128)(2,1)} %fusion.4), channel_id=1, source_target_pairs={{0,4},{1,5},{4,0},{5,1},{2,6},{3,7},{6,2},{7,3},{8,12},{9,13},{12,... | collective-permute-start | bytes 1769480 | tf_op jit(solution)/shard_map/ppermute | solution.py:347
  89.1 0.0 copy-done.3
  89.1 2.7 %fusion.5 = (bf16[96,3072]{1,0:T(8,128)(2,1)}, bf16[96,3072]{1,0:T(8,128)(2,1)}) fusion(bf16[2,96,3072]{2,1,0:T(8,128)(2,1)} %collective-permute-done.1, bf16[2,96,3072]{2,1,0:T(8,128)(2,1)S(1)} %copy-done.3), kind=kLoop, calls=%fused_computation.12 | loop fusion | flops 2359296 | bytes 3538944 | tf_op jit(solution)/shard_map/convert_element_type | solution.py:358
  91.8 0.0 copy-done.1
  91.8 0.7 collective-permute-start.3
  92.5 2.6 %collective-permute-start.4 = (bf16[96,3072]{1,0:T(8,128)(2,1)}, bf16[96,3072]{1,0:T(8,128)(2,1)}, u32[]{:S(2)}, u32[]{:S(2)}) collective-permute-start(bf16[96,3072]{1,0:T(8,128)(2,1)} %get-tuple-element.49), channel_id=1, source_target_pairs={{0,5},{1,0},{4,1},{5,4},{2,7},{3,2},{6,3},{7,6},{8,13},{9,8},{12,9... | collective-permute-start | bytes 1769480 | tf_op jit(solution)/shard_map/ppermute | solution.py:347
  95.1 7.0 %all-to-all-start.3 = ((bf16[16,64,768]{2,1,0:T(8,128)(2,1)}), bf16[16,64,768]{2,1,0:T(8,128)(2,1)S(1)}, u32[]{:S(2)}, u32[]{:S(2)}) async-start(bf16[16,64,768]{2,1,0:T(8,128)(2,1)} %bitcast.54), calls=%async_computation.3 | async-start | bytes 3145728 | tf_op jit(solution)/shard_map/all_to_all | solution.py:342
  102.1 0.0 copy-start
  102.2 0.0 copy-start.2
  102.2 1.2 broadcast_multiply_fusion.1
  103.4 0.5 collective-permute-done.2
  104.0 11.8 %collective-permute-done.3 = bf16[96,3072]{1,0:T(8,128)(2,1)} collective-permute-done((bf16[96,3072]{1,0:T(8,128)(2,1)}, bf16[96,3072]{1,0:T(8,128)(2,1)}, u32[]{:S(2)}, u32[]{:S(2)}) %collective-permute-start.3) | collective-permute-done | bytes 589856 | tf_op jit(solution)/shard_map/ppermute | solution.py:347
  115.8 0.4 collective-permute-done.4
  116.1 0.0 copy-done
  116.1 0.0 copy-done.2
  116.1 1.9 %fusion.2 = bf16[96,3072]{1,0:T(8,128)(2,1)S(1)} fusion(bf16[96,3072]{1,0:T(8,128)(2,1)} %collective-permute-done.4, bf16[96,3072]{1,0:T(8,128)(2,1)} %collective-permute-done.3, bf16[96,3072]{1,0:T(8,128)(2,1)} %collective-permute-done.2, bf16[2,96,3072]{2,1,0:T(8,128)(2,1)S(1)} %copy-done.2, bf16[2,96,3072]{2,1,0:T(8,128)(2,1)S(1)} %copy-done), kind=kLoop, calls=%fused_computation.3 | loop fusion | flops 3538944 | bytes 3538944 | tf_op jit(solution)/shard_map/convert_element_type | solution.py:362
  118.1 3.2 %collective-permute-start.5 = (bf16[24,3072]{1,0:T(8,128)(2,1)S(1)}, bf16[24,3072]{1,0:T(8,128)(2,1)S(1)}, u32[]{:S(2)}, u32[]{:S(2)}) collective-permute-start(bf16[24,3072]{1,0:T(8,128)(2,1)S(1)} %get-tuple-element.50), channel_id=1, source_target_pairs={{0,64},{2,18},{8,72},{10,26},{16,80},{18,2},{24,88},{26,10},{32,96... | collective-permute-start | bytes 442376 | tf_op jit(solution)/shard_map/ppermute | solution.py:379
  121.3 0.6 collective-permute-start.6
  121.9 2.6 %collective-permute-start.7 = (bf16[24,3072]{1,0:T(8,128)(2,1)S(1)}, bf16[24,3072]{1,0:T(8,128)(2,1)S(1)}, u32[]{:S(2)}, u32[]{:S(2)}) collective-permute-start(bf16[24,3072]{1,0:T(8,128)(2,1)S(1)} %get-tuple-element.51), channel_id=1, source_target_pairs={{0,96},{2,26},{8,104},{10,2},{16,112},{18,10},{24,120},{26,18},{32... | collective-permute-start | bytes 442376 | tf_op jit(solution)/shard_map/ppermute | solution.py:379
  124.6 0.9 all-to-all-done.3
  125.5 1.2 broadcast_multiply_fusion
  126.7 0.0 collective-permute-done.5
  126.7 0.9 collective-permute-done.6
  127.7 0.0 collective-permute-done.7
  127.7 0.1 fusion.9
  127.8 0.1 reshape.71
  127.8 2.8 %collective-permute-start.10 = (bf16[6,3072]{1,0:T(8,128)(2,1)S(1)}, bf16[6,3072]{1,0:T(8,128)(2,1)S(1)}, u32[]{:S(2)}, u32[]{:S(2)}) collective-permute-start(bf16[6,3072]{1,0:T(8,128)(2,1)S(1)} %get-tuple-element.54), channel_id=1, source_target_pairs={{0,24},{2,98},{8,0},{10,106},{16,8},{18,114},{24,16},{26,122},{32,... | collective-permute-start | bytes 110600 | tf_op jit(solution)/shard_map/ppermute | solution.py:379
  130.6 0.8 collective-permute-start.8
  131.5 0.9 collective-permute-start.9
  132.3 0.0 collective-permute-done.10
  132.4 3.8 %collective-permute-done.8 = bf16[6,3072]{1,0:T(8,128)(2,1)S(1)} collective-permute-done((bf16[6,3072]{1,0:T(8,128)(2,1)S(1)}, bf16[6,3072]{1,0:T(8,128)(2,1)S(1)}, u32[]{:S(2)}, u32[]{:S(2)}) %collective-permute-start.8) | collective-permute-done | bytes 36896 | tf_op jit(solution)/shard_map/ppermute | solution.py:379
  136.2 0.5 collective-permute-done.9
  136.9 0.7 copy.9
  137.5 0.6 copy.12
  (6 shorter events, 0.2 us)
Async XLA Ops:
  31.2 26.4 %all-to-all-start = ((bf16[16,64,768]{2,1,0:T(8,128)(2,1)}), bf16[16,64,768]{2,1,0:T(8,128)(2,1)S(1)}, u32[]{:S(2)}, u32[]{:S(2)}) async-start(bf16[16,64,768]{2,1,0:T(8,128)(2,1)} %bitcast.53), calls=%async_computation | async-start | bytes 3145728 | tf_op jit(solution)/shard_map/all_to_all | solution.py:342
  57.5 26.3 %all-to-all-start.2 = ((bf16[16,64,768]{2,1,0:T(8,128)(2,1)}), bf16[16,64,768]{2,1,0:T(8,128)(2,1)S(1)}, u32[]{:S(2)}, u32[]{:S(2)}) async-start(bf16[16,64,768]{2,1,0:T(8,128)(2,1)} %bitcast.55), calls=%async_computation.2 | async-start | bytes 3145728 | tf_op jit(solution)/shard_map/all_to_all | solution.py:342
  78.8 3.9 %collective-permute-start = (bf16[2,96,3072]{2,1,0:T(8,128)(2,1)}, bf16[2,96,3072]{2,1,0:T(8,128)(2,1)S(1)}, u32[]{:S(2)}, u32[]{:S(2)}) collective-permute-start(bf16[2,96,3072]{2,1,0:T(8,128)(2,1)} %get-tuple-element.33), channel_id=1, source_target_pairs={{0,2},{2,0},{1,3},{3,1},{4,6},{6,4},{5,7},{7,5},{8,10},{10,8},{9,1... | collective-permute-start | bytes 3538952 | tf_op jit(solution)/shard_map/ppermute | solution.py:347
  78.9 4.9 %collective-permute-start.1 = (bf16[2,96,3072]{2,1,0:T(8,128)(2,1)}, bf16[2,96,3072]{2,1,0:T(8,128)(2,1)}, u32[]{:S(2)}, u32[]{:S(2)}) collective-permute-start(bf16[2,96,3072]{2,1,0:T(8,128)(2,1)} %get-tuple-element.34), channel_id=1, source_target_pairs={{0,2},{2,0},{1,3},{3,1},{4,6},{6,4},{5,7},{7,5},{8,10},{10,8},{9,1... | collective-permute-start | bytes 3538952 | tf_op jit(solution)/shard_map/ppermute | solution.py:347
  82.7 9.1 %copy-start.1 = (bf16[2,96,3072]{2,1,0:T(8,128)(2,1)}, bf16[2,96,3072]{2,1,0:T(8,128)(2,1)S(1)}, u32[]{:S(2)}) copy-start(bf16[2,96,3072]{2,1,0:T(8,128)(2,1)S(1)} %collective-permute-done) | copy-start | bytes 3538948
  83.8 5.3 %copy-start.3 = (bf16[2,96,3072]{2,1,0:T(8,128)(2,1)S(1)}, bf16[2,96,3072]{2,1,0:T(8,128)(2,1)}, u32[]{:S(2)}) copy-start(bf16[2,96,3072]{2,1,0:T(8,128)(2,1)} %get-tuple-element.37) | copy-start | bytes 3538948
  85.9 18.0 %collective-permute-start.2 = (bf16[96,3072]{1,0:T(8,128)(2,1)}, bf16[96,3072]{1,0:T(8,128)(2,1)}, u32[]{:S(2)}, u32[]{:S(2)}) collective-permute-start(bf16[96,3072]{1,0:T(8,128)(2,1)} %fusion.4), channel_id=1, source_target_pairs={{0,4},{1,5},{4,0},{5,1},{2,6},{3,7},{6,2},{7,3},{8,12},{9,13},{12,... | collective-permute-start | bytes 1769480 | tf_op jit(solution)/shard_map/ppermute | solution.py:347
  91.8 23.9 %collective-permute-start.3 = (bf16[96,3072]{1,0:T(8,128)(2,1)}, bf16[96,3072]{1,0:T(8,128)(2,1)}, u32[]{:S(2)}, u32[]{:S(2)}) collective-permute-start(bf16[96,3072]{1,0:T(8,128)(2,1)} %get-tuple-element.48), channel_id=1, source_target_pairs={{0,1},{1,4},{4,5},{5,0},{2,3},{3,6},{6,7},{7,2},{8,9},{9,12},{12,1... | collective-permute-start | bytes 1769480 | tf_op jit(solution)/shard_map/ppermute | solution.py:347
  92.5 23.6 %collective-permute-start.4 = (bf16[96,3072]{1,0:T(8,128)(2,1)}, bf16[96,3072]{1,0:T(8,128)(2,1)}, u32[]{:S(2)}, u32[]{:S(2)}) collective-permute-start(bf16[96,3072]{1,0:T(8,128)(2,1)} %get-tuple-element.49), channel_id=1, source_target_pairs={{0,5},{1,0},{4,1},{5,4},{2,7},{3,2},{6,3},{7,6},{8,13},{9,8},{12,9... | collective-permute-start | bytes 1769480 | tf_op jit(solution)/shard_map/ppermute | solution.py:347
  95.1 30.4 %all-to-all-start.3 = ((bf16[16,64,768]{2,1,0:T(8,128)(2,1)}), bf16[16,64,768]{2,1,0:T(8,128)(2,1)S(1)}, u32[]{:S(2)}, u32[]{:S(2)}) async-start(bf16[16,64,768]{2,1,0:T(8,128)(2,1)} %bitcast.54), calls=%async_computation.3 | async-start | bytes 3145728 | tf_op jit(solution)/shard_map/all_to_all | solution.py:342
  102.1 14.0 %copy-start = (bf16[2,96,3072]{2,1,0:T(8,128)(2,1)S(1)}, bf16[2,96,3072]{2,1,0:T(8,128)(2,1)}, u32[]{:S(2)}) copy-start(bf16[2,96,3072]{2,1,0:T(8,128)(2,1)} %get-tuple-element.32) | copy-start | bytes 3538948
  102.2 14.0 %copy-start.2 = (bf16[2,96,3072]{2,1,0:T(8,128)(2,1)S(1)}, bf16[2,96,3072]{2,1,0:T(8,128)(2,1)}, u32[]{:S(2)}) copy-start(bf16[2,96,3072]{2,1,0:T(8,128)(2,1)} %copy-done.1) | copy-start | bytes 3538948
  118.1 8.7 %collective-permute-start.5 = (bf16[24,3072]{1,0:T(8,128)(2,1)S(1)}, bf16[24,3072]{1,0:T(8,128)(2,1)S(1)}, u32[]{:S(2)}, u32[]{:S(2)}) collective-permute-start(bf16[24,3072]{1,0:T(8,128)(2,1)S(1)} %get-tuple-element.50), channel_id=1, source_target_pairs={{0,64},{2,18},{8,72},{10,26},{16,80},{18,2},{24,88},{26,10},{32,96... | collective-permute-start | bytes 442376 | tf_op jit(solution)/shard_map/ppermute | solution.py:379
  121.3 6.4 %collective-permute-start.6 = (bf16[24,3072]{1,0:T(8,128)(2,1)S(1)}, bf16[24,3072]{1,0:T(8,128)(2,1)S(1)}, u32[]{:S(2)}, u32[]{:S(2)}) collective-permute-start(bf16[24,3072]{1,0:T(8,128)(2,1)S(1)} %get-tuple-element.52), channel_id=1, source_target_pairs={{0,32},{2,10},{8,40},{10,18},{16,48},{18,26},{24,56},{26,2},{32,64... | collective-permute-start | bytes 442376 | tf_op jit(solution)/shard_map/ppermute | solution.py:379
  121.9 5.8 %collective-permute-start.7 = (bf16[24,3072]{1,0:T(8,128)(2,1)S(1)}, bf16[24,3072]{1,0:T(8,128)(2,1)S(1)}, u32[]{:S(2)}, u32[]{:S(2)}) collective-permute-start(bf16[24,3072]{1,0:T(8,128)(2,1)S(1)} %get-tuple-element.51), channel_id=1, source_target_pairs={{0,96},{2,26},{8,104},{10,2},{16,112},{18,10},{24,120},{26,18},{32... | collective-permute-start | bytes 442376 | tf_op jit(solution)/shard_map/ppermute | solution.py:379
  127.8 4.5 %collective-permute-start.10 = (bf16[6,3072]{1,0:T(8,128)(2,1)S(1)}, bf16[6,3072]{1,0:T(8,128)(2,1)S(1)}, u32[]{:S(2)}, u32[]{:S(2)}) collective-permute-start(bf16[6,3072]{1,0:T(8,128)(2,1)S(1)} %get-tuple-element.54), channel_id=1, source_target_pairs={{0,24},{2,98},{8,0},{10,106},{16,8},{18,114},{24,16},{26,122},{32,... | collective-permute-start | bytes 110600 | tf_op jit(solution)/shard_map/ppermute | solution.py:379
  130.6 5.6 %collective-permute-start.8 = (bf16[6,3072]{1,0:T(8,128)(2,1)S(1)}, bf16[6,3072]{1,0:T(8,128)(2,1)S(1)}, u32[]{:S(2)}, u32[]{:S(2)}) collective-permute-start(bf16[6,3072]{1,0:T(8,128)(2,1)S(1)} %get-tuple-element.53), channel_id=1, source_target_pairs={{0,16},{2,66},{8,24},{10,74},{16,0},{18,82},{24,8},{26,90},{32,48}... | collective-permute-start | bytes 110600 | tf_op jit(solution)/shard_map/ppermute | solution.py:379
  131.5 5.3 %collective-permute-start.9 = (bf16[6,3072]{1,0:T(8,128)(2,1)S(1)}, bf16[6,3072]{1,0:T(8,128)(2,1)S(1)}, u32[]{:S(2)}, u32[]{:S(2)}) collective-permute-start(bf16[6,3072]{1,0:T(8,128)(2,1)S(1)} %get-tuple-element.55), channel_id=1, source_target_pairs={{0,8},{2,34},{8,16},{10,42},{16,24},{18,50},{24,0},{26,58},{32,40}... | collective-permute-start | bytes 110600 | tf_op jit(solution)/shard_map/ppermute | solution.py:379

commit v4 on v3

--- a/solution.py
+++ b/solution.py
@@ -263,23 +263,24 @@
         out_ref[rows, :] = grown.astype(BF)
 
 
-def slot_of(place_ref, c, y):
-    half, slot = (c + place_ref[0]) % 2, (y + 4 - place_ref[1]) % 4
-    return half * 2 + slot % 2, slot // 2
-
-
-def conv_terms(place_ref, feature_ref, taps_ref, part_ref, at):
+def slot_of(place_ref, c, y, b):
+    half, k = (c + place_ref[0]) % 2, (y + 4 - place_ref[1]) % 4
+    early = (k >= 2) if b == 0 else (k == 1) | (k == 2)
+    return half * 2 + jnp.where(early, 0, 1), jnp.where(k % 2 == 0, b, (k + 3) // 2)
+
+
+def conv_terms(place_ref, feature_ref, taps_ref, part_ref, b):
     chans, wide = feature_ref.shape[1], taps_ref.shape[1]
     rows = chans // 8
     for c in range(2):
         half = slice(4 * c * rows, 4 * (c + 1) * rows)
         terms = dot_rows(feature_ref[:, half], taps_ref[...]).astype(BF)
         for y in range(4):
-            pair, slot = slot_of(place_ref, c, y)
-            part_ref[pair, slot, :, at : at + wide] = terms[y * rows : (y + 1) * rows]
-
-
-def proj_terms(place_ref, grad_ref, activ_ref, part_ref, at, sum_ref, order_ref):
+            group, slot = slot_of(place_ref, c, y, b)
+            part_ref[group, slot, :, :wide] = terms[y * rows : (y + 1) * rows]
+
+
+def proj_terms(place_ref, grad_ref, activ_ref, part_ref, b, sum_ref, order_ref):
     chans, wide = grad_ref.shape[1], activ_ref.shape[1]
     share = chans // 128
     sum_ref[...] = dot_rows(grad_ref[...], activ_ref[...])
@@ -291,8 +292,8 @@
                 ordered[q * share : (q + 1) * share, :] = sum_ref[
                     owner * share : (owner + 1) * share, :
                 ]
-            pair, slot = slot_of(place_ref, c, y)
-            part_ref[pair, slot, :, at : at + wide] = ordered[...].astype(BF)
+            group, slot = slot_of(place_ref, c, y, b)
+            part_ref[group, slot, :, 3 * wide :] = ordered[...].astype(BF)
 
 
 def backward(grad, saved, conv, proj, step, place):
@@ -311,14 +312,11 @@
         for b in (1, 0):
             mine, queue = queue[:6], queue[6:]
             out_ref = grown_ref if b == 1 else out.source
-            at = 4 * mids * b
             proj_ref, slope_ref = get_then(mine[:2], mine[2:] if b == 1 else [])
             pull(grad_ref, proj_ref, slope_ref, taps_ref, step * 2**b)
             feature_ref, activ_ref = get_then(mine[2:4], [])
-            conv_terms(place_ref, feature_ref, taps_ref, part.source, at)
-            proj_terms(
-                place_ref, grad_ref, activ_ref, part.source, at + 3 * mids, sum_ref, order_ref
-            )
+            conv_terms(place_ref, feature_ref, taps_ref, part.source, b)
+            proj_terms(place_ref, grad_ref, activ_ref, part.source, b, sum_ref, order_ref)
             if b == 0:
                 part.send()
             flat_ref, slope_in_ref = get_then(mine[4:], queue)
@@ -327,7 +325,7 @@
         out.send()
 
     return staged_call(
-        body, "backward", ins, [((total, chans), None), ((4, 2, rows, 8 * mids), 4)],
+        body, "backward", ins, [((total, chans), None), ((4, 4, rows, 4 * mids), 4)],
         [
             pltpu.VMEM((total, chans), BF),
             pltpu.VMEM((total, 3 * mids), BF),
@@ -355,20 +353,28 @@
 
 
 def core_sum(mine, came):
-    return [total_of([mine[k % 2][k // 2], came[k % 2][k // 2]]).astype(BF) for k in range(4)]
-
-
-def column_sum(both):
-    return total_of([both[0]] + [passed(both[k], COLUMN, k) for k in (2, 1, 3)]).astype(BF)
+    return [total_of([mine[i], came[i]]).astype(BF) for i in range(4)]
+
+
+def column_sum(first, second, beside):
+    two0, two1, right1, left0 = first
+    own0, own1, right0, left1 = second
+    two0, two1 = passed(two0, COLUMN, 1), passed(two1, COLUMN, -1)
+    right1, left0 = passed(right1, COLUMN, 1), passed(left0, COLUMN, -1)
+    right0 = passed(total_of([right0, two0]).astype(BF), COLUMN, 1)
+    left1 = passed(total_of([left1, two1]).astype(BF), COLUMN, -1)
+    right0, left1, beside = lax.optimization_barrier((right0, left1, beside))
+    sums = total_of([own0, left0, right0]), total_of([own1, right1, left1])
+    return jnp.stack(sums).astype(BF), beside
 
 
 def ring_step(rows, second):
-    pieces = rows.reshape(4, -1, rows.shape[-1])
+    pieces = rows.reshape(2, 4, -1, rows.shape[-1])
     x, z, c = (lax.axis_index(axis) for axis in ("x", "z", "c"))
     me = jnp.where(c == second, x, z)
 
     def piece(k):
-        return lax.dynamic_index_in_dim(pieces, (me + k) % 4, 0, keepdims=False)
+        return lax.dynamic_index_in_dim(pieces, (me + k) % 4, 1, keepdims=False)
 
     def sent(k):
         route = []
@@ -401,17 +407,17 @@
     outputs = unring(out)
     grad, *parts = backward(grad, saved, conv, proj, step, place)
     input_grad = unring(grad)
-    came = [passed(part, "c", 1) for part in parts[:1:-1]][::-1]
+    came = [passed(part, "c", 1) for part in parts[2:]]
     *came, outputs = lax.optimization_barrier((*came, outputs))
-    share = ring_step(column_sum(core_sum(parts[:2], came)), 0).astype(BF)
+    first, second = core_sum(parts[0], came[0]), core_sum(parts[1], came[1])
+    share, input_grad = column_sum(first, second, input_grad)
+    share = ring_step(share, 0).astype(BF)
     outputs, input_grad = settled(outputs), settled(input_grad)
     share, outputs, input_grad = lax.optimization_barrier((share, outputs, input_grad))
-    share = ring_step(share, 1)
-    share = share * jnp.float32(1.0 / math.sqrt(total * 128))
-    wide = 3 * mids
-    share = share.reshape(-1, 2, 4, mids)
-    conv_out = share[:, :, :3].transpose(1, 2, 0, 3)
-    proj_out = share[:, :, 3].transpose(1, 2, 0)
+    share = ring_step(share, 1) * jnp.float32(1.0 / math.sqrt(total * 128))
+    share = share.reshape(2, -1, 4, mids)
+    conv_out = share[:, :, :3].transpose(0, 2, 1, 3)
+    proj_out = share[:, :, 3].transpose(0, 2, 1)
     return outputs, input_grad, conv_out, proj_out
 
 

time: 139 us -> 139 us (level)
  waiting for transfers between devices: 30.4 us -> 27.6 us
  other arithmetic: 9.4 us -> 11.2 us
    ppermute x5 -> x8, waiting for transfers between devices: 17.1 us -> 7.97 us  [passed(): lax.ppermute(block, axis, [(i, (i + distance) % size) for i in range(size)])]
    all_to_all x3, waiting for transfers between devices: 7.94 us -> 12.4 us  [to_rings(): return lax.all_to_all(block, RING, 0, 0, tiled=True)]
    all_to_all x3, starting transfers between devices: 14.7 us -> 12.2 us  [to_rings(): return lax.all_to_all(block, RING, 0, 0, tiled=True)]
    ppermute x5 -> x8, starting transfers between devices: 7.01 us -> 9.08 us  [passed(): lax.ppermute(block, axis, [(i, (i + distance) % size) for i in range(size)])]
    another operation x0 -> x1, other arithmetic: none -> 1.88 us
    ppermute x6, waiting for transfers between devices: 5.37 us -> 7.2 us  [sent(): return lax.ppermute(piece(k), ('x', 'z', 'c'), route)]
    convert_element_type x4 -> x3, other arithmetic: 6.79 us -> 5.68 us  [the longest x1 2.68 us: core_sum(): return [total_of([mine[i], came[i]]).astype(BF) for i in range(4)]]
  transfers between devices with their start and end apart: 14 -> 17, of which waited for: 10 -> 10; matrix products, arithmetic and copies ran while one was open for 5% -> 6% of each run, Pallas kernels for 24% -> 24%
where the time goes in v4:
time: 139 us; the launch traced here: 138 us
  starting transfers between devices  32.8 us (24%)
  Pallas kernels  32.8 us (24%)
  blocking collectives  30.5 us (22%)
  waiting for transfers between devices  27.6 us (20%)
  other arithmetic  11.2 us (8%)
  local copies, waits for them, and re-layouts  2.37 us (2%)
    pallas_call x2, Pallas kernels, staged_call(): pl.pallas_call(kernel, out_shape=[out_shape(i) for i, _ in results], in_s...  32.8 us
    all_to_all x1, blocking collectives, to_rings(): return lax.all_to_all(block, RING, 0, 0, tiled=True)  30.5 us
    all_to_all x3, waiting for transfers between devices, to_rings(): return lax.all_to_all(block, RING, 0, 0, tiled=True)  12.4 us
    all_to_all x3, starting transfers between devices, to_rings(): return lax.all_to_all(block, RING, 0, 0, tiled=True)  12.2 us
    ppermute x6, starting transfers between devices, sent(): return lax.ppermute(piece(k), ('x', 'z', 'c'), route)  11.5 us
    ppermute x8, starting transfers between devices, passed(): lax.ppermute(block, axis, [(i, (i + distance) % size) for i in range(size)])  9.08 us
    ppermute x8, waiting for transfers between devices, passed(): lax.ppermute(block, axis, [(i, (i + distance) % size) for i in range(size)])  7.97 us
    ppermute x6, waiting for transfers between devices, sent(): return lax.ppermute(piece(k), ('x', 'z', 'c'), route)  7.2 us
  transfers between devices with their start and end apart: 17, of which 10 were waited for; matrix products, arithmetic and copies ran while one was open for 6% of the time, Pallas kernels for 24%

profile of v4, /device:TPU:0, one launch (start us, length us, event | category | flops | bytes accessed | tf_op | source)
XLA Modules:
  0.0 138.0 jit_solution(11717524336724265374)
XLA Ops:
  0.6 30.5 %all_to_all.20 = bf16[16,64,768]{2,1,0:T(8,128)(2,1)S(1)} all-to-all(bf16[16,64,768]{2,1,0:T(8,128)(2,1)} %bitcast.74), channel_id=1, replica_groups=mesh['x'=4,'z'=4,'yh'=2,'c'=2,'yl'=2] {'x','z'}, dimensions={0} | all-to-all | bytes 3145728 | tf_op jit(solution)/shard_map/all_to_all | solution.py:340
  31.2 3.8 %all-to-all-start = ((bf16[16,64,768]{2,1,0:T(8,128)(2,1)}), bf16[16,64,768]{2,1,0:T(8,128)(2,1)S(1)}, u32[]{:S(2)}, u32[]{:S(2)}) async-start(bf16[16,64,768]{2,1,0:T(8,128)(2,1)} %bitcast.75), calls=%async_computation | async-start | bytes 3145728 | tf_op jit(solution)/shard_map/all_to_all | solution.py:340
  35.0 15.5 %forward.1 = (bf16[1024,768]{1,0:T(8,128)(2,1)}, bf16[1024,768]{1,0:T(8,128)(2,1)}, bf16[1024,768]{1,0:T(8,128)(2,1)}, bf16[1024,384]{1,0:T(8,128)(2,1)}, bf16[1...) custom-call(bf16[1024,768]{1,0:T(8,128)(2,1)S(1)} %bitcast.71, ...), custom_call_target="tpu_custom_call" | custom-call | flops 1 | bytes 1 | tf_op jit(solution)/shard_map/forward/pallas_call | solution.py:141
  50.5 7.0 %all-to-all-done = bf16[16,64,768]{2,1,0:T(8,128)(2,1)S(1)} async-done(((bf16[16,64,768]{2,1,0:T(8,128)(2,1)}), bf16[16,64,768]{2,1,0:T(8,128)(2,1)S(1)}, u32[]{:S(2)}, u32[]{:S(2)}) %all-to-all-start) | async-done | bytes 1572896 | tf_op jit(solution)/shard_map/all_to_all | solution.py:340
  57.5 3.9 %all-to-all-start.2 = ((bf16[16,64,768]{2,1,0:T(8,128)(2,1)}), bf16[16,64,768]{2,1,0:T(8,128)(2,1)S(1)}, u32[]{:S(2)}, u32[]{:S(2)}) async-start(bf16[16,64,768]{2,1,0:T(8,128)(2,1)} %bitcast.77), calls=%async_computation.2 | async-start | bytes 3145728 | tf_op jit(solution)/shard_map/all_to_all | solution.py:340
  61.4 0.1 pad_add_fusion.refs_0_
  61.5 17.3 %backward.1 = (bf16[1024,768]{1,0:T(8,128)(2,1)}, bf16[4,96,1536]{2,1,0:T(8,128)(2,1)}, bf16[4,96,1536]{2,1,0:T(8,128)(2,1)}, bf16[4,96,1536]{2,1,0:T(8,128)(2,1)}, bf16[4,96,1536]{2,1,0:T(8,128)(2,1)}) custom-call(s32[2]{0:T(128)S(1)} %pad_add_fusion.refs_0_, bf16[1024,768]{1,0:T(8,128)(2,1)S(1)} %bitcast.70, bf16[2,384,768]{2,1,0:T(8,128)(2,1)} %refs_8_.1, ...), custom_call_target="tpu_custom_call" | custom-call | flops 1 | bytes 1 | tf_op jit(solution)/shard_map/backward/pallas_call | solution.py:141
  78.8 0.1 collective-permute-start
  78.9 0.5 collective-permute-start.1
  79.4 2.6 %all-to-all-done.2 = bf16[16,64,768]{2,1,0:T(8,128)(2,1)S(1)} async-done(((bf16[16,64,768]{2,1,0:T(8,128)(2,1)}), bf16[16,64,768]{2,1,0:T(8,128)(2,1)S(1)}, u32[]{:S(2)}, u32[]{:S(2)}) %all-to-all-start.2) | async-done | bytes 1572896 | tf_op jit(solution)/shard_map/all_to_all | solution.py:340
  81.9 4.4 %all-to-all-start.3 = ((bf16[16,64,768]{2,1,0:T(8,128)(2,1)}), bf16[16,64,768]{2,1,0:T(8,128)(2,1)S(1)}, u32[]{:S(2)}, u32[]{:S(2)}) async-start(bf16[16,64,768]{2,1,0:T(8,128)(2,1)} %bitcast.76), calls=%async_computation.3 | async-start | bytes 3145728 | tf_op jit(solution)/shard_map/all_to_all | solution.py:340
  86.4 0.0 collective-permute-done
  86.4 0.0 collective-permute-done.1
  86.4 2.7 %fusion.7 = (bf16[96,1536]{1,0:T(8,128)(2,1)}, bf16[96,1536]{1,0:T(8,128)(2,1)S(1)}, bf16[96,1536]{1,0:T(8,128)(2,1)}, bf16[96,1536]{1,0:T(8,128)(2,1)}) fusion(bf16[4,96,1536]{2,1,0:T(8,128)(2,1)} %collective-permute-done, bf16[4,96,1536]{2,1,0:T(8,128)(2,1)} %get-tuple-element.40), kind=kLoop, calls=%fused_computation.21 | loop fusion | flops 2359296 | bytes 3538944 | tf_op jit(solution)/shard_map/convert_element_type | solution.py:356
  89.1 1.6 %collective-permute-start.3 = (bf16[96,1536]{1,0:T(8,128)(2,1)}, bf16[96,1536]{1,0:T(8,128)(2,1)}, u32[]{:S(2)}, u32[]{:S(2)}) collective-permute-start(bf16[96,1536]{1,0:T(8,128)(2,1)} %get-tuple-element.59), channel_id=1, source_target_pairs={{0,1},{1,4},{4,5},{5,0},{2,3},{3,6},{6,7},{7,2},{8,9},{9,12},{12,1... | collective-permute-start | bytes 884744 | tf_op jit(solution)/shard_map/ppermute | solution.py:345
  90.6 1.7 %collective-permute-start.5 = (bf16[96,1536]{1,0:T(8,128)(2,1)}, bf16[96,1536]{1,0:T(8,128)(2,1)}, u32[]{:S(2)}, u32[]{:S(2)}) collective-permute-start(bf16[96,1536]{1,0:T(8,128)(2,1)} %get-tuple-element.58), channel_id=1, source_target_pairs={{0,5},{1,0},{4,1},{5,4},{2,7},{3,2},{6,3},{7,6},{8,13},{9,8},{12,9... | collective-permute-start | bytes 884744 | tf_op jit(solution)/shard_map/ppermute | solution.py:345
  92.3 1.8 %collective-permute-start.2 = (bf16[96,1536]{1,0:T(8,128)(2,1)}, bf16[96,1536]{1,0:T(8,128)(2,1)}, u32[]{:S(2)}, u32[]{:S(2)}) collective-permute-start(bf16[96,1536]{1,0:T(8,128)(2,1)} %get-tuple-element.56), channel_id=1, source_target_pairs={{0,5},{1,0},{4,1},{5,4},{2,7},{3,2},{6,3},{7,6},{8,13},{9,8},{12,9... | collective-permute-start | bytes 884744 | tf_op jit(solution)/shard_map/ppermute | solution.py:345
  94.1 0.2 collective-permute-start.7
  94.3 6.2 %collective-permute-done.3 = bf16[96,1536]{1,0:T(8,128)(2,1)} collective-permute-done((bf16[96,1536]{1,0:T(8,128)(2,1)}, bf16[96,1536]{1,0:T(8,128)(2,1)}, u32[]{:S(2)}, u32[]{:S(2)}) %collective-permute-start.3) | collective-permute-done | bytes 294944 | tf_op jit(solution)/shard_map/ppermute | solution.py:345
  100.5 0.4 collective-permute-done.5
  100.9 2.4 %fusion.2 = (bf16[96,1536]{1,0:T(8,128)(2,1)}, bf16[96,1536]{1,0:T(8,128)(2,1)}) fusion(bf16[96,1536]{1,0:T(8,128)(2,1)} %collective-permute-done.5, bf16[4,96,1536]{2,1,0:T(8,128)(2,1)} %collective-permute-done.1, bf16[4,96,1536]{2,1,0:T(8,128)(2,1)} %get-tuple-element.35, bf16[96,1536]{1,0:T(8,128)(2,1)} %collective-permute-done.3), kind=kLoop, calls=%fused_computation.6 | loop fusion | flops 2359296 | bytes 2359296 | tf_op jit(solution)/shard_map/convert_element_type | solution.py:365
  103.3 1.6 %collective-permute-start.4 = (bf16[96,1536]{1,0:T(8,128)(2,1)}, bf16[96,1536]{1,0:T(8,128)(2,1)}, u32[]{:S(2)}, u32[]{:S(2)}) collective-permute-start(bf16[96,1536]{1,0:T(8,128)(2,1)} %get-tuple-element.61), channel_id=1, source_target_pairs={{0,1},{1,4},{4,5},{5,0},{2,3},{3,6},{6,7},{7,2},{8,9},{9,12},{12,1... | collective-permute-start | bytes 884744 | tf_op jit(solution)/shard_map/ppermute | solution.py:345
  104.9 1.6 %collective-permute-start.6 = (bf16[96,1536]{1,0:T(8,128)(2,1)}, bf16[96,1536]{1,0:T(8,128)(2,1)}, u32[]{:S(2)}, u32[]{:S(2)}) collective-permute-start(bf16[96,1536]{1,0:T(8,128)(2,1)} %get-tuple-element.60), channel_id=1, source_target_pairs={{0,5},{1,0},{4,1},{5,4},{2,7},{3,2},{6,3},{7,6},{8,13},{9,8},{12,9... | collective-permute-start | bytes 884744 | tf_op jit(solution)/shard_map/ppermute | solution.py:345
  106.6 1.2 broadcast_multiply_fusion.1
  107.8 2.8 %all-to-all-done.3 = bf16[16,64,768]{2,1,0:T(8,128)(2,1)S(1)} async-done(((bf16[16,64,768]{2,1,0:T(8,128)(2,1)}), bf16[16,64,768]{2,1,0:T(8,128)(2,1)S(1)}, u32[]{:S(2)}, u32[]{:S(2)}) %all-to-all-start.3) | async-done | bytes 1572896 | tf_op jit(solution)/shard_map/all_to_all | solution.py:340
  110.6 1.4 %collective-permute-done.4 = bf16[96,1536]{1,0:T(8,128)(2,1)} collective-permute-done((bf16[96,1536]{1,0:T(8,128)(2,1)}, bf16[96,1536]{1,0:T(8,128)(2,1)}, u32[]{:S(2)}, u32[]{:S(2)}) %collective-permute-start.4) | collective-permute-done | bytes 294944 | tf_op jit(solution)/shard_map/ppermute | solution.py:345
  112.0 0.0 collective-permute-done.6
  112.0 0.0 collective-permute-done.2
  112.0 0.0 collective-permute-done.7
  112.0 1.9 %fusion.5 = (bf16[96,1536]{1,0:T(8,128)(2,1)S(1)}, bf16[96,1536]{1,0:T(8,128)(2,1)S(1)}) fusion(bf16[96,1536]{1,0:T(8,128)(2,1)} %collective-permute-done.4, bf16[96,1536]{1,0:T(8,128)(2,1)} %collective-permute-done.2, bf16[4,96,1536]{2,1,0:T(8,128)(2,1)} %collective-permute-done.1, bf16[4,96,1536]{2,1,0:T(8,128)(2,1)} %get-tuple-element.35, ...), kind=kLoop, calls=%fused_computation.11 | loop fusion | flops 2949120 | bytes 2949120 | tf_op jit(solution)/shard_map/convert.9
  113.9 0.5 copy.10
  114.4 0.5 copy.9
  114.9 1.0 maximum_bitcast_fusion.1
  115.9 3.1 %collective-permute-start.10 = (bf16[2,24,1536]{2,0,1:T(2,128)(2,1)S(1)}, bf16[2,24,1536]{2,0,1:T(2,128)(2,1)S(1)}, u32[]{:S(2)}, u32[]{:S(2)}) collective-permute-start(bf16[2,24,1536]{2,0,1:T(2,128)(2,1)S(1)} %get-tuple-element.64), channel_id=1, source_target_pairs={{0,96},{2,26},{8,104},{10,2},{16,112},{18,10},{24,120},{26,18},{32... | collective-permute-start | bytes 442376 | tf_op jit(solution)/shard_map/ppermute | solution.py:385
  119.0 0.9 collective-permute-start.8
  119.9 0.9 collective-permute-start.9
  120.7 1.2 broadcast_multiply_fusion
  122.0 1.3 collective-permute-done.10
  123.3 2.5 %collective-permute-done.8 = bf16[2,24,1536]{2,0,1:T(2,128)(2,1)S(1)} collective-permute-done((bf16[2,24,1536]{2,0,1:T(2,128)(2,1)S(1)}, bf16[2,24,1536]{2,0,1:T(2,128)(2,1)S(1)}, u32[]{:S(2)}, u32[]{:S(2)}) %collective-permute-start.8) | collective-permute-done | bytes 147488 | tf_op jit(solution)/shard_map/ppermute | solution.py:385
  125.8 1.5 %collective-permute-done.9 = bf16[2,24,1536]{2,0,1:T(2,128)(2,1)S(1)} collective-permute-done((bf16[2,24,1536]{2,0,1:T(2,128)(2,1)S(1)}, bf16[2,24,1536]{2,0,1:T(2,128)(2,1)S(1)}, u32[]{:S(2)}, u32[]{:S(2)}) %collective-permute-start.9) | collective-permute-done | bytes 147488 | tf_op jit(solution)/shard_map/ppermute | solution.py:385
  127.2 0.6 fusion.16
  127.8 0.1 dynamic-slice_bitcast_fusion.2
  127.9 3.4 %collective-permute-start.11 = (bf16[2,6,1536]{2,0,1:T(2,128)(2,1)S(1)}, bf16[2,6,1536]{2,0,1:T(2,128)(2,1)S(1)}, u32[]{:S(2)}, u32[]{:S(2)}) collective-permute-start(bf16[2,6,1536]{2,0,1:T(2,128)(2,1)S(1)} %get-tuple-element.65), channel_id=1, source_target_pairs={{0,16},{2,66},{8,24},{10,74},{16,0},{18,82},{24,8},{26,90},{32,48}... | collective-permute-start | bytes 110600 | tf_op jit(solution)/shard_map/ppermute | solution.py:385
  131.3 0.6 collective-permute-start.12
  131.9 2.7 %collective-permute-start.13 = (bf16[2,6,1536]{2,0,1:T(2,128)(2,1)S(1)}, bf16[2,6,1536]{2,0,1:T(2,128)(2,1)S(1)}, u32[]{:S(2)}, u32[]{:S(2)}) collective-permute-start(bf16[2,6,1536]{2,0,1:T(2,128)(2,1)S(1)} %get-tuple-element.66), channel_id=1, source_target_pairs={{0,24},{2,98},{8,0},{10,106},{16,8},{18,114},{24,16},{26,122},{32,... | collective-permute-start | bytes 110600 | tf_op jit(solution)/shard_map/ppermute | solution.py:385
  134.6 0.0 collective-permute-done.11
  134.6 1.9 %collective-permute-done.12 = bf16[2,6,1536]{2,0,1:T(2,128)(2,1)S(1)} collective-permute-done((bf16[2,6,1536]{2,0,1:T(2,128)(2,1)S(1)}, bf16[2,6,1536]{2,0,1:T(2,128)(2,1)S(1)}, u32[]{:S(2)}, u32[]{:S(2)}) %collective-permute-start.12) | collective-permute-done | bytes 36896 | tf_op jit(solution)/shard_map/ppermute | solution.py:385
  136.5 0.0 collective-permute-done.13
  136.5 0.1 fusion.20
  136.6 0.1 reshape.98
  136.7 0.7 copy.11
  137.4 0.6 copy.14
  (2 shorter events, 0.0 us)
Async XLA Ops:
  31.2 26.4 %all-to-all-start = ((bf16[16,64,768]{2,1,0:T(8,128)(2,1)}), bf16[16,64,768]{2,1,0:T(8,128)(2,1)S(1)}, u32[]{:S(2)}, u32[]{:S(2)}) async-start(bf16[16,64,768]{2,1,0:T(8,128)(2,1)} %bitcast.75), calls=%async_computation | async-start | bytes 3145728 | tf_op jit(solution)/shard_map/all_to_all | solution.py:340
  57.5 24.4 %all-to-all-start.2 = ((bf16[16,64,768]{2,1,0:T(8,128)(2,1)}), bf16[16,64,768]{2,1,0:T(8,128)(2,1)S(1)}, u32[]{:S(2)}, u32[]{:S(2)}) async-start(bf16[16,64,768]{2,1,0:T(8,128)(2,1)} %bitcast.77), calls=%async_computation.2 | async-start | bytes 3145728 | tf_op jit(solution)/shard_map/all_to_all | solution.py:340
  78.8 7.6 %collective-permute-start = (bf16[4,96,1536]{2,1,0:T(8,128)(2,1)}, bf16[4,96,1536]{2,1,0:T(8,128)(2,1)}, u32[]{:S(2)}, u32[]{:S(2)}) collective-permute-start(bf16[4,96,1536]{2,1,0:T(8,128)(2,1)} %get-tuple-element.36), channel_id=1, source_target_pairs={{0,2},{2,0},{1,3},{3,1},{4,6},{6,4},{5,7},{7,5},{8,10},{10,8},{9,1... | collective-permute-start | bytes 3538952 | tf_op jit(solution)/shard_map/ppermute | solution.py:345
  78.9 7.5 %collective-permute-start.1 = (bf16[4,96,1536]{2,1,0:T(8,128)(2,1)}, bf16[4,96,1536]{2,1,0:T(8,128)(2,1)}, u32[]{:S(2)}, u32[]{:S(2)}) collective-permute-start(bf16[4,96,1536]{2,1,0:T(8,128)(2,1)} %get-tuple-element.37), channel_id=1, source_target_pairs={{0,2},{2,0},{1,3},{3,1},{4,6},{6,4},{5,7},{7,5},{8,10},{10,8},{9,1... | collective-permute-start | bytes 3538952 | tf_op jit(solution)/shard_map/ppermute | solution.py:345
  81.9 28.7 %all-to-all-start.3 = ((bf16[16,64,768]{2,1,0:T(8,128)(2,1)}), bf16[16,64,768]{2,1,0:T(8,128)(2,1)S(1)}, u32[]{:S(2)}, u32[]{:S(2)}) async-start(bf16[16,64,768]{2,1,0:T(8,128)(2,1)} %bitcast.76), calls=%async_computation.3 | async-start | bytes 3145728 | tf_op jit(solution)/shard_map/all_to_all | solution.py:340
  89.1 11.4 %collective-permute-start.3 = (bf16[96,1536]{1,0:T(8,128)(2,1)}, bf16[96,1536]{1,0:T(8,128)(2,1)}, u32[]{:S(2)}, u32[]{:S(2)}) collective-permute-start(bf16[96,1536]{1,0:T(8,128)(2,1)} %get-tuple-element.59), channel_id=1, source_target_pairs={{0,1},{1,4},{4,5},{5,0},{2,3},{3,6},{6,7},{7,2},{8,9},{9,12},{12,1... | collective-permute-start | bytes 884744 | tf_op jit(solution)/shard_map/ppermute | solution.py:345
  90.6 10.3 %collective-permute-start.5 = (bf16[96,1536]{1,0:T(8,128)(2,1)}, bf16[96,1536]{1,0:T(8,128)(2,1)}, u32[]{:S(2)}, u32[]{:S(2)}) collective-permute-start(bf16[96,1536]{1,0:T(8,128)(2,1)} %get-tuple-element.58), channel_id=1, source_target_pairs={{0,5},{1,0},{4,1},{5,4},{2,7},{3,2},{6,3},{7,6},{8,13},{9,8},{12,9... | collective-permute-start | bytes 884744 | tf_op jit(solution)/shard_map/ppermute | solution.py:345
  92.3 19.7 %collective-permute-start.2 = (bf16[96,1536]{1,0:T(8,128)(2,1)}, bf16[96,1536]{1,0:T(8,128)(2,1)}, u32[]{:S(2)}, u32[]{:S(2)}) collective-permute-start(bf16[96,1536]{1,0:T(8,128)(2,1)} %get-tuple-element.56), channel_id=1, source_target_pairs={{0,5},{1,0},{4,1},{5,4},{2,7},{3,2},{6,3},{7,6},{8,13},{9,8},{12,9... | collective-permute-start | bytes 884744 | tf_op jit(solution)/shard_map/ppermute | solution.py:345
  94.1 17.9 %collective-permute-start.7 = (bf16[96,1536]{1,0:T(8,128)(2,1)S(1)}, bf16[96,1536]{1,0:T(8,128)(2,1)}, u32[]{:S(2)}, u32[]{:S(2)}) collective-permute-start(bf16[96,1536]{1,0:T(8,128)(2,1)S(1)} %get-tuple-element.57), channel_id=1, source_target_pairs={{0,1},{1,4},{4,5},{5,0},{2,3},{3,6},{6,7},{7,2},{8,9},{9,12},{12,1... | collective-permute-start | bytes 884744 | tf_op jit(solution)/shard_map/ppermute | solution.py:345
  103.3 8.7 %collective-permute-start.4 = (bf16[96,1536]{1,0:T(8,128)(2,1)}, bf16[96,1536]{1,0:T(8,128)(2,1)}, u32[]{:S(2)}, u32[]{:S(2)}) collective-permute-start(bf16[96,1536]{1,0:T(8,128)(2,1)} %get-tuple-element.61), channel_id=1, source_target_pairs={{0,1},{1,4},{4,5},{5,0},{2,3},{3,6},{6,7},{7,2},{8,9},{9,12},{12,1... | collective-permute-start | bytes 884744 | tf_op jit(solution)/shard_map/ppermute | solution.py:345
  104.9 7.1 %collective-permute-start.6 = (bf16[96,1536]{1,0:T(8,128)(2,1)}, bf16[96,1536]{1,0:T(8,128)(2,1)}, u32[]{:S(2)}, u32[]{:S(2)}) collective-permute-start(bf16[96,1536]{1,0:T(8,128)(2,1)} %get-tuple-element.60), channel_id=1, source_target_pairs={{0,5},{1,0},{4,1},{5,4},{2,7},{3,2},{6,3},{7,6},{8,13},{9,8},{12,9... | collective-permute-start | bytes 884744 | tf_op jit(solution)/shard_map/ppermute | solution.py:345
  115.9 7.4 %collective-permute-start.10 = (bf16[2,24,1536]{2,0,1:T(2,128)(2,1)S(1)}, bf16[2,24,1536]{2,0,1:T(2,128)(2,1)S(1)}, u32[]{:S(2)}, u32[]{:S(2)}) collective-permute-start(bf16[2,24,1536]{2,0,1:T(2,128)(2,1)S(1)} %get-tuple-element.64), channel_id=1, source_target_pairs={{0,96},{2,26},{8,104},{10,2},{16,112},{18,10},{24,120},{26,18},{32... | collective-permute-start | bytes 442376 | tf_op jit(solution)/shard_map/ppermute | solution.py:385
  119.0 6.8 %collective-permute-start.8 = (bf16[2,24,1536]{2,0,1:T(2,128)(2,1)S(1)}, bf16[2,24,1536]{2,0,1:T(2,128)(2,1)S(1)}, u32[]{:S(2)}, u32[]{:S(2)}) collective-permute-start(bf16[2,24,1536]{2,0,1:T(2,128)(2,1)S(1)} %get-tuple-element.62), channel_id=1, source_target_pairs={{0,64},{2,18},{8,72},{10,26},{16,80},{18,2},{24,88},{26,10},{32,96... | collective-permute-start | bytes 442376 | tf_op jit(solution)/shard_map/ppermute | solution.py:385
  119.9 7.4 %collective-permute-start.9 = (bf16[2,24,1536]{2,0,1:T(2,128)(2,1)S(1)}, bf16[2,24,1536]{2,0,1:T(2,128)(2,1)S(1)}, u32[]{:S(2)}, u32[]{:S(2)}) collective-permute-start(bf16[2,24,1536]{2,0,1:T(2,128)(2,1)S(1)} %get-tuple-element.63), channel_id=1, source_target_pairs={{0,32},{2,10},{8,40},{10,18},{16,48},{18,26},{24,56},{26,2},{32,64... | collective-permute-start | bytes 442376 | tf_op jit(solution)/shard_map/ppermute | solution.py:385
  127.9 6.7 %collective-permute-start.11 = (bf16[2,6,1536]{2,0,1:T(2,128)(2,1)S(1)}, bf16[2,6,1536]{2,0,1:T(2,128)(2,1)S(1)}, u32[]{:S(2)}, u32[]{:S(2)}) collective-permute-start(bf16[2,6,1536]{2,0,1:T(2,128)(2,1)S(1)} %get-tuple-element.65), channel_id=1, source_target_pairs={{0,16},{2,66},{8,24},{10,74},{16,0},{18,82},{24,8},{26,90},{32,48}... | collective-permute-start | bytes 110600 | tf_op jit(solution)/shard_map/ppermute | solution.py:385
  131.3 5.2 %collective-permute-start.12 = (bf16[2,6,1536]{2,0,1:T(2,128)(2,1)S(1)}, bf16[2,6,1536]{2,0,1:T(2,128)(2,1)S(1)}, u32[]{:S(2)}, u32[]{:S(2)}) collective-permute-start(bf16[2,6,1536]{2,0,1:T(2,128)(2,1)S(1)} %get-tuple-element.67), channel_id=1, source_target_pairs={{0,8},{2,34},{8,16},{10,42},{16,24},{18,50},{24,0},{26,58},{32,40}... | collective-permute-start | bytes 110600 | tf_op jit(solution)/shard_map/ppermute | solution.py:385
  131.9 4.6 %collective-permute-start.13 = (bf16[2,6,1536]{2,0,1:T(2,128)(2,1)S(1)}, bf16[2,6,1536]{2,0,1:T(2,128)(2,1)S(1)}, u32[]{:S(2)}, u32[]{:S(2)}) collective-permute-start(bf16[2,6,1536]{2,0,1:T(2,128)(2,1)S(1)} %get-tuple-element.66), channel_id=1, source_target_pairs={{0,24},{2,98},{8,0},{10,106},{16,8},{18,114},{24,16},{26,122},{32,... | collective-permute-start | bytes 110600 | tf_op jit(solution)/shard_map/ppermute | solution.py:385

commit v5 on v4

--- a/solution.py
+++ b/solution.py
@@ -352,20 +352,19 @@
     return out
 
 
-def core_sum(mine, came):
-    return [total_of([mine[i], came[i]]).astype(BF) for i in range(4)]
+def core_sum(mine, came, *at):
+    return [total_of([mine[i], came[i]]).astype(BF) for i in at]
 
 
 def column_sum(first, second, beside):
     two0, two1, right1, left0 = first
-    own0, own1, right0, left1 = second
+    own, right0, left1 = second
     two0, two1 = passed(two0, COLUMN, 1), passed(two1, COLUMN, -1)
     right1, left0 = passed(right1, COLUMN, 1), passed(left0, COLUMN, -1)
     right0 = passed(total_of([right0, two0]).astype(BF), COLUMN, 1)
     left1 = passed(total_of([left1, two1]).astype(BF), COLUMN, -1)
     right0, left1, beside = lax.optimization_barrier((right0, left1, beside))
-    sums = total_of([own0, left0, right0]), total_of([own1, right1, left1])
-    return jnp.stack(sums).astype(BF), beside
+    return total_of([own, jnp.stack([left0, right1]), jnp.stack([right0, left1])]).astype(BF), beside
 
 
 def ring_step(rows, second):
@@ -409,7 +408,8 @@
     input_grad = unring(grad)
     came = [passed(part, "c", 1) for part in parts[2:]]
     *came, outputs = lax.optimization_barrier((*came, outputs))
-    first, second = core_sum(parts[0], came[0]), core_sum(parts[1], came[1])
+    first = core_sum(parts[0], came[0], 0, 1, 2, 3)
+    second = core_sum(parts[1], came[1], slice(2), 2, 3)
     share, input_grad = column_sum(first, second, input_grad)
     share = ring_step(share, 0).astype(BF)
     outputs, input_grad = settled(outputs), settled(input_grad)

time: 139 us -> 137 us (0.986)
  waiting for transfers between devices: 27.6 us -> 26.2 us
    convert_element_type x1 -> x2, other arithmetic: 2.68 us -> 4.58 us  [the longest x1 2.69 us: core_sum(): return [total_of([mine[i], came[i]]).astype(BF) for i in at]]
    another operation x1 -> x0, other arithmetic: 1.88 us -> none
  transfers between devices with their start and end apart: 17 -> 17, of which waited for: 10 -> 9; matrix products, arithmetic and copies ran while one was open for 6% -> 6% of each run, Pallas kernels for 24% -> 24%
where the time goes in v5:
time: 137 us; the launch traced here: 136 us
  starting transfers between devices  34.1 us (25%)
  Pallas kernels  32.7 us (24%)
  blocking collectives  30.5 us (22%)
  waiting for transfers between devices  26.2 us (19%)
  other arithmetic  9.94 us (7%)
  local copies, waits for them, and re-layouts  1.87 us (1%)
    pallas_call x2, Pallas kernels, staged_call(): pl.pallas_call(kernel, out_shape=[out_shape(i) for i, _ in results], in_s...  32.7 us
    all_to_all x1, blocking collectives, to_rings(): return lax.all_to_all(block, RING, 0, 0, tiled=True)  30.5 us
    all_to_all x3, waiting for transfers between devices, to_rings(): return lax.all_to_all(block, RING, 0, 0, tiled=True)  12.4 us
    all_to_all x3, starting transfers between devices, to_rings(): return lax.all_to_all(block, RING, 0, 0, tiled=True)  12.2 us
    ppermute x6, starting transfers between devices, sent(): return lax.ppermute(piece(k), ('x', 'z', 'c'), route)  11.7 us
    ppermute x8, starting transfers between devices, passed(): lax.ppermute(block, axis, [(i, (i + distance) % size) for i in range(size)])  10.3 us
    ppermute x6, waiting for transfers between devices, sent(): return lax.ppermute(piece(k), ('x', 'z', 'c'), route)  7.01 us
    ppermute x8, waiting for transfers between devices, passed(): lax.ppermute(block, axis, [(i, (i + distance) % size) for i in range(size)])  6.76 us
  transfers between devices with their start and end apart: 17, of which 9 were waited for; matrix products, arithmetic and copies ran while one was open for 6% of the time, Pallas kernels for 24%

profile of v5, /device:TPU:0, one launch (start us, length us, event | category | flops | bytes accessed | tf_op | source)
XLA Modules:
  0.0 136.2 jit_solution(5994062235150207581)
XLA Ops:
  0.6 30.5 %all_to_all.20 = bf16[16,64,768]{2,1,0:T(8,128)(2,1)S(1)} all-to-all(bf16[16,64,768]{2,1,0:T(8,128)(2,1)} %bitcast.71), channel_id=1, replica_groups=mesh['x'=4,'z'=4,'yh'=2,'c'=2,'yl'=2] {'x','z'}, dimensions={0} | all-to-all | bytes 3145728 | tf_op jit(solution)/shard_map/all_to_all | solution.py:340
  31.2 3.8 %all-to-all-start = ((bf16[16,64,768]{2,1,0:T(8,128)(2,1)}), bf16[16,64,768]{2,1,0:T(8,128)(2,1)S(1)}, u32[]{:S(2)}, u32[]{:S(2)}) async-start(bf16[16,64,768]{2,1,0:T(8,128)(2,1)} %bitcast.72), calls=%async_computation | async-start | bytes 3145728 | tf_op jit(solution)/shard_map/all_to_all | solution.py:340
  35.0 15.5 %forward.1 = (bf16[1024,768]{1,0:T(8,128)(2,1)}, bf16[1024,768]{1,0:T(8,128)(2,1)}, bf16[1024,768]{1,0:T(8,128)(2,1)}, bf16[1024,384]{1,0:T(8,128)(2,1)}, bf16[1...) custom-call(bf16[1024,768]{1,0:T(8,128)(2,1)S(1)} %bitcast.67, ...), custom_call_target="tpu_custom_call" | custom-call | flops 1 | bytes 1 | tf_op jit(solution)/shard_map/forward/pallas_call | solution.py:141
  50.5 7.0 %all-to-all-done = bf16[16,64,768]{2,1,0:T(8,128)(2,1)S(1)} async-done(((bf16[16,64,768]{2,1,0:T(8,128)(2,1)}), bf16[16,64,768]{2,1,0:T(8,128)(2,1)S(1)}, u32[]{:S(2)}, u32[]{:S(2)}) %all-to-all-start) | async-done | bytes 1572896 | tf_op jit(solution)/shard_map/all_to_all | solution.py:340
  57.5 3.9 %all-to-all-start.2 = ((bf16[16,64,768]{2,1,0:T(8,128)(2,1)}), bf16[16,64,768]{2,1,0:T(8,128)(2,1)S(1)}, u32[]{:S(2)}, u32[]{:S(2)}) async-start(bf16[16,64,768]{2,1,0:T(8,128)(2,1)} %bitcast.74), calls=%async_computation.2 | async-start | bytes 3145728 | tf_op jit(solution)/shard_map/all_to_all | solution.py:340
  61.4 0.1 pad_add_fusion.refs_0_
  61.5 17.3 %backward.1 = (bf16[1024,768]{1,0:T(8,128)(2,1)}, bf16[4,96,1536]{2,1,0:T(8,128)(2,1)}, bf16[4,96,1536]{2,1,0:T(8,128)(2,1)}, bf16[4,96,1536]{2,1,0:T(8,128)(2,1)}, bf16[4,96,1536]{2,1,0:T(8,128)(2,1)}) custom-call(s32[2]{0:T(128)S(1)} %pad_add_fusion.refs_0_, bf16[1024,768]{1,0:T(8,128)(2,1)S(1)} %bitcast.66, bf16[2,384,768]{2,1,0:T(8,128)(2,1)} %refs_8_.1, ...), custom_call_target="tpu_custom_call" | custom-call | flops 1 | bytes 1 | tf_op jit(solution)/shard_map/backward/pallas_call | solution.py:141
  78.8 0.1 collective-permute-start
  78.9 0.5 collective-permute-start.1
  79.4 2.6 %all-to-all-done.2 = bf16[16,64,768]{2,1,0:T(8,128)(2,1)S(1)} async-done(((bf16[16,64,768]{2,1,0:T(8,128)(2,1)}), bf16[16,64,768]{2,1,0:T(8,128)(2,1)S(1)}, u32[]{:S(2)}, u32[]{:S(2)}) %all-to-all-start.2) | async-done | bytes 1572896 | tf_op jit(solution)/shard_map/all_to_all | solution.py:340
  81.9 4.4 %all-to-all-start.3 = ((bf16[16,64,768]{2,1,0:T(8,128)(2,1)}), bf16[16,64,768]{2,1,0:T(8,128)(2,1)S(1)}, u32[]{:S(2)}, u32[]{:S(2)}) async-start(bf16[16,64,768]{2,1,0:T(8,128)(2,1)} %bitcast.73), calls=%async_computation.3 | async-start | bytes 3145728 | tf_op jit(solution)/shard_map/all_to_all | solution.py:340
  86.4 0.0 collective-permute-done
  86.4 0.0 collective-permute-done.1
  86.4 2.7 %fusion.7 = (bf16[96,1536]{1,0:T(8,128)(2,1)}, bf16[96,1536]{1,0:T(8,128)(2,1)}, bf16[96,1536]{1,0:T(8,128)(2,1)}, bf16[96,1536]{1,0:T(8,128)(2,1)S(1)}) fusion(bf16[4,96,1536]{2,1,0:T(8,128)(2,1)} %collective-permute-done, bf16[4,96,1536]{2,1,0:T(8,128)(2,1)} %get-tuple-element.40), kind=kLoop, calls=%fused_computation.19 | loop fusion | flops 2359296 | bytes 3538944 | tf_op jit(solution)/shard_map/convert_element_type | solution.py:356
  89.1 1.6 %collective-permute-start.4 = (bf16[96,1536]{1,0:T(8,128)(2,1)}, bf16[96,1536]{1,0:T(8,128)(2,1)}, u32[]{:S(2)}, u32[]{:S(2)}) collective-permute-start(bf16[96,1536]{1,0:T(8,128)(2,1)} %get-tuple-element.57), channel_id=1, source_target_pairs={{0,1},{1,4},{4,5},{5,0},{2,3},{3,6},{6,7},{7,2},{8,9},{9,12},{12,1... | collective-permute-start | bytes 884744 | tf_op jit(solution)/shard_map/ppermute | solution.py:345
  90.6 1.7 %collective-permute-start.6 = (bf16[96,1536]{1,0:T(8,128)(2,1)}, bf16[96,1536]{1,0:T(8,128)(2,1)}, u32[]{:S(2)}, u32[]{:S(2)}) collective-permute-start(bf16[96,1536]{1,0:T(8,128)(2,1)} %get-tuple-element.56), channel_id=1, source_target_pairs={{0,5},{1,0},{4,1},{5,4},{2,7},{3,2},{6,3},{7,6},{8,13},{9,8},{12,9... | collective-permute-start | bytes 884744 | tf_op jit(solution)/shard_map/ppermute | solution.py:345
  92.3 0.4 collective-permute-start.3
  92.7 2.9 %collective-permute-start.2 = (bf16[96,1536]{1,0:T(8,128)(2,1)S(1)}, bf16[96,1536]{1,0:T(8,128)(2,1)}, u32[]{:S(2)}, u32[]{:S(2)}) collective-permute-start(bf16[96,1536]{1,0:T(8,128)(2,1)S(1)} %get-tuple-element.59), channel_id=1, source_target_pairs={{0,5},{1,0},{4,1},{5,4},{2,7},{3,2},{6,3},{7,6},{8,13},{9,8},{12,9... | collective-permute-start | bytes 884744 | tf_op jit(solution)/shard_map/ppermute | solution.py:345
  95.5 4.9 %collective-permute-done.4 = bf16[96,1536]{1,0:T(8,128)(2,1)} collective-permute-done((bf16[96,1536]{1,0:T(8,128)(2,1)}, bf16[96,1536]{1,0:T(8,128)(2,1)}, u32[]{:S(2)}, u32[]{:S(2)}) %collective-permute-start.4) | collective-permute-done | bytes 294944 | tf_op jit(solution)/shard_map/ppermute | solution.py:345
  100.5 0.4 collective-permute-done.6
  100.9 2.4 %fusion = (bf16[96,1536]{1,0:T(8,128)(2,1)}, bf16[96,1536]{1,0:T(8,128)(2,1)}) fusion(bf16[96,1536]{1,0:T(8,128)(2,1)} %collective-permute-done.6, bf16[4,96,1536]{2,1,0:T(8,128)(2,1)} %collective-permute-done.1, bf16[4,96,1536]{2,1,0:T(8,128)(2,1)} %get-tuple-element.35, bf16[96,1536]{1,0:T(8,128)(2,1)} %collective-permute-done.4), kind=kLoop, calls=%fused_computation.5 | loop fusion | flops 2359296 | bytes 2359296 | tf_op jit(solution)/shard_map/convert_element_type | solution.py:365
  103.3 1.6 %collective-permute-start.5 = (bf16[96,1536]{1,0:T(8,128)(2,1)}, bf16[96,1536]{1,0:T(8,128)(2,1)}, u32[]{:S(2)}, u32[]{:S(2)}) collective-permute-start(bf16[96,1536]{1,0:T(8,128)(2,1)} %get-tuple-element.55), channel_id=1, source_target_pairs={{0,1},{1,4},{4,5},{5,0},{2,3},{3,6},{6,7},{7,2},{8,9},{9,12},{12,1... | collective-permute-start | bytes 884744 | tf_op jit(solution)/shard_map/ppermute | solution.py:345
  104.9 1.6 %collective-permute-start.7 = (bf16[96,1536]{1,0:T(8,128)(2,1)}, bf16[96,1536]{1,0:T(8,128)(2,1)}, u32[]{:S(2)}, u32[]{:S(2)}) collective-permute-start(bf16[96,1536]{1,0:T(8,128)(2,1)} %get-tuple-element.54), channel_id=1, source_target_pairs={{0,5},{1,0},{4,1},{5,4},{2,7},{3,2},{6,3},{7,6},{8,13},{9,8},{12,9... | collective-permute-start | bytes 884744 | tf_op jit(solution)/shard_map/ppermute | solution.py:345
  106.5 1.2 broadcast_multiply_fusion.1
  107.8 2.8 %all-to-all-done.3 = bf16[16,64,768]{2,1,0:T(8,128)(2,1)S(1)} async-done(((bf16[16,64,768]{2,1,0:T(8,128)(2,1)}), bf16[16,64,768]{2,1,0:T(8,128)(2,1)S(1)}, u32[]{:S(2)}, u32[]{:S(2)}) %all-to-all-start.3) | async-done | bytes 1572896 | tf_op jit(solution)/shard_map/all_to_all | solution.py:340
  110.6 1.4 %collective-permute-done.5 = bf16[96,1536]{1,0:T(8,128)(2,1)} collective-permute-done((bf16[96,1536]{1,0:T(8,128)(2,1)}, bf16[96,1536]{1,0:T(8,128)(2,1)}, u32[]{:S(2)}, u32[]{:S(2)}) %collective-permute-start.5) | collective-permute-done | bytes 294944 | tf_op jit(solution)/shard_map/ppermute | solution.py:345
  112.0 0.0 collective-permute-done.7
  112.0 0.0 collective-permute-done.3
  112.0 0.0 collective-permute-done.2
  112.0 1.9 %add_convert_fusion = bf16[2,96,1536]{2,1,0:T(8,128)(2,1)S(1)} fusion(bf16[1,96,1536]{2,1,0:T(8,128)(2,1)} %bitcast.11, bf16[1,96,1536]{2,1,0:T(8,128)(2,1)} %bitcast.9, bf16[1,96,1536]{2,1,0:T(8,128)(2,1)} %bitcast.19, bf16[1,96,1536]{2,1,0:T(8,128)(2,1)} %bitcast.18, bf16[4,96,1536]{2,1,0:T(8,128)(2,1)} %collective-permute-done.1, ...), kind=kLoop, calls=%fused_computation | loop fusion | flops 3538944 | bytes 2949120 | tf_op jit(solution)/shard_map/convert_element_type | solution.py:367
  113.9 0.1 constant_dynamic-slice_fusion.3
  114.0 0.1 copy.23
  114.1 3.1 %collective-permute-start.10 = (bf16[2,24,1536]{2,0,1:T(2,128)(2,1)S(1)}, bf16[2,24,1536]{2,0,1:T(2,128)(2,1)S(1)}, u32[]{:S(2)}, u32[]{:S(2)}) collective-permute-start(bf16[2,24,1536]{2,0,1:T(2,128)(2,1)S(1)} %bitcast.77), channel_id=1, source_target_pairs={{0,96},{2,26},{8,104},{10,2},{16,112},{18,10},{24,120},{26,18},{32... | collective-permute-start | bytes 442376 | tf_op jit(solution)/shard_map/ppermute | solution.py:384
  117.3 0.1 copy.25
  117.4 0.9 collective-permute-start.8
  118.3 0.1 copy.24
  118.4 0.9 collective-permute-start.9
  119.4 1.2 broadcast_multiply_fusion
  120.6 0.0 collective-permute-done.10
  120.6 3.6 %collective-permute-done.8 = bf16[2,24,1536]{2,0,1:T(2,128)(2,1)S(1)} collective-permute-done((bf16[2,24,1536]{2,0,1:T(2,128)(2,1)S(1)}, bf16[2,24,1536]{2,0,1:T(2,128)(2,1)S(1)}, u32[]{:S(2)}, u32[]{:S(2)}) %collective-permute-start.8) | collective-permute-done | bytes 147488 | tf_op jit(solution)/shard_map/ppermute | solution.py:384
  124.2 1.5 %collective-permute-done.9 = bf16[2,24,1536]{2,0,1:T(2,128)(2,1)S(1)} collective-permute-done((bf16[2,24,1536]{2,0,1:T(2,128)(2,1)S(1)}, bf16[2,24,1536]{2,0,1:T(2,128)(2,1)S(1)}, u32[]{:S(2)}, u32[]{:S(2)}) %collective-permute-start.9) | collective-permute-done | bytes 147488 | tf_op jit(solution)/shard_map/ppermute | solution.py:384
  125.7 0.3 fusion.10
  126.0 0.1 dynamic-slice_bitcast_fusion.2
  126.1 3.4 %collective-permute-start.11 = (bf16[2,6,1536]{2,0,1:T(2,128)(2,1)S(1)}, bf16[2,6,1536]{2,0,1:T(2,128)(2,1)S(1)}, u32[]{:S(2)}, u32[]{:S(2)}) collective-permute-start(bf16[2,6,1536]{2,0,1:T(2,128)(2,1)S(1)} %get-tuple-element.64), channel_id=1, source_target_pairs={{0,16},{2,66},{8,24},{10,74},{16,0},{18,82},{24,8},{26,90},{32,48}... | collective-permute-start | bytes 110600 | tf_op jit(solution)/shard_map/ppermute | solution.py:384
  129.5 0.6 collective-permute-start.12
  130.1 2.7 %collective-permute-start.13 = (bf16[2,6,1536]{2,0,1:T(2,128)(2,1)S(1)}, bf16[2,6,1536]{2,0,1:T(2,128)(2,1)S(1)}, u32[]{:S(2)}, u32[]{:S(2)}) collective-permute-start(bf16[2,6,1536]{2,0,1:T(2,128)(2,1)S(1)} %get-tuple-element.65), channel_id=1, source_target_pairs={{0,24},{2,98},{8,0},{10,106},{16,8},{18,114},{24,16},{26,122},{32,... | collective-permute-start | bytes 110600 | tf_op jit(solution)/shard_map/ppermute | solution.py:384
  132.7 0.0 collective-permute-done.11
  132.7 1.9 %collective-permute-done.12 = bf16[2,6,1536]{2,0,1:T(2,128)(2,1)S(1)} collective-permute-done((bf16[2,6,1536]{2,0,1:T(2,128)(2,1)S(1)}, bf16[2,6,1536]{2,0,1:T(2,128)(2,1)S(1)}, u32[]{:S(2)}, u32[]{:S(2)}) %collective-permute-start.12) | collective-permute-done | bytes 36896 | tf_op jit(solution)/shard_map/ppermute | solution.py:384
  134.7 0.0 collective-permute-done.13
  134.7 0.1 fusion.13
  134.8 0.1 reshape.83
  134.9 0.7 copy.13
  135.5 0.6 copy.26
  (2 shorter events, 0.0 us)
Async XLA Ops:
  31.2 26.4 %all-to-all-start = ((bf16[16,64,768]{2,1,0:T(8,128)(2,1)}), bf16[16,64,768]{2,1,0:T(8,128)(2,1)S(1)}, u32[]{:S(2)}, u32[]{:S(2)}) async-start(bf16[16,64,768]{2,1,0:T(8,128)(2,1)} %bitcast.72), calls=%async_computation | async-start | bytes 3145728 | tf_op jit(solution)/shard_map/all_to_all | solution.py:340
  57.5 24.4 %all-to-all-start.2 = ((bf16[16,64,768]{2,1,0:T(8,128)(2,1)}), bf16[16,64,768]{2,1,0:T(8,128)(2,1)S(1)}, u32[]{:S(2)}, u32[]{:S(2)}) async-start(bf16[16,64,768]{2,1,0:T(8,128)(2,1)} %bitcast.74), calls=%async_computation.2 | async-start | bytes 3145728 | tf_op jit(solution)/shard_map/all_to_all | solution.py:340
  78.8 7.6 %collective-permute-start = (bf16[4,96,1536]{2,1,0:T(8,128)(2,1)}, bf16[4,96,1536]{2,1,0:T(8,128)(2,1)}, u32[]{:S(2)}, u32[]{:S(2)}) collective-permute-start(bf16[4,96,1536]{2,1,0:T(8,128)(2,1)} %get-tuple-element.36), channel_id=1, source_target_pairs={{0,2},{2,0},{1,3},{3,1},{4,6},{6,4},{5,7},{7,5},{8,10},{10,8},{9,1... | collective-permute-start | bytes 3538952 | tf_op jit(solution)/shard_map/ppermute | solution.py:345
  78.9 7.5 %collective-permute-start.1 = (bf16[4,96,1536]{2,1,0:T(8,128)(2,1)}, bf16[4,96,1536]{2,1,0:T(8,128)(2,1)}, u32[]{:S(2)}, u32[]{:S(2)}) collective-permute-start(bf16[4,96,1536]{2,1,0:T(8,128)(2,1)} %get-tuple-element.37), channel_id=1, source_target_pairs={{0,2},{2,0},{1,3},{3,1},{4,6},{6,4},{5,7},{7,5},{8,10},{10,8},{9,1... | collective-permute-start | bytes 3538952 | tf_op jit(solution)/shard_map/ppermute | solution.py:345
  81.9 28.7 %all-to-all-start.3 = ((bf16[16,64,768]{2,1,0:T(8,128)(2,1)}), bf16[16,64,768]{2,1,0:T(8,128)(2,1)S(1)}, u32[]{:S(2)}, u32[]{:S(2)}) async-start(bf16[16,64,768]{2,1,0:T(8,128)(2,1)} %bitcast.73), calls=%async_computation.3 | async-start | bytes 3145728 | tf_op jit(solution)/shard_map/all_to_all | solution.py:340
  89.1 11.4 %collective-permute-start.4 = (bf16[96,1536]{1,0:T(8,128)(2,1)}, bf16[96,1536]{1,0:T(8,128)(2,1)}, u32[]{:S(2)}, u32[]{:S(2)}) collective-permute-start(bf16[96,1536]{1,0:T(8,128)(2,1)} %get-tuple-element.57), channel_id=1, source_target_pairs={{0,1},{1,4},{4,5},{5,0},{2,3},{3,6},{6,7},{7,2},{8,9},{9,12},{12,1... | collective-permute-start | bytes 884744 | tf_op jit(solution)/shard_map/ppermute | solution.py:345
  90.6 10.3 %collective-permute-start.6 = (bf16[96,1536]{1,0:T(8,128)(2,1)}, bf16[96,1536]{1,0:T(8,128)(2,1)}, u32[]{:S(2)}, u32[]{:S(2)}) collective-permute-start(bf16[96,1536]{1,0:T(8,128)(2,1)} %get-tuple-element.56), channel_id=1, source_target_pairs={{0,5},{1,0},{4,1},{5,4},{2,7},{3,2},{6,3},{7,6},{8,13},{9,8},{12,9... | collective-permute-start | bytes 884744 | tf_op jit(solution)/shard_map/ppermute | solution.py:345
  92.3 19.7 %collective-permute-start.3 = (bf16[96,1536]{1,0:T(8,128)(2,1)}, bf16[96,1536]{1,0:T(8,128)(2,1)}, u32[]{:S(2)}, u32[]{:S(2)}) collective-permute-start(bf16[96,1536]{1,0:T(8,128)(2,1)} %get-tuple-element.58), channel_id=1, source_target_pairs={{0,1},{1,4},{4,5},{5,0},{2,3},{3,6},{6,7},{7,2},{8,9},{9,12},{12,1... | collective-permute-start | bytes 884744 | tf_op jit(solution)/shard_map/ppermute | solution.py:345
  92.7 19.4 %collective-permute-start.2 = (bf16[96,1536]{1,0:T(8,128)(2,1)S(1)}, bf16[96,1536]{1,0:T(8,128)(2,1)}, u32[]{:S(2)}, u32[]{:S(2)}) collective-permute-start(bf16[96,1536]{1,0:T(8,128)(2,1)S(1)} %get-tuple-element.59), channel_id=1, source_target_pairs={{0,5},{1,0},{4,1},{5,4},{2,7},{3,2},{6,3},{7,6},{8,13},{9,8},{12,9... | collective-permute-start | bytes 884744 | tf_op jit(solution)/shard_map/ppermute | solution.py:345
  103.3 8.7 %collective-permute-start.5 = (bf16[96,1536]{1,0:T(8,128)(2,1)}, bf16[96,1536]{1,0:T(8,128)(2,1)}, u32[]{:S(2)}, u32[]{:S(2)}) collective-permute-start(bf16[96,1536]{1,0:T(8,128)(2,1)} %get-tuple-element.55), channel_id=1, source_target_pairs={{0,1},{1,4},{4,5},{5,0},{2,3},{3,6},{6,7},{7,2},{8,9},{9,12},{12,1... | collective-permute-start | bytes 884744 | tf_op jit(solution)/shard_map/ppermute | solution.py:345
  104.9 7.1 %collective-permute-start.7 = (bf16[96,1536]{1,0:T(8,128)(2,1)}, bf16[96,1536]{1,0:T(8,128)(2,1)}, u32[]{:S(2)}, u32[]{:S(2)}) collective-permute-start(bf16[96,1536]{1,0:T(8,128)(2,1)} %get-tuple-element.54), channel_id=1, source_target_pairs={{0,5},{1,0},{4,1},{5,4},{2,7},{3,2},{6,3},{7,6},{8,13},{9,8},{12,9... | collective-permute-start | bytes 884744 | tf_op jit(solution)/shard_map/ppermute | solution.py:345
  114.1 6.5 %collective-permute-start.10 = (bf16[2,24,1536]{2,0,1:T(2,128)(2,1)S(1)}, bf16[2,24,1536]{2,0,1:T(2,128)(2,1)S(1)}, u32[]{:S(2)}, u32[]{:S(2)}) collective-permute-start(bf16[2,24,1536]{2,0,1:T(2,128)(2,1)S(1)} %bitcast.77), channel_id=1, source_target_pairs={{0,96},{2,26},{8,104},{10,2},{16,112},{18,10},{24,120},{26,18},{32... | collective-permute-start | bytes 442376 | tf_op jit(solution)/shard_map/ppermute | solution.py:384
  117.4 6.8 %collective-permute-start.8 = (bf16[2,24,1536]{2,0,1:T(2,128)(2,1)S(1)}, bf16[2,24,1536]{2,0,1:T(2,128)(2,1)S(1)}, u32[]{:S(2)}, u32[]{:S(2)}) collective-permute-start(bf16[2,24,1536]{2,0,1:T(2,128)(2,1)S(1)} %bitcast.78), channel_id=1, source_target_pairs={{0,64},{2,18},{8,72},{10,26},{16,80},{18,2},{24,88},{26,10},{32,96... | collective-permute-start | bytes 442376 | tf_op jit(solution)/shard_map/ppermute | solution.py:384
  118.4 7.3 %collective-permute-start.9 = (bf16[2,24,1536]{2,0,1:T(2,128)(2,1)S(1)}, bf16[2,24,1536]{2,0,1:T(2,128)(2,1)S(1)}, u32[]{:S(2)}, u32[]{:S(2)}) collective-permute-start(bf16[2,24,1536]{2,0,1:T(2,128)(2,1)S(1)} %bitcast.79), channel_id=1, source_target_pairs={{0,32},{2,10},{8,40},{10,18},{16,48},{18,26},{24,56},{26,2},{32,64... | collective-permute-start | bytes 442376 | tf_op jit(solution)/shard_map/ppermute | solution.py:384
  126.1 6.7 %collective-permute-start.11 = (bf16[2,6,1536]{2,0,1:T(2,128)(2,1)S(1)}, bf16[2,6,1536]{2,0,1:T(2,128)(2,1)S(1)}, u32[]{:S(2)}, u32[]{:S(2)}) collective-permute-start(bf16[2,6,1536]{2,0,1:T(2,128)(2,1)S(1)} %get-tuple-element.64), channel_id=1, source_target_pairs={{0,16},{2,66},{8,24},{10,74},{16,0},{18,82},{24,8},{26,90},{32,48}... | collective-permute-start | bytes 110600 | tf_op jit(solution)/shard_map/ppermute | solution.py:384
  129.5 5.2 %collective-permute-start.12 = (bf16[2,6,1536]{2,0,1:T(2,128)(2,1)S(1)}, bf16[2,6,1536]{2,0,1:T(2,128)(2,1)S(1)}, u32[]{:S(2)}, u32[]{:S(2)}) collective-permute-start(bf16[2,6,1536]{2,0,1:T(2,128)(2,1)S(1)} %get-tuple-element.66), channel_id=1, source_target_pairs={{0,8},{2,34},{8,16},{10,42},{16,24},{18,50},{24,0},{26,58},{32,40}... | collective-permute-start | bytes 110600 | tf_op jit(solution)/shard_map/ppermute | solution.py:384
  130.1 4.6 %collective-permute-start.13 = (bf16[2,6,1536]{2,0,1:T(2,128)(2,1)S(1)}, bf16[2,6,1536]{2,0,1:T(2,128)(2,1)S(1)}, u32[]{:S(2)}, u32[]{:S(2)}) collective-permute-start(bf16[2,6,1536]{2,0,1:T(2,128)(2,1)S(1)} %get-tuple-element.65), channel_id=1, source_target_pairs={{0,24},{2,98},{8,0},{10,106},{16,8},{18,114},{24,16},{26,122},{32,... | collective-permute-start | bytes 110600 | tf_op jit(solution)/shard_map/ppermute | solution.py:384

commit v6 on v5

--- a/solution.py
+++ b/solution.py
@@ -408,7 +408,9 @@
     input_grad = unring(grad)
     came = [passed(part, "c", 1) for part in parts[2:]]
     *came, outputs = lax.optimization_barrier((*came, outputs))
-    first = core_sum(parts[0], came[0], 0, 1, 2, 3)
+    first = core_sum(parts[0], came[0], 0, 1)
+    *first, rest = lax.optimization_barrier((*first, came[0]))
+    first += core_sum(parts[0], rest, 2, 3)
     second = core_sum(parts[1], came[1], slice(2), 2, 3)
     share, input_grad = column_sum(first, second, input_grad)
     share = ring_step(share, 0).astype(BF)

time: 137 us -> 135 us (0.985)
    ppermute x8, waiting for transfers between devices: 6.76 us -> 4.34 us  [passed(): lax.ppermute(block, axis, [(i, (i + distance) % size) for i in range(size)])]
    all_to_all x3, waiting for transfers between devices: 12.4 us -> 14.2 us  [to_rings(): return lax.all_to_all(block, RING, 0, 0, tiled=True)]
    convert_element_type x1 -> x2, other arithmetic: 2.69 us -> 3.46 us  [core_sum(): return [total_of([mine[i], came[i]]).astype(BF) for i in at]]
where the time goes in v6:
time: 135 us
  starting transfers between devices  32.8 us (24%)
  Pallas kernels  32.8 us (24%)
  blocking collectives  30.5 us (23%)
  waiting for transfers between devices  25.6 us (19%)
  other arithmetic  10.3 us (8%)
  local copies, waits for them, and re-layouts  1.87 us (1%)
    pallas_call x2, Pallas kernels, staged_call(): pl.pallas_call(kernel, out_shape=[out_shape(i) for i, _ in results], in_s...  32.8 us
    all_to_all x1, blocking collectives, to_rings(): return lax.all_to_all(block, RING, 0, 0, tiled=True)  30.5 us
    all_to_all x3, waiting for transfers between devices, to_rings(): return lax.all_to_all(block, RING, 0, 0, tiled=True)  14.2 us
    all_to_all x3, starting transfers between devices, to_rings(): return lax.all_to_all(block, RING, 0, 0, tiled=True)  12.2 us
    ppermute x6, starting transfers between devices, sent(): return lax.ppermute(piece(k), ('x', 'z', 'c'), route)  11.5 us
    ppermute x8, starting transfers between devices, passed(): lax.ppermute(block, axis, [(i, (i + distance) % size) for i in range(size)])  9.15 us
    ppermute x6, waiting for transfers between devices, sent(): return lax.ppermute(piece(k), ('x', 'z', 'c'), route)  7.01 us
    ppermute x8, waiting for transfers between devices, passed(): lax.ppermute(block, axis, [(i, (i + distance) % size) for i in range(size)])  4.34 us
  transfers between devices with their start and end apart: 17, of which 9 were waited for; matrix products, arithmetic and copies ran while one was open for 6% of the time, Pallas kernels for 24%

profile of v6, /device:TPU:0, one launch (start us, length us, event | category | flops | bytes accessed | tf_op | source)
XLA Modules:
  0.0 134.6 jit_solution(14670260194952858649)
XLA Ops:
  0.6 30.5 %all_to_all.20 = bf16[16,64,768]{2,1,0:T(8,128)(2,1)S(1)} all-to-all(bf16[16,64,768]{2,1,0:T(8,128)(2,1)} %bitcast.71), channel_id=1, replica_groups=mesh['x'=4,'z'=4,'yh'=2,'c'=2,'yl'=2] {'x','z'}, dimensions={0} | all-to-all | bytes 3145728 | tf_op jit(solution)/shard_map/all_to_all | solution.py:340
  31.2 3.8 %all-to-all-start = ((bf16[16,64,768]{2,1,0:T(8,128)(2,1)}), bf16[16,64,768]{2,1,0:T(8,128)(2,1)S(1)}, u32[]{:S(2)}, u32[]{:S(2)}) async-start(bf16[16,64,768]{2,1,0:T(8,128)(2,1)} %bitcast.72), calls=%async_computation | async-start | bytes 3145728 | tf_op jit(solution)/shard_map/all_to_all | solution.py:340
  35.0 15.5 %forward.1 = (bf16[1024,768]{1,0:T(8,128)(2,1)}, bf16[1024,768]{1,0:T(8,128)(2,1)}, bf16[1024,768]{1,0:T(8,128)(2,1)}, bf16[1024,384]{1,0:T(8,128)(2,1)}, bf16[1...) custom-call(bf16[1024,768]{1,0:T(8,128)(2,1)S(1)} %bitcast.67, ...), custom_call_target="tpu_custom_call" | custom-call | flops 1 | bytes 1 | tf_op jit(solution)/shard_map/forward/pallas_call | solution.py:141
  50.5 7.0 %all-to-all-done = bf16[16,64,768]{2,1,0:T(8,128)(2,1)S(1)} async-done(((bf16[16,64,768]{2,1,0:T(8,128)(2,1)}), bf16[16,64,768]{2,1,0:T(8,128)(2,1)S(1)}, u32[]{:S(2)}, u32[]{:S(2)}) %all-to-all-start) | async-done | bytes 1572896 | tf_op jit(solution)/shard_map/all_to_all | solution.py:340
  57.5 3.9 %all-to-all-start.2 = ((bf16[16,64,768]{2,1,0:T(8,128)(2,1)}), bf16[16,64,768]{2,1,0:T(8,128)(2,1)S(1)}, u32[]{:S(2)}, u32[]{:S(2)}) async-start(bf16[16,64,768]{2,1,0:T(8,128)(2,1)} %bitcast.74), calls=%async_computation.2 | async-start | bytes 3145728 | tf_op jit(solution)/shard_map/all_to_all | solution.py:340
  61.4 0.1 pad_add_fusion.refs_0_
  61.5 17.3 %backward.1 = (bf16[1024,768]{1,0:T(8,128)(2,1)}, bf16[4,96,1536]{2,1,0:T(8,128)(2,1)}, bf16[4,96,1536]{2,1,0:T(8,128)(2,1)}, bf16[4,96,1536]{2,1,0:T(8,128)(2,1)}, bf16[4,96,1536]{2,1,0:T(8,128)(2,1)}) custom-call(s32[2]{0:T(128)S(1)} %pad_add_fusion.refs_0_, bf16[1024,768]{1,0:T(8,128)(2,1)S(1)} %bitcast.66, bf16[2,384,768]{2,1,0:T(8,128)(2,1)} %refs_8_.1, ...), custom_call_target="tpu_custom_call" | custom-call | flops 1 | bytes 1 | tf_op jit(solution)/shard_map/backward/pallas_call | solution.py:141
  78.8 0.1 collective-permute-start
  78.9 0.5 collective-permute-start.1
  79.4 2.6 %all-to-all-done.2 = bf16[16,64,768]{2,1,0:T(8,128)(2,1)S(1)} async-done(((bf16[16,64,768]{2,1,0:T(8,128)(2,1)}), bf16[16,64,768]{2,1,0:T(8,128)(2,1)S(1)}, u32[]{:S(2)}, u32[]{:S(2)}) %all-to-all-start.2) | async-done | bytes 1572896 | tf_op jit(solution)/shard_map/all_to_all | solution.py:340
  81.9 4.4 %all-to-all-start.3 = ((bf16[16,64,768]{2,1,0:T(8,128)(2,1)}), bf16[16,64,768]{2,1,0:T(8,128)(2,1)S(1)}, u32[]{:S(2)}, u32[]{:S(2)}) async-start(bf16[16,64,768]{2,1,0:T(8,128)(2,1)} %bitcast.73), calls=%async_computation.3 | async-start | bytes 3145728 | tf_op jit(solution)/shard_map/all_to_all | solution.py:340
  86.4 0.0 copy-start
  86.4 0.0 collective-permute-done
  86.4 0.0 collective-permute-done.1
  86.4 1.5 %fusion.3 = (bf16[96,1536]{1,0:T(8,128)(2,1)S(1)}, bf16[96,1536]{1,0:T(8,128)(2,1)S(1)}) fusion(bf16[4,96,1536]{2,1,0:T(8,128)(2,1)} %collective-permute-done, bf16[4,96,1536]{2,1,0:T(8,128)(2,1)} %get-tuple-element.43), kind=kLoop, calls=%fused_computation.15 | loop fusion | flops 1179648 | bytes 1769472 | tf_op jit(solution)/shard_map/convert_element_type | solution.py:356
  87.9 0.0 copy-start.1
  87.9 1.6 %collective-permute-start.4 = (bf16[96,1536]{1,0:T(8,128)(2,1)S(1)}, bf16[96,1536]{1,0:T(8,128)(2,1)S(1)}, u32[]{:S(2)}, u32[]{:S(2)}) collective-permute-start(bf16[96,1536]{1,0:T(8,128)(2,1)S(1)} %get-tuple-element.46), channel_id=1, source_target_pairs={{0,1},{1,4},{4,5},{5,0},{2,3},{3,6},{6,7},{7,2},{8,9},{9,12},{12,1... | collective-permute-start | bytes 884744 | tf_op jit(solution)/shard_map/ppermute | solution.py:345
  89.5 1.7 %collective-permute-start.6 = (bf16[96,1536]{1,0:T(8,128)(2,1)S(1)}, bf16[96,1536]{1,0:T(8,128)(2,1)S(1)}, u32[]{:S(2)}, u32[]{:S(2)}) collective-permute-start(bf16[96,1536]{1,0:T(8,128)(2,1)S(1)} %get-tuple-element.47), channel_id=1, source_target_pairs={{0,5},{1,0},{4,1},{5,4},{2,7},{3,2},{6,3},{7,6},{8,13},{9,8},{12,9... | collective-permute-start | bytes 884744 | tf_op jit(solution)/shard_map/ppermute | solution.py:345
  91.2 0.0 copy-done
  91.2 2.0 %fusion.4 = (bf16[96,1536]{1,0:T(8,128)(2,1)}, bf16[96,1536]{1,0:T(8,128)(2,1)}) fusion(bf16[4,96,1536]{2,1,0:T(8,128)(2,1)} %collective-permute-done, bf16[4,96,1536]{2,1,0:T(8,128)(2,1)S(1)} %copy-done), kind=kLoop, calls=%fused_computation.16 | loop fusion | flops 1179648 | bytes 1769472 | tf_op jit(solution)/shard_map/convert_element_type | solution.py:356
  93.2 1.8 %collective-permute-start.2 = (bf16[96,1536]{1,0:T(8,128)(2,1)}, bf16[96,1536]{1,0:T(8,128)(2,1)S(1)}, u32[]{:S(2)}, u32[]{:S(2)}) collective-permute-start(bf16[96,1536]{1,0:T(8,128)(2,1)} %get-tuple-element.62), channel_id=1, source_target_pairs={{0,5},{1,0},{4,1},{5,4},{2,7},{3,2},{6,3},{7,6},{8,13},{9,8},{12,9... | collective-permute-start | bytes 884744 | tf_op jit(solution)/shard_map/ppermute | solution.py:345
  95.0 0.2 collective-permute-start.3
  95.2 2.7 %collective-permute-done.4 = bf16[96,1536]{1,0:T(8,128)(2,1)S(1)} collective-permute-done((bf16[96,1536]{1,0:T(8,128)(2,1)S(1)}, bf16[96,1536]{1,0:T(8,128)(2,1)S(1)}, u32[]{:S(2)}, u32[]{:S(2)}) %collective-permute-start.4) | collective-permute-done | bytes 294944 | tf_op jit(solution)/shard_map/ppermute | solution.py:345
  97.9 1.5 %collective-permute-done.6 = bf16[96,1536]{1,0:T(8,128)(2,1)S(1)} collective-permute-done((bf16[96,1536]{1,0:T(8,128)(2,1)S(1)}, bf16[96,1536]{1,0:T(8,128)(2,1)S(1)}, u32[]{:S(2)}, u32[]{:S(2)}) %collective-permute-start.6) | collective-permute-done | bytes 294944 | tf_op jit(solution)/shard_map/ppermute | solution.py:345
  99.4 0.0 copy-done.1
  99.4 2.1 %fusion = (bf16[96,1536]{1,0:T(8,128)(2,1)}, bf16[96,1536]{1,0:T(8,128)(2,1)}) fusion(bf16[96,1536]{1,0:T(8,128)(2,1)S(1)} %collective-permute-done.6, bf16[4,96,1536]{2,1,0:T(8,128)(2,1)} %collective-permute-done.1, bf16[4,96,1536]{2,1,0:T(8,128)(2,1)S(1)} %copy-done.1, bf16[96,1536]{1,0:T(8,128)(2,1)S(1)} %collective-permute-done.4), kind=kLoop, calls=%fused_computation.5 | loop fusion | flops 2359296 | bytes 2359296 | tf_op jit(solution)/shard_map/convert_element_type | solution.py:365
  101.5 1.6 %collective-permute-start.5 = (bf16[96,1536]{1,0:T(8,128)(2,1)}, bf16[96,1536]{1,0:T(8,128)(2,1)}, u32[]{:S(2)}, u32[]{:S(2)}) collective-permute-start(bf16[96,1536]{1,0:T(8,128)(2,1)} %get-tuple-element.61), channel_id=1, source_target_pairs={{0,1},{1,4},{4,5},{5,0},{2,3},{3,6},{6,7},{7,2},{8,9},{9,12},{12,1... | collective-permute-start | bytes 884744 | tf_op jit(solution)/shard_map/ppermute | solution.py:345
  103.1 1.6 %collective-permute-start.7 = (bf16[96,1536]{1,0:T(8,128)(2,1)}, bf16[96,1536]{1,0:T(8,128)(2,1)}, u32[]{:S(2)}, u32[]{:S(2)}) collective-permute-start(bf16[96,1536]{1,0:T(8,128)(2,1)} %get-tuple-element.60), channel_id=1, source_target_pairs={{0,5},{1,0},{4,1},{5,4},{2,7},{3,2},{6,3},{7,6},{8,13},{9,8},{12,9... | collective-permute-start | bytes 884744 | tf_op jit(solution)/shard_map/ppermute | solution.py:345
  104.8 1.2 broadcast_multiply_fusion.1
  106.0 4.6 %all-to-all-done.3 = bf16[16,64,768]{2,1,0:T(8,128)(2,1)S(1)} async-done(((bf16[16,64,768]{2,1,0:T(8,128)(2,1)}), bf16[16,64,768]{2,1,0:T(8,128)(2,1)S(1)}, u32[]{:S(2)}, u32[]{:S(2)}) %all-to-all-start.3) | async-done | bytes 1572896 | tf_op jit(solution)/shard_map/all_to_all | solution.py:340
  110.6 0.1 collective-permute-done.5
  110.7 0.0 collective-permute-done.7
  110.7 0.0 collective-permute-done.2
  110.7 0.0 collective-permute-done.3
  110.7 1.8 %add_convert_fusion = bf16[2,96,1536]{2,1,0:T(8,128)(2,1)S(1)} fusion(bf16[1,96,1536]{2,1,0:T(8,128)(2,1)} %bitcast.13, bf16[1,96,1536]{2,1,0:T(8,128)(2,1)S(1)} %bitcast.77, bf16[1,96,1536]{2,1,0:T(8,128)(2,1)} %bitcast.19, bf16[1,96,1536]{2,1,0:T(8,128)(2,1)} %bitcast.18, bf16[4,96,1536]{2,1,0:T(8,128)(2,1)} %collective-permute-done.1, ...), kind=kLoop, calls=%fused_computation | loop fusion | flops 3538944 | bytes 2949120 | tf_op jit(solution)/shard_map/convert_element_type | solution.py:367
  112.6 0.1 constant_dynamic-slice_fusion.3
  112.6 0.1 copy.23
  112.7 2.9 %collective-permute-start.10 = (bf16[2,24,1536]{2,0,1:T(2,128)(2,1)S(1)}, bf16[2,24,1536]{2,0,1:T(2,128)(2,1)S(1)}, u32[]{:S(2)}, u32[]{:S(2)}) collective-permute-start(bf16[2,24,1536]{2,0,1:T(2,128)(2,1)S(1)} %bitcast.78), channel_id=1, source_target_pairs={{0,96},{2,26},{8,104},{10,2},{16,112},{18,10},{24,120},{26,18},{32... | collective-permute-start | bytes 442376 | tf_op jit(solution)/shard_map/ppermute | solution.py:384
  115.7 0.1 copy.25
  115.8 0.9 collective-permute-start.8
  116.7 0.1 copy.24
  116.8 0.9 collective-permute-start.9
  117.8 1.2 broadcast_multiply_fusion
  119.0 0.0 collective-permute-done.10
  119.0 3.6 %collective-permute-done.8 = bf16[2,24,1536]{2,0,1:T(2,128)(2,1)S(1)} collective-permute-done((bf16[2,24,1536]{2,0,1:T(2,128)(2,1)S(1)}, bf16[2,24,1536]{2,0,1:T(2,128)(2,1)S(1)}, u32[]{:S(2)}, u32[]{:S(2)}) %collective-permute-start.8) | collective-permute-done | bytes 147488 | tf_op jit(solution)/shard_map/ppermute | solution.py:384
  122.6 1.5 %collective-permute-done.9 = bf16[2,24,1536]{2,0,1:T(2,128)(2,1)S(1)} collective-permute-done((bf16[2,24,1536]{2,0,1:T(2,128)(2,1)S(1)}, bf16[2,24,1536]{2,0,1:T(2,128)(2,1)S(1)}, u32[]{:S(2)}, u32[]{:S(2)}) %collective-permute-start.9) | collective-permute-done | bytes 147488 | tf_op jit(solution)/shard_map/ppermute | solution.py:384
  124.1 0.3 fusion.10
  124.4 0.1 dynamic-slice_bitcast_fusion.2
  124.5 3.4 %collective-permute-start.11 = (bf16[2,6,1536]{2,0,1:T(2,128)(2,1)S(1)}, bf16[2,6,1536]{2,0,1:T(2,128)(2,1)S(1)}, u32[]{:S(2)}, u32[]{:S(2)}) collective-permute-start(bf16[2,6,1536]{2,0,1:T(2,128)(2,1)S(1)} %get-tuple-element.70), channel_id=1, source_target_pairs={{0,16},{2,66},{8,24},{10,74},{16,0},{18,82},{24,8},{26,90},{32,48}... | collective-permute-start | bytes 110600 | tf_op jit(solution)/shard_map/ppermute | solution.py:384
  127.9 0.6 collective-permute-start.12
  128.5 2.7 %collective-permute-start.13 = (bf16[2,6,1536]{2,0,1:T(2,128)(2,1)S(1)}, bf16[2,6,1536]{2,0,1:T(2,128)(2,1)S(1)}, u32[]{:S(2)}, u32[]{:S(2)}) collective-permute-start(bf16[2,6,1536]{2,0,1:T(2,128)(2,1)S(1)} %get-tuple-element.71), channel_id=1, source_target_pairs={{0,24},{2,98},{8,0},{10,106},{16,8},{18,114},{24,16},{26,122},{32,... | collective-permute-start | bytes 110600 | tf_op jit(solution)/shard_map/ppermute | solution.py:384
  131.1 0.0 collective-permute-done.11
  131.1 1.9 %collective-permute-done.12 = bf16[2,6,1536]{2,0,1:T(2,128)(2,1)S(1)} collective-permute-done((bf16[2,6,1536]{2,0,1:T(2,128)(2,1)S(1)}, bf16[2,6,1536]{2,0,1:T(2,128)(2,1)S(1)}, u32[]{:S(2)}, u32[]{:S(2)}) %collective-permute-start.12) | collective-permute-done | bytes 36896 | tf_op jit(solution)/shard_map/ppermute | solution.py:384
  133.1 0.0 collective-permute-done.13
  133.1 0.1 fusion.13
  133.2 0.1 reshape.83
  133.3 0.7 copy.13
  134.0 0.6 copy.26
  (2 shorter events, 0.0 us)
Async XLA Ops:
  31.2 26.4 %all-to-all-start = ((bf16[16,64,768]{2,1,0:T(8,128)(2,1)}), bf16[16,64,768]{2,1,0:T(8,128)(2,1)S(1)}, u32[]{:S(2)}, u32[]{:S(2)}) async-start(bf16[16,64,768]{2,1,0:T(8,128)(2,1)} %bitcast.72), calls=%async_computation | async-start | bytes 3145728 | tf_op jit(solution)/shard_map/all_to_all | solution.py:340
  57.5 24.4 %all-to-all-start.2 = ((bf16[16,64,768]{2,1,0:T(8,128)(2,1)}), bf16[16,64,768]{2,1,0:T(8,128)(2,1)S(1)}, u32[]{:S(2)}, u32[]{:S(2)}) async-start(bf16[16,64,768]{2,1,0:T(8,128)(2,1)} %bitcast.74), calls=%async_computation.2 | async-start | bytes 3145728 | tf_op jit(solution)/shard_map/all_to_all | solution.py:340
  78.8 7.6 %collective-permute-start = (bf16[4,96,1536]{2,1,0:T(8,128)(2,1)}, bf16[4,96,1536]{2,1,0:T(8,128)(2,1)}, u32[]{:S(2)}, u32[]{:S(2)}) collective-permute-start(bf16[4,96,1536]{2,1,0:T(8,128)(2,1)} %get-tuple-element.39), channel_id=1, source_target_pairs={{0,2},{2,0},{1,3},{3,1},{4,6},{6,4},{5,7},{7,5},{8,10},{10,8},{9,1... | collective-permute-start | bytes 3538952 | tf_op jit(solution)/shard_map/ppermute | solution.py:345
  78.9 7.5 %collective-permute-start.1 = (bf16[4,96,1536]{2,1,0:T(8,128)(2,1)}, bf16[4,96,1536]{2,1,0:T(8,128)(2,1)}, u32[]{:S(2)}, u32[]{:S(2)}) collective-permute-start(bf16[4,96,1536]{2,1,0:T(8,128)(2,1)} %get-tuple-element.40), channel_id=1, source_target_pairs={{0,2},{2,0},{1,3},{3,1},{4,6},{6,4},{5,7},{7,5},{8,10},{10,8},{9,1... | collective-permute-start | bytes 3538952 | tf_op jit(solution)/shard_map/ppermute | solution.py:345
  81.9 28.7 %all-to-all-start.3 = ((bf16[16,64,768]{2,1,0:T(8,128)(2,1)}), bf16[16,64,768]{2,1,0:T(8,128)(2,1)S(1)}, u32[]{:S(2)}, u32[]{:S(2)}) async-start(bf16[16,64,768]{2,1,0:T(8,128)(2,1)} %bitcast.73), calls=%async_computation.3 | async-start | bytes 3145728 | tf_op jit(solution)/shard_map/all_to_all | solution.py:340
  86.4 4.8 %copy-start = (bf16[4,96,1536]{2,1,0:T(8,128)(2,1)S(1)}, bf16[4,96,1536]{2,1,0:T(8,128)(2,1)}, u32[]{:S(2)}) copy-start(bf16[4,96,1536]{2,1,0:T(8,128)(2,1)} %get-tuple-element.43) | copy-start | bytes 3538948
  87.9 11.6 %copy-start.1 = (bf16[4,96,1536]{2,1,0:T(8,128)(2,1)S(1)}, bf16[4,96,1536]{2,1,0:T(8,128)(2,1)}, u32[]{:S(2)}) copy-start(bf16[4,96,1536]{2,1,0:T(8,128)(2,1)} %get-tuple-element.38) | copy-start | bytes 3538948
  87.9 10.1 %collective-permute-start.4 = (bf16[96,1536]{1,0:T(8,128)(2,1)S(1)}, bf16[96,1536]{1,0:T(8,128)(2,1)S(1)}, u32[]{:S(2)}, u32[]{:S(2)}) collective-permute-start(bf16[96,1536]{1,0:T(8,128)(2,1)S(1)} %get-tuple-element.46), channel_id=1, source_target_pairs={{0,1},{1,4},{4,5},{5,0},{2,3},{3,6},{6,7},{7,2},{8,9},{9,12},{12,1... | collective-permute-start | bytes 884744 | tf_op jit(solution)/shard_map/ppermute | solution.py:345
  89.5 9.9 %collective-permute-start.6 = (bf16[96,1536]{1,0:T(8,128)(2,1)S(1)}, bf16[96,1536]{1,0:T(8,128)(2,1)S(1)}, u32[]{:S(2)}, u32[]{:S(2)}) collective-permute-start(bf16[96,1536]{1,0:T(8,128)(2,1)S(1)} %get-tuple-element.47), channel_id=1, source_target_pairs={{0,5},{1,0},{4,1},{5,4},{2,7},{3,2},{6,3},{7,6},{8,13},{9,8},{12,9... | collective-permute-start | bytes 884744 | tf_op jit(solution)/shard_map/ppermute | solution.py:345
  93.2 17.6 %collective-permute-start.2 = (bf16[96,1536]{1,0:T(8,128)(2,1)}, bf16[96,1536]{1,0:T(8,128)(2,1)S(1)}, u32[]{:S(2)}, u32[]{:S(2)}) collective-permute-start(bf16[96,1536]{1,0:T(8,128)(2,1)} %get-tuple-element.62), channel_id=1, source_target_pairs={{0,5},{1,0},{4,1},{5,4},{2,7},{3,2},{6,3},{7,6},{8,13},{9,8},{12,9... | collective-permute-start | bytes 884744 | tf_op jit(solution)/shard_map/ppermute | solution.py:345
  95.0 15.7 %collective-permute-start.3 = (bf16[96,1536]{1,0:T(8,128)(2,1)}, bf16[96,1536]{1,0:T(8,128)(2,1)}, u32[]{:S(2)}, u32[]{:S(2)}) collective-permute-start(bf16[96,1536]{1,0:T(8,128)(2,1)} %get-tuple-element.63), channel_id=1, source_target_pairs={{0,1},{1,4},{4,5},{5,0},{2,3},{3,6},{6,7},{7,2},{8,9},{9,12},{12,1... | collective-permute-start | bytes 884744 | tf_op jit(solution)/shard_map/ppermute | solution.py:345
  101.5 9.2 %collective-permute-start.5 = (bf16[96,1536]{1,0:T(8,128)(2,1)}, bf16[96,1536]{1,0:T(8,128)(2,1)}, u32[]{:S(2)}, u32[]{:S(2)}) collective-permute-start(bf16[96,1536]{1,0:T(8,128)(2,1)} %get-tuple-element.61), channel_id=1, source_target_pairs={{0,1},{1,4},{4,5},{5,0},{2,3},{3,6},{6,7},{7,2},{8,9},{9,12},{12,1... | collective-permute-start | bytes 884744 | tf_op jit(solution)/shard_map/ppermute | solution.py:345
  103.1 7.6 %collective-permute-start.7 = (bf16[96,1536]{1,0:T(8,128)(2,1)}, bf16[96,1536]{1,0:T(8,128)(2,1)}, u32[]{:S(2)}, u32[]{:S(2)}) collective-permute-start(bf16[96,1536]{1,0:T(8,128)(2,1)} %get-tuple-element.60), channel_id=1, source_target_pairs={{0,5},{1,0},{4,1},{5,4},{2,7},{3,2},{6,3},{7,6},{8,13},{9,8},{12,9... | collective-permute-start | bytes 884744 | tf_op jit(solution)/shard_map/ppermute | solution.py:345
  112.7 6.3 %collective-permute-start.10 = (bf16[2,24,1536]{2,0,1:T(2,128)(2,1)S(1)}, bf16[2,24,1536]{2,0,1:T(2,128)(2,1)S(1)}, u32[]{:S(2)}, u32[]{:S(2)}) collective-permute-start(bf16[2,24,1536]{2,0,1:T(2,128)(2,1)S(1)} %bitcast.78), channel_id=1, source_target_pairs={{0,96},{2,26},{8,104},{10,2},{16,112},{18,10},{24,120},{26,18},{32... | collective-permute-start | bytes 442376 | tf_op jit(solution)/shard_map/ppermute | solution.py:384
  115.8 6.8 %collective-permute-start.8 = (bf16[2,24,1536]{2,0,1:T(2,128)(2,1)S(1)}, bf16[2,24,1536]{2,0,1:T(2,128)(2,1)S(1)}, u32[]{:S(2)}, u32[]{:S(2)}) collective-permute-start(bf16[2,24,1536]{2,0,1:T(2,128)(2,1)S(1)} %bitcast.79), channel_id=1, source_target_pairs={{0,64},{2,18},{8,72},{10,26},{16,80},{18,2},{24,88},{26,10},{32,96... | collective-permute-start | bytes 442376 | tf_op jit(solution)/shard_map/ppermute | solution.py:384
  116.8 7.3 %collective-permute-start.9 = (bf16[2,24,1536]{2,0,1:T(2,128)(2,1)S(1)}, bf16[2,24,1536]{2,0,1:T(2,128)(2,1)S(1)}, u32[]{:S(2)}, u32[]{:S(2)}) collective-permute-start(bf16[2,24,1536]{2,0,1:T(2,128)(2,1)S(1)} %bitcast.80), channel_id=1, source_target_pairs={{0,32},{2,10},{8,40},{10,18},{16,48},{18,26},{24,56},{26,2},{32,64... | collective-permute-start | bytes 442376 | tf_op jit(solution)/shard_map/ppermute | solution.py:384
  124.5 6.7 %collective-permute-start.11 = (bf16[2,6,1536]{2,0,1:T(2,128)(2,1)S(1)}, bf16[2,6,1536]{2,0,1:T(2,128)(2,1)S(1)}, u32[]{:S(2)}, u32[]{:S(2)}) collective-permute-start(bf16[2,6,1536]{2,0,1:T(2,128)(2,1)S(1)} %get-tuple-element.70), channel_id=1, source_target_pairs={{0,16},{2,66},{8,24},{10,74},{16,0},{18,82},{24,8},{26,90},{32,48}... | collective-permute-start | bytes 110600 | tf_op jit(solution)/shard_map/ppermute | solution.py:384
  127.9 5.2 %collective-permute-start.12 = (bf16[2,6,1536]{2,0,1:T(2,128)(2,1)S(1)}, bf16[2,6,1536]{2,0,1:T(2,128)(2,1)S(1)}, u32[]{:S(2)}, u32[]{:S(2)}) collective-permute-start(bf16[2,6,1536]{2,0,1:T(2,128)(2,1)S(1)} %get-tuple-element.72), channel_id=1, source_target_pairs={{0,8},{2,34},{8,16},{10,42},{16,24},{18,50},{24,0},{26,58},{32,40}... | collective-permute-start | bytes 110600 | tf_op jit(solution)/shard_map/ppermute | solution.py:384
  128.5 4.6 %collective-permute-start.13 = (bf16[2,6,1536]{2,0,1:T(2,128)(2,1)S(1)}, bf16[2,6,1536]{2,0,1:T(2,128)(2,1)S(1)}, u32[]{:S(2)}, u32[]{:S(2)}) collective-permute-start(bf16[2,6,1536]{2,0,1:T(2,128)(2,1)S(1)} %get-tuple-element.71), channel_id=1, source_target_pairs={{0,24},{2,98},{8,0},{10,106},{16,8},{18,114},{24,16},{26,122},{32,... | collective-permute-start | bytes 110600 | tf_op jit(solution)/shard_map/ppermute | solution.py:384

commit v7 on v6

--- a/solution.py
+++ b/solution.py
@@ -283,7 +283,7 @@
 def proj_terms(place_ref, grad_ref, activ_ref, part_ref, b, sum_ref, order_ref):
     chans, wide = grad_ref.shape[1], activ_ref.shape[1]
     share = chans // 128
-    sum_ref[...] = dot_rows(grad_ref[...], activ_ref[...])
+    sum_ref[:chans, :] = dot_rows(grad_ref[...], activ_ref[...])
     for c in range(2):
         for y in range(4):
             ordered = order_ref.at[c * 4 + y]
@@ -329,8 +329,8 @@
         [
             pltpu.VMEM((total, chans), BF),
             pltpu.VMEM((total, 3 * mids), BF),
-            pltpu.VMEM((chans, mids), F32),
-            pltpu.VMEM((8, rows, mids), F32),
+            pltpu.VMEM((chans + 8, mids), F32),
+            pltpu.VMEM((9, rows, mids), F32),
         ],
         3, place,
     )

time: 135 us -> 135 us (level)
  no operation moved by 1% of the time
where the time goes in v7:
time: 135 us
  starting transfers between devices  32.8 us (24%)
  Pallas kernels  32.8 us (24%)
  blocking collectives  30.5 us (23%)
  waiting for transfers between devices  25.5 us (19%)
  other arithmetic  10.3 us (8%)
  local copies, waits for them, and re-layouts  1.87 us (1%)
    pallas_call x2, Pallas kernels, staged_call(): pl.pallas_call(kernel, out_shape=[out_shape(i) for i, _ in results], in_s...  32.8 us
    all_to_all x1, blocking collectives, to_rings(): return lax.all_to_all(block, RING, 0, 0, tiled=True)  30.5 us
    all_to_all x3, waiting for transfers between devices, to_rings(): return lax.all_to_all(block, RING, 0, 0, tiled=True)  14.2 us
    all_to_all x3, starting transfers between devices, to_rings(): return lax.all_to_all(block, RING, 0, 0, tiled=True)  12.2 us
    ppermute x6, starting transfers between devices, sent(): return lax.ppermute(piece(k), ('x', 'z', 'c'), route)  11.5 us
    ppermute x8, starting transfers between devices, passed(): lax.ppermute(block, axis, [(i, (i + distance) % size) for i in range(size)])  9.15 us
    ppermute x6, waiting for transfers between devices, sent(): return lax.ppermute(piece(k), ('x', 'z', 'c'), route)  7.01 us
    ppermute x8, waiting for transfers between devices, passed(): lax.ppermute(block, axis, [(i, (i + distance) % size) for i in range(size)])  4.33 us
  transfers between devices with their start and end apart: 17, of which 9 were waited for; matrix products, arithmetic and copies ran while one was open for 6% of the time, Pallas kernels for 24%

profile of v7, /device:TPU:0, one launch (start us, length us, event | category | flops | bytes accessed | tf_op | source)
XLA Modules:
  0.0 134.6 jit_solution(13616807988968916380)
XLA Ops:
  0.6 30.5 %all_to_all.20 = bf16[16,64,768]{2,1,0:T(8,128)(2,1)S(1)} all-to-all(bf16[16,64,768]{2,1,0:T(8,128)(2,1)} %bitcast.71), channel_id=1, replica_groups=mesh['x'=4,'z'=4,'yh'=2,'c'=2,'yl'=2] {'x','z'}, dimensions={0} | all-to-all | bytes 3145728 | tf_op jit(solution)/shard_map/all_to_all | solution.py:340
  31.2 3.8 %all-to-all-start = ((bf16[16,64,768]{2,1,0:T(8,128)(2,1)}), bf16[16,64,768]{2,1,0:T(8,128)(2,1)S(1)}, u32[]{:S(2)}, u32[]{:S(2)}) async-start(bf16[16,64,768]{2,1,0:T(8,128)(2,1)} %bitcast.72), calls=%async_computation | async-start | bytes 3145728 | tf_op jit(solution)/shard_map/all_to_all | solution.py:340
  35.0 15.5 %forward.1 = (bf16[1024,768]{1,0:T(8,128)(2,1)}, bf16[1024,768]{1,0:T(8,128)(2,1)}, bf16[1024,768]{1,0:T(8,128)(2,1)}, bf16[1024,384]{1,0:T(8,128)(2,1)}, bf16[1...) custom-call(bf16[1024,768]{1,0:T(8,128)(2,1)S(1)} %bitcast.67, ...), custom_call_target="tpu_custom_call" | custom-call | flops 1 | bytes 1 | tf_op jit(solution)/shard_map/forward/pallas_call | solution.py:141
  50.5 7.0 %all-to-all-done = bf16[16,64,768]{2,1,0:T(8,128)(2,1)S(1)} async-done(((bf16[16,64,768]{2,1,0:T(8,128)(2,1)}), bf16[16,64,768]{2,1,0:T(8,128)(2,1)S(1)}, u32[]{:S(2)}, u32[]{:S(2)}) %all-to-all-start) | async-done | bytes 1572896 | tf_op jit(solution)/shard_map/all_to_all | solution.py:340
  57.5 3.9 %all-to-all-start.2 = ((bf16[16,64,768]{2,1,0:T(8,128)(2,1)}), bf16[16,64,768]{2,1,0:T(8,128)(2,1)S(1)}, u32[]{:S(2)}, u32[]{:S(2)}) async-start(bf16[16,64,768]{2,1,0:T(8,128)(2,1)} %bitcast.74), calls=%async_computation.2 | async-start | bytes 3145728 | tf_op jit(solution)/shard_map/all_to_all | solution.py:340
  61.4 0.1 pad_add_fusion.refs_0_
  61.5 17.3 %backward.1 = (bf16[1024,768]{1,0:T(8,128)(2,1)}, bf16[4,96,1536]{2,1,0:T(8,128)(2,1)}, bf16[4,96,1536]{2,1,0:T(8,128)(2,1)}, bf16[4,96,1536]{2,1,0:T(8,128)(2,1)}, bf16[4,96,1536]{2,1,0:T(8,128)(2,1)}) custom-call(s32[2]{0:T(128)S(1)} %pad_add_fusion.refs_0_, bf16[1024,768]{1,0:T(8,128)(2,1)S(1)} %bitcast.66, bf16[2,384,768]{2,1,0:T(8,128)(2,1)} %refs_8_.1, ...), custom_call_target="tpu_custom_call" | custom-call | flops 1 | bytes 1 | tf_op jit(solution)/shard_map/backward/pallas_call | solution.py:141
  78.8 0.1 collective-permute-start
  78.9 0.5 collective-permute-start.1
  79.4 2.6 %all-to-all-done.2 = bf16[16,64,768]{2,1,0:T(8,128)(2,1)S(1)} async-done(((bf16[16,64,768]{2,1,0:T(8,128)(2,1)}), bf16[16,64,768]{2,1,0:T(8,128)(2,1)S(1)}, u32[]{:S(2)}, u32[]{:S(2)}) %all-to-all-start.2) | async-done | bytes 1572896 | tf_op jit(solution)/shard_map/all_to_all | solution.py:340
  81.9 4.4 %all-to-all-start.3 = ((bf16[16,64,768]{2,1,0:T(8,128)(2,1)}), bf16[16,64,768]{2,1,0:T(8,128)(2,1)S(1)}, u32[]{:S(2)}, u32[]{:S(2)}) async-start(bf16[16,64,768]{2,1,0:T(8,128)(2,1)} %bitcast.73), calls=%async_computation.3 | async-start | bytes 3145728 | tf_op jit(solution)/shard_map/all_to_all | solution.py:340
  86.4 0.0 copy-start
  86.4 0.0 collective-permute-done
  86.4 0.0 collective-permute-done.1
  86.4 1.5 %fusion.3 = (bf16[96,1536]{1,0:T(8,128)(2,1)S(1)}, bf16[96,1536]{1,0:T(8,128)(2,1)S(1)}) fusion(bf16[4,96,1536]{2,1,0:T(8,128)(2,1)} %collective-permute-done, bf16[4,96,1536]{2,1,0:T(8,128)(2,1)} %get-tuple-element.43), kind=kLoop, calls=%fused_computation.15 | loop fusion | flops 1179648 | bytes 1769472 | tf_op jit(solution)/shard_map/convert_element_type | solution.py:356
  87.9 0.0 copy-start.1
  87.9 1.6 %collective-permute-start.4 = (bf16[96,1536]{1,0:T(8,128)(2,1)S(1)}, bf16[96,1536]{1,0:T(8,128)(2,1)S(1)}, u32[]{:S(2)}, u32[]{:S(2)}) collective-permute-start(bf16[96,1536]{1,0:T(8,128)(2,1)S(1)} %get-tuple-element.46), channel_id=1, source_target_pairs={{0,1},{1,4},{4,5},{5,0},{2,3},{3,6},{6,7},{7,2},{8,9},{9,12},{12,1... | collective-permute-start | bytes 884744 | tf_op jit(solution)/shard_map/ppermute | solution.py:345
  89.5 1.7 %collective-permute-start.6 = (bf16[96,1536]{1,0:T(8,128)(2,1)S(1)}, bf16[96,1536]{1,0:T(8,128)(2,1)S(1)}, u32[]{:S(2)}, u32[]{:S(2)}) collective-permute-start(bf16[96,1536]{1,0:T(8,128)(2,1)S(1)} %get-tuple-element.47), channel_id=1, source_target_pairs={{0,5},{1,0},{4,1},{5,4},{2,7},{3,2},{6,3},{7,6},{8,13},{9,8},{12,9... | collective-permute-start | bytes 884744 | tf_op jit(solution)/shard_map/ppermute | solution.py:345
  91.2 0.0 copy-done
  91.2 2.0 %fusion.4 = (bf16[96,1536]{1,0:T(8,128)(2,1)}, bf16[96,1536]{1,0:T(8,128)(2,1)}) fusion(bf16[4,96,1536]{2,1,0:T(8,128)(2,1)} %collective-permute-done, bf16[4,96,1536]{2,1,0:T(8,128)(2,1)S(1)} %copy-done), kind=kLoop, calls=%fused_computation.16 | loop fusion | flops 1179648 | bytes 1769472 | tf_op jit(solution)/shard_map/convert_element_type | solution.py:356
  93.2 1.8 %collective-permute-start.2 = (bf16[96,1536]{1,0:T(8,128)(2,1)}, bf16[96,1536]{1,0:T(8,128)(2,1)S(1)}, u32[]{:S(2)}, u32[]{:S(2)}) collective-permute-start(bf16[96,1536]{1,0:T(8,128)(2,1)} %get-tuple-element.62), channel_id=1, source_target_pairs={{0,5},{1,0},{4,1},{5,4},{2,7},{3,2},{6,3},{7,6},{8,13},{9,8},{12,9... | collective-permute-start | bytes 884744 | tf_op jit(solution)/shard_map/ppermute | solution.py:345
  95.0 0.2 collective-permute-start.3
  95.2 2.7 %collective-permute-done.4 = bf16[96,1536]{1,0:T(8,128)(2,1)S(1)} collective-permute-done((bf16[96,1536]{1,0:T(8,128)(2,1)S(1)}, bf16[96,1536]{1,0:T(8,128)(2,1)S(1)}, u32[]{:S(2)}, u32[]{:S(2)}) %collective-permute-start.4) | collective-permute-done | bytes 294944 | tf_op jit(solution)/shard_map/ppermute | solution.py:345
  97.9 1.5 %collective-permute-done.6 = bf16[96,1536]{1,0:T(8,128)(2,1)S(1)} collective-permute-done((bf16[96,1536]{1,0:T(8,128)(2,1)S(1)}, bf16[96,1536]{1,0:T(8,128)(2,1)S(1)}, u32[]{:S(2)}, u32[]{:S(2)}) %collective-permute-start.6) | collective-permute-done | bytes 294944 | tf_op jit(solution)/shard_map/ppermute | solution.py:345
  99.4 0.0 copy-done.1
  99.4 2.1 %fusion = (bf16[96,1536]{1,0:T(8,128)(2,1)}, bf16[96,1536]{1,0:T(8,128)(2,1)}) fusion(bf16[96,1536]{1,0:T(8,128)(2,1)S(1)} %collective-permute-done.6, bf16[4,96,1536]{2,1,0:T(8,128)(2,1)} %collective-permute-done.1, bf16[4,96,1536]{2,1,0:T(8,128)(2,1)S(1)} %copy-done.1, bf16[96,1536]{1,0:T(8,128)(2,1)S(1)} %collective-permute-done.4), kind=kLoop, calls=%fused_computation.5 | loop fusion | flops 2359296 | bytes 2359296 | tf_op jit(solution)/shard_map/convert_element_type | solution.py:365
  101.5 1.6 %collective-permute-start.5 = (bf16[96,1536]{1,0:T(8,128)(2,1)}, bf16[96,1536]{1,0:T(8,128)(2,1)}, u32[]{:S(2)}, u32[]{:S(2)}) collective-permute-start(bf16[96,1536]{1,0:T(8,128)(2,1)} %get-tuple-element.61), channel_id=1, source_target_pairs={{0,1},{1,4},{4,5},{5,0},{2,3},{3,6},{6,7},{7,2},{8,9},{9,12},{12,1... | collective-permute-start | bytes 884744 | tf_op jit(solution)/shard_map/ppermute | solution.py:345
  103.1 1.7 %collective-permute-start.7 = (bf16[96,1536]{1,0:T(8,128)(2,1)}, bf16[96,1536]{1,0:T(8,128)(2,1)}, u32[]{:S(2)}, u32[]{:S(2)}) collective-permute-start(bf16[96,1536]{1,0:T(8,128)(2,1)} %get-tuple-element.60), channel_id=1, source_target_pairs={{0,5},{1,0},{4,1},{5,4},{2,7},{3,2},{6,3},{7,6},{8,13},{9,8},{12,9... | collective-permute-start | bytes 884744 | tf_op jit(solution)/shard_map/ppermute | solution.py:345
  104.8 1.2 broadcast_multiply_fusion.1
  106.0 4.6 %all-to-all-done.3 = bf16[16,64,768]{2,1,0:T(8,128)(2,1)S(1)} async-done(((bf16[16,64,768]{2,1,0:T(8,128)(2,1)}), bf16[16,64,768]{2,1,0:T(8,128)(2,1)S(1)}, u32[]{:S(2)}, u32[]{:S(2)}) %all-to-all-start.3) | async-done | bytes 1572896 | tf_op jit(solution)/shard_map/all_to_all | solution.py:340
  110.6 0.1 collective-permute-done.5
  110.7 0.0 collective-permute-done.7
  110.7 0.0 collective-permute-done.2
  110.7 0.0 collective-permute-done.3
  110.7 1.8 %add_convert_fusion = bf16[2,96,1536]{2,1,0:T(8,128)(2,1)S(1)} fusion(bf16[1,96,1536]{2,1,0:T(8,128)(2,1)} %bitcast.13, bf16[1,96,1536]{2,1,0:T(8,128)(2,1)S(1)} %bitcast.77, bf16[1,96,1536]{2,1,0:T(8,128)(2,1)} %bitcast.19, bf16[1,96,1536]{2,1,0:T(8,128)(2,1)} %bitcast.18, bf16[4,96,1536]{2,1,0:T(8,128)(2,1)} %collective-permute-done.1, ...), kind=kLoop, calls=%fused_computation | loop fusion | flops 3538944 | bytes 2949120 | tf_op jit(solution)/shard_map/convert_element_type | solution.py:367
  112.5 0.1 constant_dynamic-slice_fusion.3
  112.6 0.1 copy.23
  112.7 2.9 %collective-permute-start.10 = (bf16[2,24,1536]{2,0,1:T(2,128)(2,1)S(1)}, bf16[2,24,1536]{2,0,1:T(2,128)(2,1)S(1)}, u32[]{:S(2)}, u32[]{:S(2)}) collective-permute-start(bf16[2,24,1536]{2,0,1:T(2,128)(2,1)S(1)} %bitcast.78), channel_id=1, source_target_pairs={{0,96},{2,26},{8,104},{10,2},{16,112},{18,10},{24,120},{26,18},{32... | collective-permute-start | bytes 442376 | tf_op jit(solution)/shard_map/ppermute | solution.py:384
  115.7 0.1 copy.25
  115.8 0.9 collective-permute-start.8
  116.7 0.1 copy.24
  116.8 0.9 collective-permute-start.9
  117.8 1.2 broadcast_multiply_fusion
  119.0 0.0 collective-permute-done.10
  119.0 3.6 %collective-permute-done.8 = bf16[2,24,1536]{2,0,1:T(2,128)(2,1)S(1)} collective-permute-done((bf16[2,24,1536]{2,0,1:T(2,128)(2,1)S(1)}, bf16[2,24,1536]{2,0,1:T(2,128)(2,1)S(1)}, u32[]{:S(2)}, u32[]{:S(2)}) %collective-permute-start.8) | collective-permute-done | bytes 147488 | tf_op jit(solution)/shard_map/ppermute | solution.py:384
  122.6 1.5 %collective-permute-done.9 = bf16[2,24,1536]{2,0,1:T(2,128)(2,1)S(1)} collective-permute-done((bf16[2,24,1536]{2,0,1:T(2,128)(2,1)S(1)}, bf16[2,24,1536]{2,0,1:T(2,128)(2,1)S(1)}, u32[]{:S(2)}, u32[]{:S(2)}) %collective-permute-start.9) | collective-permute-done | bytes 147488 | tf_op jit(solution)/shard_map/ppermute | solution.py:384
  124.1 0.3 fusion.10
  124.4 0.1 dynamic-slice_bitcast_fusion.2
  124.5 3.4 %collective-permute-start.11 = (bf16[2,6,1536]{2,0,1:T(2,128)(2,1)S(1)}, bf16[2,6,1536]{2,0,1:T(2,128)(2,1)S(1)}, u32[]{:S(2)}, u32[]{:S(2)}) collective-permute-start(bf16[2,6,1536]{2,0,1:T(2,128)(2,1)S(1)} %get-tuple-element.70), channel_id=1, source_target_pairs={{0,16},{2,66},{8,24},{10,74},{16,0},{18,82},{24,8},{26,90},{32,48}... | collective-permute-start | bytes 110600 | tf_op jit(solution)/shard_map/ppermute | solution.py:384
  127.9 0.6 collective-permute-start.12
  128.5 2.7 %collective-permute-start.13 = (bf16[2,6,1536]{2,0,1:T(2,128)(2,1)S(1)}, bf16[2,6,1536]{2,0,1:T(2,128)(2,1)S(1)}, u32[]{:S(2)}, u32[]{:S(2)}) collective-permute-start(bf16[2,6,1536]{2,0,1:T(2,128)(2,1)S(1)} %get-tuple-element.71), channel_id=1, source_target_pairs={{0,24},{2,98},{8,0},{10,106},{16,8},{18,114},{24,16},{26,122},{32,... | collective-permute-start | bytes 110600 | tf_op jit(solution)/shard_map/ppermute | solution.py:384
  131.1 0.0 collective-permute-done.11
  131.1 1.9 %collective-permute-done.12 = bf16[2,6,1536]{2,0,1:T(2,128)(2,1)S(1)} collective-permute-done((bf16[2,6,1536]{2,0,1:T(2,128)(2,1)S(1)}, bf16[2,6,1536]{2,0,1:T(2,128)(2,1)S(1)}, u32[]{:S(2)}, u32[]{:S(2)}) %collective-permute-start.12) | collective-permute-done | bytes 36896 | tf_op jit(solution)/shard_map/ppermute | solution.py:384
  133.1 0.0 collective-permute-done.13
  133.1 0.1 fusion.13
  133.2 0.1 reshape.83
  133.3 0.7 copy.13
  133.9 0.6 copy.26
  (2 shorter events, 0.0 us)
Async XLA Ops:
  31.2 26.4 %all-to-all-start = ((bf16[16,64,768]{2,1,0:T(8,128)(2,1)}), bf16[16,64,768]{2,1,0:T(8,128)(2,1)S(1)}, u32[]{:S(2)}, u32[]{:S(2)}) async-start(bf16[16,64,768]{2,1,0:T(8,128)(2,1)} %bitcast.72), calls=%async_computation | async-start | bytes 3145728 | tf_op jit(solution)/shard_map/all_to_all | solution.py:340
  57.5 24.4 %all-to-all-start.2 = ((bf16[16,64,768]{2,1,0:T(8,128)(2,1)}), bf16[16,64,768]{2,1,0:T(8,128)(2,1)S(1)}, u32[]{:S(2)}, u32[]{:S(2)}) async-start(bf16[16,64,768]{2,1,0:T(8,128)(2,1)} %bitcast.74), calls=%async_computation.2 | async-start | bytes 3145728 | tf_op jit(solution)/shard_map/all_to_all | solution.py:340
  78.8 7.6 %collective-permute-start = (bf16[4,96,1536]{2,1,0:T(8,128)(2,1)}, bf16[4,96,1536]{2,1,0:T(8,128)(2,1)}, u32[]{:S(2)}, u32[]{:S(2)}) collective-permute-start(bf16[4,96,1536]{2,1,0:T(8,128)(2,1)} %get-tuple-element.39), channel_id=1, source_target_pairs={{0,2},{2,0},{1,3},{3,1},{4,6},{6,4},{5,7},{7,5},{8,10},{10,8},{9,1... | collective-permute-start | bytes 3538952 | tf_op jit(solution)/shard_map/ppermute | solution.py:345
  78.9 7.5 %collective-permute-start.1 = (bf16[4,96,1536]{2,1,0:T(8,128)(2,1)}, bf16[4,96,1536]{2,1,0:T(8,128)(2,1)}, u32[]{:S(2)}, u32[]{:S(2)}) collective-permute-start(bf16[4,96,1536]{2,1,0:T(8,128)(2,1)} %get-tuple-element.40), channel_id=1, source_target_pairs={{0,2},{2,0},{1,3},{3,1},{4,6},{6,4},{5,7},{7,5},{8,10},{10,8},{9,1... | collective-permute-start | bytes 3538952 | tf_op jit(solution)/shard_map/ppermute | solution.py:345
  81.9 28.7 %all-to-all-start.3 = ((bf16[16,64,768]{2,1,0:T(8,128)(2,1)}), bf16[16,64,768]{2,1,0:T(8,128)(2,1)S(1)}, u32[]{:S(2)}, u32[]{:S(2)}) async-start(bf16[16,64,768]{2,1,0:T(8,128)(2,1)} %bitcast.73), calls=%async_computation.3 | async-start | bytes 3145728 | tf_op jit(solution)/shard_map/all_to_all | solution.py:340
  86.4 4.8 %copy-start = (bf16[4,96,1536]{2,1,0:T(8,128)(2,1)S(1)}, bf16[4,96,1536]{2,1,0:T(8,128)(2,1)}, u32[]{:S(2)}) copy-start(bf16[4,96,1536]{2,1,0:T(8,128)(2,1)} %get-tuple-element.43) | copy-start | bytes 3538948
  87.9 11.6 %copy-start.1 = (bf16[4,96,1536]{2,1,0:T(8,128)(2,1)S(1)}, bf16[4,96,1536]{2,1,0:T(8,128)(2,1)}, u32[]{:S(2)}) copy-start(bf16[4,96,1536]{2,1,0:T(8,128)(2,1)} %get-tuple-element.38) | copy-start | bytes 3538948
  87.9 10.1 %collective-permute-start.4 = (bf16[96,1536]{1,0:T(8,128)(2,1)S(1)}, bf16[96,1536]{1,0:T(8,128)(2,1)S(1)}, u32[]{:S(2)}, u32[]{:S(2)}) collective-permute-start(bf16[96,1536]{1,0:T(8,128)(2,1)S(1)} %get-tuple-element.46), channel_id=1, source_target_pairs={{0,1},{1,4},{4,5},{5,0},{2,3},{3,6},{6,7},{7,2},{8,9},{9,12},{12,1... | collective-permute-start | bytes 884744 | tf_op jit(solution)/shard_map/ppermute | solution.py:345
  89.5 9.9 %collective-permute-start.6 = (bf16[96,1536]{1,0:T(8,128)(2,1)S(1)}, bf16[96,1536]{1,0:T(8,128)(2,1)S(1)}, u32[]{:S(2)}, u32[]{:S(2)}) collective-permute-start(bf16[96,1536]{1,0:T(8,128)(2,1)S(1)} %get-tuple-element.47), channel_id=1, source_target_pairs={{0,5},{1,0},{4,1},{5,4},{2,7},{3,2},{6,3},{7,6},{8,13},{9,8},{12,9... | collective-permute-start | bytes 884744 | tf_op jit(solution)/shard_map/ppermute | solution.py:345
  93.2 17.5 %collective-permute-start.2 = (bf16[96,1536]{1,0:T(8,128)(2,1)}, bf16[96,1536]{1,0:T(8,128)(2,1)S(1)}, u32[]{:S(2)}, u32[]{:S(2)}) collective-permute-start(bf16[96,1536]{1,0:T(8,128)(2,1)} %get-tuple-element.62), channel_id=1, source_target_pairs={{0,5},{1,0},{4,1},{5,4},{2,7},{3,2},{6,3},{7,6},{8,13},{9,8},{12,9... | collective-permute-start | bytes 884744 | tf_op jit(solution)/shard_map/ppermute | solution.py:345
  95.0 15.7 %collective-permute-start.3 = (bf16[96,1536]{1,0:T(8,128)(2,1)}, bf16[96,1536]{1,0:T(8,128)(2,1)}, u32[]{:S(2)}, u32[]{:S(2)}) collective-permute-start(bf16[96,1536]{1,0:T(8,128)(2,1)} %get-tuple-element.63), channel_id=1, source_target_pairs={{0,1},{1,4},{4,5},{5,0},{2,3},{3,6},{6,7},{7,2},{8,9},{9,12},{12,1... | collective-permute-start | bytes 884744 | tf_op jit(solution)/shard_map/ppermute | solution.py:345
  101.5 9.2 %collective-permute-start.5 = (bf16[96,1536]{1,0:T(8,128)(2,1)}, bf16[96,1536]{1,0:T(8,128)(2,1)}, u32[]{:S(2)}, u32[]{:S(2)}) collective-permute-start(bf16[96,1536]{1,0:T(8,128)(2,1)} %get-tuple-element.61), channel_id=1, source_target_pairs={{0,1},{1,4},{4,5},{5,0},{2,3},{3,6},{6,7},{7,2},{8,9},{9,12},{12,1... | collective-permute-start | bytes 884744 | tf_op jit(solution)/shard_map/ppermute | solution.py:345
  103.1 7.6 %collective-permute-start.7 = (bf16[96,1536]{1,0:T(8,128)(2,1)}, bf16[96,1536]{1,0:T(8,128)(2,1)}, u32[]{:S(2)}, u32[]{:S(2)}) collective-permute-start(bf16[96,1536]{1,0:T(8,128)(2,1)} %get-tuple-element.60), channel_id=1, source_target_pairs={{0,5},{1,0},{4,1},{5,4},{2,7},{3,2},{6,3},{7,6},{8,13},{9,8},{12,9... | collective-permute-start | bytes 884744 | tf_op jit(solution)/shard_map/ppermute | solution.py:345
  112.7 6.3 %collective-permute-start.10 = (bf16[2,24,1536]{2,0,1:T(2,128)(2,1)S(1)}, bf16[2,24,1536]{2,0,1:T(2,128)(2,1)S(1)}, u32[]{:S(2)}, u32[]{:S(2)}) collective-permute-start(bf16[2,24,1536]{2,0,1:T(2,128)(2,1)S(1)} %bitcast.78), channel_id=1, source_target_pairs={{0,96},{2,26},{8,104},{10,2},{16,112},{18,10},{24,120},{26,18},{32... | collective-permute-start | bytes 442376 | tf_op jit(solution)/shard_map/ppermute | solution.py:384
  115.8 6.8 %collective-permute-start.8 = (bf16[2,24,1536]{2,0,1:T(2,128)(2,1)S(1)}, bf16[2,24,1536]{2,0,1:T(2,128)(2,1)S(1)}, u32[]{:S(2)}, u32[]{:S(2)}) collective-permute-start(bf16[2,24,1536]{2,0,1:T(2,128)(2,1)S(1)} %bitcast.79), channel_id=1, source_target_pairs={{0,64},{2,18},{8,72},{10,26},{16,80},{18,2},{24,88},{26,10},{32,96... | collective-permute-start | bytes 442376 | tf_op jit(solution)/shard_map/ppermute | solution.py:384
  116.8 7.3 %collective-permute-start.9 = (bf16[2,24,1536]{2,0,1:T(2,128)(2,1)S(1)}, bf16[2,24,1536]{2,0,1:T(2,128)(2,1)S(1)}, u32[]{:S(2)}, u32[]{:S(2)}) collective-permute-start(bf16[2,24,1536]{2,0,1:T(2,128)(2,1)S(1)} %bitcast.80), channel_id=1, source_target_pairs={{0,32},{2,10},{8,40},{10,18},{16,48},{18,26},{24,56},{26,2},{32,64... | collective-permute-start | bytes 442376 | tf_op jit(solution)/shard_map/ppermute | solution.py:384
  124.5 6.7 %collective-permute-start.11 = (bf16[2,6,1536]{2,0,1:T(2,128)(2,1)S(1)}, bf16[2,6,1536]{2,0,1:T(2,128)(2,1)S(1)}, u32[]{:S(2)}, u32[]{:S(2)}) collective-permute-start(bf16[2,6,1536]{2,0,1:T(2,128)(2,1)S(1)} %get-tuple-element.70), channel_id=1, source_target_pairs={{0,16},{2,66},{8,24},{10,74},{16,0},{18,82},{24,8},{26,90},{32,48}... | collective-permute-start | bytes 110600 | tf_op jit(solution)/shard_map/ppermute | solution.py:384
  127.9 5.2 %collective-permute-start.12 = (bf16[2,6,1536]{2,0,1:T(2,128)(2,1)S(1)}, bf16[2,6,1536]{2,0,1:T(2,128)(2,1)S(1)}, u32[]{:S(2)}, u32[]{:S(2)}) collective-permute-start(bf16[2,6,1536]{2,0,1:T(2,128)(2,1)S(1)} %get-tuple-element.72), channel_id=1, source_target_pairs={{0,8},{2,34},{8,16},{10,42},{16,24},{18,50},{24,0},{26,58},{32,40}... | collective-permute-start | bytes 110600 | tf_op jit(solution)/shard_map/ppermute | solution.py:384
  128.5 4.6 %collective-permute-start.13 = (bf16[2,6,1536]{2,0,1:T(2,128)(2,1)S(1)}, bf16[2,6,1536]{2,0,1:T(2,128)(2,1)S(1)}, u32[]{:S(2)}, u32[]{:S(2)}) collective-permute-start(bf16[2,6,1536]{2,0,1:T(2,128)(2,1)S(1)} %get-tuple-element.71), channel_id=1, source_target_pairs={{0,24},{2,98},{8,0},{10,106},{16,8},{18,114},{24,16},{26,122},{32,... | collective-permute-start | bytes 110600 | tf_op jit(solution)/shard_map/ppermute | solution.py:384

commit v8 on v7

--- a/solution.py
+++ b/solution.py
@@ -383,7 +383,7 @@
             route.append((i, (x * 4 + z) * 2 + c))
         return lax.ppermute(piece(k), ("x", "z", "c"), route)
 
-    return total_of([piece(0)] + [sent(k) for k in (2, 1, 3)])
+    return total_of([piece(0)] + [sent(k) for k in (1, 3, 2)])
 
 
 def local(inputs, cotangent, conv, proj):

time: 135 us -> 134 us (level)
  waiting for transfers between devices: 25.5 us -> 23.4 us
    ppermute x6, waiting for transfers between devices: 7.01 us -> 4.84 us  [sent(): return lax.ppermute(piece(k), ('x', 'z', 'c'), route)]
  transfers between devices with their start and end apart: 17 -> 17, of which waited for: 9 -> 9; matrix products, arithmetic and copies ran while one was open for 6% -> 6% of each run, Pallas kernels for 24% -> 25%
where the time goes in v8:
time: 134 us; the launch traced here: 133 us
  starting transfers between devices  33.5 us (25%)
  Pallas kernels  32.8 us (24%)
  blocking collectives  30.5 us (23%)
  waiting for transfers between devices  23.4 us (17%)
  other arithmetic  10.3 us (8%)
  local copies, waits for them, and re-layouts  1.87 us (1%)
    pallas_call x2, Pallas kernels, staged_call(): pl.pallas_call(kernel, out_shape=[out_shape(i) for i, _ in results], in_s...  32.8 us
    all_to_all x1, blocking collectives, to_rings(): return lax.all_to_all(block, RING, 0, 0, tiled=True)  30.5 us
    all_to_all x3, waiting for transfers between devices, to_rings(): return lax.all_to_all(block, RING, 0, 0, tiled=True)  14.2 us
    ppermute x6, starting transfers between devices, sent(): return lax.ppermute(piece(k), ('x', 'z', 'c'), route)  12.2 us
    all_to_all x3, starting transfers between devices, to_rings(): return lax.all_to_all(block, RING, 0, 0, tiled=True)  12.2 us
    ppermute x8, starting transfers between devices, passed(): lax.ppermute(block, axis, [(i, (i + distance) % size) for i in range(size)])  9.15 us
    ppermute x6, waiting for transfers between devices, sent(): return lax.ppermute(piece(k), ('x', 'z', 'c'), route)  4.84 us
    ppermute x8, waiting for transfers between devices, passed(): lax.ppermute(block, axis, [(i, (i + distance) % size) for i in range(size)])  4.33 us
  transfers between devices with their start and end apart: 17, of which 9 were waited for; matrix products, arithmetic and copies ran while one was open for 6% of the time, Pallas kernels for 25%

profile of v8, /device:TPU:0, one launch (start us, length us, event | category | flops | bytes accessed | tf_op | source)
XLA Modules:
  0.0 133.1 jit_solution(17655082513259371592)
XLA Ops:
  0.6 30.5 %all_to_all.20 = bf16[16,64,768]{2,1,0:T(8,128)(2,1)S(1)} all-to-all(bf16[16,64,768]{2,1,0:T(8,128)(2,1)} %bitcast.71), channel_id=1, replica_groups=mesh['x'=4,'z'=4,'yh'=2,'c'=2,'yl'=2] {'x','z'}, dimensions={0} | all-to-all | bytes 3145728 | tf_op jit(solution)/shard_map/all_to_all | solution.py:340
  31.2 3.8 %all-to-all-start = ((bf16[16,64,768]{2,1,0:T(8,128)(2,1)}), bf16[16,64,768]{2,1,0:T(8,128)(2,1)S(1)}, u32[]{:S(2)}, u32[]{:S(2)}) async-start(bf16[16,64,768]{2,1,0:T(8,128)(2,1)} %bitcast.72), calls=%async_computation | async-start | bytes 3145728 | tf_op jit(solution)/shard_map/all_to_all | solution.py:340
  35.0 15.5 %forward.1 = (bf16[1024,768]{1,0:T(8,128)(2,1)}, bf16[1024,768]{1,0:T(8,128)(2,1)}, bf16[1024,768]{1,0:T(8,128)(2,1)}, bf16[1024,384]{1,0:T(8,128)(2,1)}, bf16[1...) custom-call(bf16[1024,768]{1,0:T(8,128)(2,1)S(1)} %bitcast.67, ...), custom_call_target="tpu_custom_call" | custom-call | flops 1 | bytes 1 | tf_op jit(solution)/shard_map/forward/pallas_call | solution.py:141
  50.5 7.0 %all-to-all-done = bf16[16,64,768]{2,1,0:T(8,128)(2,1)S(1)} async-done(((bf16[16,64,768]{2,1,0:T(8,128)(2,1)}), bf16[16,64,768]{2,1,0:T(8,128)(2,1)S(1)}, u32[]{:S(2)}, u32[]{:S(2)}) %all-to-all-start) | async-done | bytes 1572896 | tf_op jit(solution)/shard_map/all_to_all | solution.py:340
  57.5 3.9 %all-to-all-start.2 = ((bf16[16,64,768]{2,1,0:T(8,128)(2,1)}), bf16[16,64,768]{2,1,0:T(8,128)(2,1)S(1)}, u32[]{:S(2)}, u32[]{:S(2)}) async-start(bf16[16,64,768]{2,1,0:T(8,128)(2,1)} %bitcast.74), calls=%async_computation.2 | async-start | bytes 3145728 | tf_op jit(solution)/shard_map/all_to_all | solution.py:340
  61.4 0.1 pad_add_fusion.refs_0_
  61.5 17.3 %backward.1 = (bf16[1024,768]{1,0:T(8,128)(2,1)}, bf16[4,96,1536]{2,1,0:T(8,128)(2,1)}, bf16[4,96,1536]{2,1,0:T(8,128)(2,1)}, bf16[4,96,1536]{2,1,0:T(8,128)(2,1)}, bf16[4,96,1536]{2,1,0:T(8,128)(2,1)}) custom-call(s32[2]{0:T(128)S(1)} %pad_add_fusion.refs_0_, bf16[1024,768]{1,0:T(8,128)(2,1)S(1)} %bitcast.66, bf16[2,384,768]{2,1,0:T(8,128)(2,1)} %refs_8_.1, ...), custom_call_target="tpu_custom_call" | custom-call | flops 1 | bytes 1 | tf_op jit(solution)/shard_map/backward/pallas_call | solution.py:141
  78.8 0.1 collective-permute-start
  78.9 0.5 collective-permute-start.1
  79.4 2.6 %all-to-all-done.2 = bf16[16,64,768]{2,1,0:T(8,128)(2,1)S(1)} async-done(((bf16[16,64,768]{2,1,0:T(8,128)(2,1)}), bf16[16,64,768]{2,1,0:T(8,128)(2,1)S(1)}, u32[]{:S(2)}, u32[]{:S(2)}) %all-to-all-start.2) | async-done | bytes 1572896 | tf_op jit(solution)/shard_map/all_to_all | solution.py:340
  81.9 4.4 %all-to-all-start.3 = ((bf16[16,64,768]{2,1,0:T(8,128)(2,1)}), bf16[16,64,768]{2,1,0:T(8,128)(2,1)S(1)}, u32[]{:S(2)}, u32[]{:S(2)}) async-start(bf16[16,64,768]{2,1,0:T(8,128)(2,1)} %bitcast.73), calls=%async_computation.3 | async-start | bytes 3145728 | tf_op jit(solution)/shard_map/all_to_all | solution.py:340
  86.4 0.0 copy-start
  86.4 0.0 collective-permute-done
  86.4 0.0 collective-permute-done.1
  86.4 1.5 %fusion.3 = (bf16[96,1536]{1,0:T(8,128)(2,1)S(1)}, bf16[96,1536]{1,0:T(8,128)(2,1)S(1)}) fusion(bf16[4,96,1536]{2,1,0:T(8,128)(2,1)} %collective-permute-done, bf16[4,96,1536]{2,1,0:T(8,128)(2,1)} %get-tuple-element.43), kind=kLoop, calls=%fused_computation.15 | loop fusion | flops 1179648 | bytes 1769472 | tf_op jit(solution)/shard_map/convert_element_type | solution.py:356
  87.9 0.0 copy-start.1
  87.9 1.6 %collective-permute-start.4 = (bf16[96,1536]{1,0:T(8,128)(2,1)S(1)}, bf16[96,1536]{1,0:T(8,128)(2,1)S(1)}, u32[]{:S(2)}, u32[]{:S(2)}) collective-permute-start(bf16[96,1536]{1,0:T(8,128)(2,1)S(1)} %get-tuple-element.46), channel_id=1, source_target_pairs={{0,1},{1,4},{4,5},{5,0},{2,3},{3,6},{6,7},{7,2},{8,9},{9,12},{12,1... | collective-permute-start | bytes 884744 | tf_op jit(solution)/shard_map/ppermute | solution.py:345
  89.5 1.7 %collective-permute-start.6 = (bf16[96,1536]{1,0:T(8,128)(2,1)S(1)}, bf16[96,1536]{1,0:T(8,128)(2,1)S(1)}, u32[]{:S(2)}, u32[]{:S(2)}) collective-permute-start(bf16[96,1536]{1,0:T(8,128)(2,1)S(1)} %get-tuple-element.47), channel_id=1, source_target_pairs={{0,5},{1,0},{4,1},{5,4},{2,7},{3,2},{6,3},{7,6},{8,13},{9,8},{12,9... | collective-permute-start | bytes 884744 | tf_op jit(solution)/shard_map/ppermute | solution.py:345
  91.2 0.0 copy-done
  91.2 2.0 %fusion.4 = (bf16[96,1536]{1,0:T(8,128)(2,1)}, bf16[96,1536]{1,0:T(8,128)(2,1)}) fusion(bf16[4,96,1536]{2,1,0:T(8,128)(2,1)} %collective-permute-done, bf16[4,96,1536]{2,1,0:T(8,128)(2,1)S(1)} %copy-done), kind=kLoop, calls=%fused_computation.16 | loop fusion | flops 1179648 | bytes 1769472 | tf_op jit(solution)/shard_map/convert_element_type | solution.py:356
  93.2 1.8 %collective-permute-start.2 = (bf16[96,1536]{1,0:T(8,128)(2,1)}, bf16[96,1536]{1,0:T(8,128)(2,1)S(1)}, u32[]{:S(2)}, u32[]{:S(2)}) collective-permute-start(bf16[96,1536]{1,0:T(8,128)(2,1)} %get-tuple-element.62), channel_id=1, source_target_pairs={{0,5},{1,0},{4,1},{5,4},{2,7},{3,2},{6,3},{7,6},{8,13},{9,8},{12,9... | collective-permute-start | bytes 884744 | tf_op jit(solution)/shard_map/ppermute | solution.py:345
  95.0 0.2 collective-permute-start.3
  95.2 2.7 %collective-permute-done.4 = bf16[96,1536]{1,0:T(8,128)(2,1)S(1)} collective-permute-done((bf16[96,1536]{1,0:T(8,128)(2,1)S(1)}, bf16[96,1536]{1,0:T(8,128)(2,1)S(1)}, u32[]{:S(2)}, u32[]{:S(2)}) %collective-permute-start.4) | collective-permute-done | bytes 294944 | tf_op jit(solution)/shard_map/ppermute | solution.py:345
  97.9 1.5 %collective-permute-done.6 = bf16[96,1536]{1,0:T(8,128)(2,1)S(1)} collective-permute-done((bf16[96,1536]{1,0:T(8,128)(2,1)S(1)}, bf16[96,1536]{1,0:T(8,128)(2,1)S(1)}, u32[]{:S(2)}, u32[]{:S(2)}) %collective-permute-start.6) | collective-permute-done | bytes 294944 | tf_op jit(solution)/shard_map/ppermute | solution.py:345
  99.4 0.0 copy-done.1
  99.4 2.1 %fusion = (bf16[96,1536]{1,0:T(8,128)(2,1)}, bf16[96,1536]{1,0:T(8,128)(2,1)}) fusion(bf16[96,1536]{1,0:T(8,128)(2,1)S(1)} %collective-permute-done.6, bf16[4,96,1536]{2,1,0:T(8,128)(2,1)} %collective-permute-done.1, bf16[4,96,1536]{2,1,0:T(8,128)(2,1)S(1)} %copy-done.1, bf16[96,1536]{1,0:T(8,128)(2,1)S(1)} %collective-permute-done.4), kind=kLoop, calls=%fused_computation.5 | loop fusion | flops 2359296 | bytes 2359296 | tf_op jit(solution)/shard_map/convert_element_type | solution.py:365
  101.5 1.6 %collective-permute-start.5 = (bf16[96,1536]{1,0:T(8,128)(2,1)}, bf16[96,1536]{1,0:T(8,128)(2,1)}, u32[]{:S(2)}, u32[]{:S(2)}) collective-permute-start(bf16[96,1536]{1,0:T(8,128)(2,1)} %get-tuple-element.61), channel_id=1, source_target_pairs={{0,1},{1,4},{4,5},{5,0},{2,3},{3,6},{6,7},{7,2},{8,9},{9,12},{12,1... | collective-permute-start | bytes 884744 | tf_op jit(solution)/shard_map/ppermute | solution.py:345
  103.1 1.7 %collective-permute-start.7 = (bf16[96,1536]{1,0:T(8,128)(2,1)}, bf16[96,1536]{1,0:T(8,128)(2,1)}, u32[]{:S(2)}, u32[]{:S(2)}) collective-permute-start(bf16[96,1536]{1,0:T(8,128)(2,1)} %get-tuple-element.60), channel_id=1, source_target_pairs={{0,5},{1,0},{4,1},{5,4},{2,7},{3,2},{6,3},{7,6},{8,13},{9,8},{12,9... | collective-permute-start | bytes 884744 | tf_op jit(solution)/shard_map/ppermute | solution.py:345
  104.8 1.2 broadcast_multiply_fusion.1
  106.0 4.6 %all-to-all-done.3 = bf16[16,64,768]{2,1,0:T(8,128)(2,1)S(1)} async-done(((bf16[16,64,768]{2,1,0:T(8,128)(2,1)}), bf16[16,64,768]{2,1,0:T(8,128)(2,1)S(1)}, u32[]{:S(2)}, u32[]{:S(2)}) %all-to-all-start.3) | async-done | bytes 1572896 | tf_op jit(solution)/shard_map/all_to_all | solution.py:340
  110.6 0.1 collective-permute-done.5
  110.7 0.0 collective-permute-done.7
  110.7 0.0 collective-permute-done.2
  110.7 0.0 collective-permute-done.3
  110.7 1.8 %add_convert_fusion = bf16[2,96,1536]{2,1,0:T(8,128)(2,1)S(1)} fusion(bf16[1,96,1536]{2,1,0:T(8,128)(2,1)} %bitcast.13, bf16[1,96,1536]{2,1,0:T(8,128)(2,1)S(1)} %bitcast.77, bf16[1,96,1536]{2,1,0:T(8,128)(2,1)} %bitcast.19, bf16[1,96,1536]{2,1,0:T(8,128)(2,1)} %bitcast.18, bf16[4,96,1536]{2,1,0:T(8,128)(2,1)} %collective-permute-done.1, ...), kind=kLoop, calls=%fused_computation | loop fusion | flops 3538944 | bytes 2949120 | tf_op jit(solution)/shard_map/convert_element_type | solution.py:367
  112.5 0.1 constant_dynamic-slice_fusion.3
  112.6 0.1 copy.23
  112.7 3.2 %collective-permute-start.10 = (bf16[2,24,1536]{2,0,1:T(2,128)(2,1)S(1)}, bf16[2,24,1536]{2,0,1:T(2,128)(2,1)S(1)}, u32[]{:S(2)}, u32[]{:S(2)}) collective-permute-start(bf16[2,24,1536]{2,0,1:T(2,128)(2,1)S(1)} %bitcast.78), channel_id=1, source_target_pairs={{0,64},{2,18},{8,72},{10,26},{16,80},{18,2},{24,88},{26,10},{32,96... | collective-permute-start | bytes 442376 | tf_op jit(solution)/shard_map/ppermute | solution.py:384
  116.0 0.1 copy.25
  116.1 0.6 collective-permute-start.8
  116.7 0.1 copy.24
  116.8 2.7 %collective-permute-start.9 = (bf16[2,24,1536]{2,0,1:T(2,128)(2,1)S(1)}, bf16[2,24,1536]{2,0,1:T(2,128)(2,1)S(1)}, u32[]{:S(2)}, u32[]{:S(2)}) collective-permute-start(bf16[2,24,1536]{2,0,1:T(2,128)(2,1)S(1)} %bitcast.80), channel_id=1, source_target_pairs={{0,96},{2,26},{8,104},{10,2},{16,112},{18,10},{24,120},{26,18},{32... | collective-permute-start | bytes 442376 | tf_op jit(solution)/shard_map/ppermute | solution.py:384
  119.6 1.2 broadcast_multiply_fusion
  120.8 0.0 collective-permute-done.10
  120.8 1.7 %collective-permute-done.8 = bf16[2,24,1536]{2,0,1:T(2,128)(2,1)S(1)} collective-permute-done((bf16[2,24,1536]{2,0,1:T(2,128)(2,1)S(1)}, bf16[2,24,1536]{2,0,1:T(2,128)(2,1)S(1)}, u32[]{:S(2)}, u32[]{:S(2)}) %collective-permute-start.8) | collective-permute-done | bytes 147488 | tf_op jit(solution)/shard_map/ppermute | solution.py:384
  122.5 0.0 collective-permute-done.9
  122.5 0.3 fusion.10
  122.8 0.1 dynamic-slice_bitcast_fusion.2
  122.9 1.9 %collective-permute-start.11 = (bf16[2,6,1536]{2,0,1:T(2,128)(2,1)S(1)}, bf16[2,6,1536]{2,0,1:T(2,128)(2,1)S(1)}, u32[]{:S(2)}, u32[]{:S(2)}) collective-permute-start(bf16[2,6,1536]{2,0,1:T(2,128)(2,1)S(1)} %get-tuple-element.70), channel_id=1, source_target_pairs={{0,8},{2,34},{8,16},{10,42},{16,24},{18,50},{24,0},{26,58},{32,40}... | collective-permute-start | bytes 110600 | tf_op jit(solution)/shard_map/ppermute | solution.py:384
  124.8 1.4 %collective-permute-start.12 = (bf16[2,6,1536]{2,0,1:T(2,128)(2,1)S(1)}, bf16[2,6,1536]{2,0,1:T(2,128)(2,1)S(1)}, u32[]{:S(2)}, u32[]{:S(2)}) collective-permute-start(bf16[2,6,1536]{2,0,1:T(2,128)(2,1)S(1)} %get-tuple-element.72), channel_id=1, source_target_pairs={{0,24},{2,98},{8,0},{10,106},{16,8},{18,114},{24,16},{26,122},{32,... | collective-permute-start | bytes 110600 | tf_op jit(solution)/shard_map/ppermute | solution.py:384
  126.2 2.3 %collective-permute-start.13 = (bf16[2,6,1536]{2,0,1:T(2,128)(2,1)S(1)}, bf16[2,6,1536]{2,0,1:T(2,128)(2,1)S(1)}, u32[]{:S(2)}, u32[]{:S(2)}) collective-permute-start(bf16[2,6,1536]{2,0,1:T(2,128)(2,1)S(1)} %get-tuple-element.71), channel_id=1, source_target_pairs={{0,16},{2,66},{8,24},{10,74},{16,0},{18,82},{24,8},{26,90},{32,48}... | collective-permute-start | bytes 110600 | tf_op jit(solution)/shard_map/ppermute | solution.py:384
  128.5 0.0 collective-permute-done.11
  128.5 0.3 collective-permute-done.12
  128.8 2.9 %collective-permute-done.13 = bf16[2,6,1536]{2,0,1:T(2,128)(2,1)S(1)} collective-permute-done((bf16[2,6,1536]{2,0,1:T(2,128)(2,1)S(1)}, bf16[2,6,1536]{2,0,1:T(2,128)(2,1)S(1)}, u32[]{:S(2)}, u32[]{:S(2)}) %collective-permute-start.13) | collective-permute-done | bytes 36896 | tf_op jit(solution)/shard_map/ppermute | solution.py:384
  131.6 0.1 fusion.13
  131.7 0.1 reshape.83
  131.9 0.7 copy.13
  132.5 0.6 copy.26
  (2 shorter events, 0.0 us)
Async XLA Ops:
  31.2 26.4 %all-to-all-start = ((bf16[16,64,768]{2,1,0:T(8,128)(2,1)}), bf16[16,64,768]{2,1,0:T(8,128)(2,1)S(1)}, u32[]{:S(2)}, u32[]{:S(2)}) async-start(bf16[16,64,768]{2,1,0:T(8,128)(2,1)} %bitcast.72), calls=%async_computation | async-start | bytes 3145728 | tf_op jit(solution)/shard_map/all_to_all | solution.py:340
  57.5 24.4 %all-to-all-start.2 = ((bf16[16,64,768]{2,1,0:T(8,128)(2,1)}), bf16[16,64,768]{2,1,0:T(8,128)(2,1)S(1)}, u32[]{:S(2)}, u32[]{:S(2)}) async-start(bf16[16,64,768]{2,1,0:T(8,128)(2,1)} %bitcast.74), calls=%async_computation.2 | async-start | bytes 3145728 | tf_op jit(solution)/shard_map/all_to_all | solution.py:340
  78.8 7.6 %collective-permute-start = (bf16[4,96,1536]{2,1,0:T(8,128)(2,1)}, bf16[4,96,1536]{2,1,0:T(8,128)(2,1)}, u32[]{:S(2)}, u32[]{:S(2)}) collective-permute-start(bf16[4,96,1536]{2,1,0:T(8,128)(2,1)} %get-tuple-element.39), channel_id=1, source_target_pairs={{0,2},{2,0},{1,3},{3,1},{4,6},{6,4},{5,7},{7,5},{8,10},{10,8},{9,1... | collective-permute-start | bytes 3538952 | tf_op jit(solution)/shard_map/ppermute | solution.py:345
  78.9 7.5 %collective-permute-start.1 = (bf16[4,96,1536]{2,1,0:T(8,128)(2,1)}, bf16[4,96,1536]{2,1,0:T(8,128)(2,1)}, u32[]{:S(2)}, u32[]{:S(2)}) collective-permute-start(bf16[4,96,1536]{2,1,0:T(8,128)(2,1)} %get-tuple-element.40), channel_id=1, source_target_pairs={{0,2},{2,0},{1,3},{3,1},{4,6},{6,4},{5,7},{7,5},{8,10},{10,8},{9,1... | collective-permute-start | bytes 3538952 | tf_op jit(solution)/shard_map/ppermute | solution.py:345
  81.9 28.7 %all-to-all-start.3 = ((bf16[16,64,768]{2,1,0:T(8,128)(2,1)}), bf16[16,64,768]{2,1,0:T(8,128)(2,1)S(1)}, u32[]{:S(2)}, u32[]{:S(2)}) async-start(bf16[16,64,768]{2,1,0:T(8,128)(2,1)} %bitcast.73), calls=%async_computation.3 | async-start | bytes 3145728 | tf_op jit(solution)/shard_map/all_to_all | solution.py:340
  86.4 4.8 %copy-start = (bf16[4,96,1536]{2,1,0:T(8,128)(2,1)S(1)}, bf16[4,96,1536]{2,1,0:T(8,128)(2,1)}, u32[]{:S(2)}) copy-start(bf16[4,96,1536]{2,1,0:T(8,128)(2,1)} %get-tuple-element.43) | copy-start | bytes 3538948
  87.9 11.6 %copy-start.1 = (bf16[4,96,1536]{2,1,0:T(8,128)(2,1)S(1)}, bf16[4,96,1536]{2,1,0:T(8,128)(2,1)}, u32[]{:S(2)}) copy-start(bf16[4,96,1536]{2,1,0:T(8,128)(2,1)} %get-tuple-element.38) | copy-start | bytes 3538948
  87.9 10.1 %collective-permute-start.4 = (bf16[96,1536]{1,0:T(8,128)(2,1)S(1)}, bf16[96,1536]{1,0:T(8,128)(2,1)S(1)}, u32[]{:S(2)}, u32[]{:S(2)}) collective-permute-start(bf16[96,1536]{1,0:T(8,128)(2,1)S(1)} %get-tuple-element.46), channel_id=1, source_target_pairs={{0,1},{1,4},{4,5},{5,0},{2,3},{3,6},{6,7},{7,2},{8,9},{9,12},{12,1... | collective-permute-start | bytes 884744 | tf_op jit(solution)/shard_map/ppermute | solution.py:345
  89.5 9.9 %collective-permute-start.6 = (bf16[96,1536]{1,0:T(8,128)(2,1)S(1)}, bf16[96,1536]{1,0:T(8,128)(2,1)S(1)}, u32[]{:S(2)}, u32[]{:S(2)}) collective-permute-start(bf16[96,1536]{1,0:T(8,128)(2,1)S(1)} %get-tuple-element.47), channel_id=1, source_target_pairs={{0,5},{1,0},{4,1},{5,4},{2,7},{3,2},{6,3},{7,6},{8,13},{9,8},{12,9... | collective-permute-start | bytes 884744 | tf_op jit(solution)/shard_map/ppermute | solution.py:345
  93.2 17.5 %collective-permute-start.2 = (bf16[96,1536]{1,0:T(8,128)(2,1)}, bf16[96,1536]{1,0:T(8,128)(2,1)S(1)}, u32[]{:S(2)}, u32[]{:S(2)}) collective-permute-start(bf16[96,1536]{1,0:T(8,128)(2,1)} %get-tuple-element.62), channel_id=1, source_target_pairs={{0,5},{1,0},{4,1},{5,4},{2,7},{3,2},{6,3},{7,6},{8,13},{9,8},{12,9... | collective-permute-start | bytes 884744 | tf_op jit(solution)/shard_map/ppermute | solution.py:345
  95.0 15.7 %collective-permute-start.3 = (bf16[96,1536]{1,0:T(8,128)(2,1)}, bf16[96,1536]{1,0:T(8,128)(2,1)}, u32[]{:S(2)}, u32[]{:S(2)}) collective-permute-start(bf16[96,1536]{1,0:T(8,128)(2,1)} %get-tuple-element.63), channel_id=1, source_target_pairs={{0,1},{1,4},{4,5},{5,0},{2,3},{3,6},{6,7},{7,2},{8,9},{9,12},{12,1... | collective-permute-start | bytes 884744 | tf_op jit(solution)/shard_map/ppermute | solution.py:345
  101.5 9.2 %collective-permute-start.5 = (bf16[96,1536]{1,0:T(8,128)(2,1)}, bf16[96,1536]{1,0:T(8,128)(2,1)}, u32[]{:S(2)}, u32[]{:S(2)}) collective-permute-start(bf16[96,1536]{1,0:T(8,128)(2,1)} %get-tuple-element.61), channel_id=1, source_target_pairs={{0,1},{1,4},{4,5},{5,0},{2,3},{3,6},{6,7},{7,2},{8,9},{9,12},{12,1... | collective-permute-start | bytes 884744 | tf_op jit(solution)/shard_map/ppermute | solution.py:345
  103.1 7.6 %collective-permute-start.7 = (bf16[96,1536]{1,0:T(8,128)(2,1)}, bf16[96,1536]{1,0:T(8,128)(2,1)}, u32[]{:S(2)}, u32[]{:S(2)}) collective-permute-start(bf16[96,1536]{1,0:T(8,128)(2,1)} %get-tuple-element.60), channel_id=1, source_target_pairs={{0,5},{1,0},{4,1},{5,4},{2,7},{3,2},{6,3},{7,6},{8,13},{9,8},{12,9... | collective-permute-start | bytes 884744 | tf_op jit(solution)/shard_map/ppermute | solution.py:345
  112.7 8.1 %collective-permute-start.10 = (bf16[2,24,1536]{2,0,1:T(2,128)(2,1)S(1)}, bf16[2,24,1536]{2,0,1:T(2,128)(2,1)S(1)}, u32[]{:S(2)}, u32[]{:S(2)}) collective-permute-start(bf16[2,24,1536]{2,0,1:T(2,128)(2,1)S(1)} %bitcast.78), channel_id=1, source_target_pairs={{0,64},{2,18},{8,72},{10,26},{16,80},{18,2},{24,88},{26,10},{32,96... | collective-permute-start | bytes 442376 | tf_op jit(solution)/shard_map/ppermute | solution.py:384
  116.1 6.4 %collective-permute-start.8 = (bf16[2,24,1536]{2,0,1:T(2,128)(2,1)S(1)}, bf16[2,24,1536]{2,0,1:T(2,128)(2,1)S(1)}, u32[]{:S(2)}, u32[]{:S(2)}) collective-permute-start(bf16[2,24,1536]{2,0,1:T(2,128)(2,1)S(1)} %bitcast.79), channel_id=1, source_target_pairs={{0,32},{2,10},{8,40},{10,18},{16,48},{18,26},{24,56},{26,2},{32,64... | collective-permute-start | bytes 442376 | tf_op jit(solution)/shard_map/ppermute | solution.py:384
  116.8 5.7 %collective-permute-start.9 = (bf16[2,24,1536]{2,0,1:T(2,128)(2,1)S(1)}, bf16[2,24,1536]{2,0,1:T(2,128)(2,1)S(1)}, u32[]{:S(2)}, u32[]{:S(2)}) collective-permute-start(bf16[2,24,1536]{2,0,1:T(2,128)(2,1)S(1)} %bitcast.80), channel_id=1, source_target_pairs={{0,96},{2,26},{8,104},{10,2},{16,112},{18,10},{24,120},{26,18},{32... | collective-permute-start | bytes 442376 | tf_op jit(solution)/shard_map/ppermute | solution.py:384
  122.9 5.6 %collective-permute-start.11 = (bf16[2,6,1536]{2,0,1:T(2,128)(2,1)S(1)}, bf16[2,6,1536]{2,0,1:T(2,128)(2,1)S(1)}, u32[]{:S(2)}, u32[]{:S(2)}) collective-permute-start(bf16[2,6,1536]{2,0,1:T(2,128)(2,1)S(1)} %get-tuple-element.70), channel_id=1, source_target_pairs={{0,8},{2,34},{8,16},{10,42},{16,24},{18,50},{24,0},{26,58},{32,40}... | collective-permute-start | bytes 110600 | tf_op jit(solution)/shard_map/ppermute | solution.py:384
  124.8 4.0 %collective-permute-start.12 = (bf16[2,6,1536]{2,0,1:T(2,128)(2,1)S(1)}, bf16[2,6,1536]{2,0,1:T(2,128)(2,1)S(1)}, u32[]{:S(2)}, u32[]{:S(2)}) collective-permute-start(bf16[2,6,1536]{2,0,1:T(2,128)(2,1)S(1)} %get-tuple-element.72), channel_id=1, source_target_pairs={{0,24},{2,98},{8,0},{10,106},{16,8},{18,114},{24,16},{26,122},{32,... | collective-permute-start | bytes 110600 | tf_op jit(solution)/shard_map/ppermute | solution.py:384
  126.2 5.5 %collective-permute-start.13 = (bf16[2,6,1536]{2,0,1:T(2,128)(2,1)S(1)}, bf16[2,6,1536]{2,0,1:T(2,128)(2,1)S(1)}, u32[]{:S(2)}, u32[]{:S(2)}) collective-permute-start(bf16[2,6,1536]{2,0,1:T(2,128)(2,1)S(1)} %get-tuple-element.71), channel_id=1, source_target_pairs={{0,16},{2,66},{8,24},{10,74},{16,0},{18,82},{24,8},{26,90},{32,48}... | collective-permute-start | bytes 110600 | tf_op jit(solution)/shard_map/ppermute | solution.py:384

commit v9 on v8

--- a/solution.py
+++ b/solution.py
@@ -363,8 +363,9 @@
     right1, left0 = passed(right1, COLUMN, 1), passed(left0, COLUMN, -1)
     right0 = passed(total_of([right0, two0]).astype(BF), COLUMN, 1)
     left1 = passed(total_of([left1, two1]).astype(BF), COLUMN, -1)
+    near = lax.optimization_barrier(total_of([own, jnp.stack([left0, right1])]).astype(BF))
     right0, left1, beside = lax.optimization_barrier((right0, left1, beside))
-    return total_of([own, jnp.stack([left0, right1]), jnp.stack([right0, left1])]).astype(BF), beside
+    return total_of([near, jnp.stack([right0, left1])]).astype(BF), beside
 
 
 def ring_step(rows, second):

time: 134 us -> 132 us (0.985)
  other arithmetic: 10.3 us -> 8.25 us
  transfers between devices with their start and end apart: 17 -> 17, of which waited for: 9 -> 10; matrix products, arithmetic and copies ran while one was open for 6% -> 6% of each run, Pallas kernels for 25% -> 25%
where the time goes in v9:
time: 132 us; the launch traced here: 131 us
  starting transfers between devices  33.3 us (25%)
  Pallas kernels  32.8 us (25%)
  blocking collectives  30.5 us (23%)
  waiting for transfers between devices  23.8 us (18%)
  other arithmetic  8.25 us (6%)
  local copies, waits for them, and re-layouts  1.87 us (1%)
    pallas_call x2, Pallas kernels, staged_call(): pl.pallas_call(kernel, out_shape=[out_shape(i) for i, _ in results], in_s...  32.8 us
    all_to_all x1, blocking collectives, to_rings(): return lax.all_to_all(block, RING, 0, 0, tiled=True)  30.5 us
    all_to_all x3, waiting for transfers between devices, to_rings(): return lax.all_to_all(block, RING, 0, 0, tiled=True)  13.2 us
    all_to_all x3, starting transfers between devices, to_rings(): return lax.all_to_all(block, RING, 0, 0, tiled=True)  12.2 us
    ppermute x6, starting transfers between devices, sent(): return lax.ppermute(piece(k), ('x', 'z', 'c'), route)  11.6 us
    ppermute x8, starting transfers between devices, passed(): lax.ppermute(block, axis, [(i, (i + distance) % size) for i in range(size)])  9.51 us
    ppermute x6, waiting for transfers between devices, sent(): return lax.ppermute(piece(k), ('x', 'z', 'c'), route)  5.39 us
    ppermute x8, waiting for transfers between devices, passed(): lax.ppermute(block, axis, [(i, (i + distance) % size) for i in range(size)])  5.26 us
  transfers between devices with their start and end apart: 17, of which 10 were waited for; matrix products, arithmetic and copies ran while one was open for 6% of the time, Pallas kernels for 25%

profile of v9, /device:TPU:0, one launch (start us, length us, event | category | flops | bytes accessed | tf_op | source)
XLA Modules:
  0.0 131.3 jit_solution(7585864324753179125)
XLA Ops:
  0.6 30.5 %all_to_all.20 = bf16[16,64,768]{2,1,0:T(8,128)(2,1)S(1)} all-to-all(bf16[16,64,768]{2,1,0:T(8,128)(2,1)} %bitcast.71), channel_id=1, replica_groups=mesh['x'=4,'z'=4,'yh'=2,'c'=2,'yl'=2] {'x','z'}, dimensions={0} | all-to-all | bytes 3145728 | tf_op jit(solution)/shard_map/all_to_all | solution.py:340
  31.2 3.8 %all-to-all-start = ((bf16[16,64,768]{2,1,0:T(8,128)(2,1)}), bf16[16,64,768]{2,1,0:T(8,128)(2,1)S(1)}, u32[]{:S(2)}, u32[]{:S(2)}) async-start(bf16[16,64,768]{2,1,0:T(8,128)(2,1)} %bitcast.72), calls=%async_computation | async-start | bytes 3145728 | tf_op jit(solution)/shard_map/all_to_all | solution.py:340
  35.0 15.5 %forward.1 = (bf16[1024,768]{1,0:T(8,128)(2,1)}, bf16[1024,768]{1,0:T(8,128)(2,1)}, bf16[1024,768]{1,0:T(8,128)(2,1)}, bf16[1024,384]{1,0:T(8,128)(2,1)}, bf16[1...) custom-call(bf16[1024,768]{1,0:T(8,128)(2,1)S(1)} %bitcast.67, ...), custom_call_target="tpu_custom_call" | custom-call | flops 1 | bytes 1 | tf_op jit(solution)/shard_map/forward/pallas_call | solution.py:141
  50.5 7.0 %all-to-all-done = bf16[16,64,768]{2,1,0:T(8,128)(2,1)S(1)} async-done(((bf16[16,64,768]{2,1,0:T(8,128)(2,1)}), bf16[16,64,768]{2,1,0:T(8,128)(2,1)S(1)}, u32[]{:S(2)}, u32[]{:S(2)}) %all-to-all-start) | async-done | bytes 1572896 | tf_op jit(solution)/shard_map/all_to_all | solution.py:340
  57.5 3.9 %all-to-all-start.2 = ((bf16[16,64,768]{2,1,0:T(8,128)(2,1)}), bf16[16,64,768]{2,1,0:T(8,128)(2,1)S(1)}, u32[]{:S(2)}, u32[]{:S(2)}) async-start(bf16[16,64,768]{2,1,0:T(8,128)(2,1)} %bitcast.74), calls=%async_computation.2 | async-start | bytes 3145728 | tf_op jit(solution)/shard_map/all_to_all | solution.py:340
  61.4 0.1 pad_add_fusion.refs_0_
  61.5 17.3 %backward.1 = (bf16[1024,768]{1,0:T(8,128)(2,1)}, bf16[4,96,1536]{2,1,0:T(8,128)(2,1)}, bf16[4,96,1536]{2,1,0:T(8,128)(2,1)}, bf16[4,96,1536]{2,1,0:T(8,128)(2,1)}, bf16[4,96,1536]{2,1,0:T(8,128)(2,1)}) custom-call(s32[2]{0:T(128)S(1)} %pad_add_fusion.refs_0_, bf16[1024,768]{1,0:T(8,128)(2,1)S(1)} %bitcast.66, bf16[2,384,768]{2,1,0:T(8,128)(2,1)} %refs_8_.1, ...), custom_call_target="tpu_custom_call" | custom-call | flops 1 | bytes 1 | tf_op jit(solution)/shard_map/backward/pallas_call | solution.py:141
  78.8 0.1 collective-permute-start
  78.9 0.5 collective-permute-start.1
  79.4 2.6 %all-to-all-done.2 = bf16[16,64,768]{2,1,0:T(8,128)(2,1)S(1)} async-done(((bf16[16,64,768]{2,1,0:T(8,128)(2,1)}), bf16[16,64,768]{2,1,0:T(8,128)(2,1)S(1)}, u32[]{:S(2)}, u32[]{:S(2)}) %all-to-all-start.2) | async-done | bytes 1572896 | tf_op jit(solution)/shard_map/all_to_all | solution.py:340
  81.9 4.4 %all-to-all-start.3 = ((bf16[16,64,768]{2,1,0:T(8,128)(2,1)}), bf16[16,64,768]{2,1,0:T(8,128)(2,1)S(1)}, u32[]{:S(2)}, u32[]{:S(2)}) async-start(bf16[16,64,768]{2,1,0:T(8,128)(2,1)} %bitcast.73), calls=%async_computation.3 | async-start | bytes 3145728 | tf_op jit(solution)/shard_map/all_to_all | solution.py:340
  86.4 0.0 copy-start
  86.4 0.0 collective-permute-done
  86.4 0.0 collective-permute-done.1
  86.4 1.5 %fusion.3 = (bf16[96,1536]{1,0:T(8,128)(2,1)S(1)}, bf16[96,1536]{1,0:T(8,128)(2,1)S(1)}) fusion(bf16[4,96,1536]{2,1,0:T(8,128)(2,1)} %collective-permute-done, bf16[4,96,1536]{2,1,0:T(8,128)(2,1)} %get-tuple-element.43), kind=kLoop, calls=%fused_computation.16 | loop fusion | flops 1179648 | bytes 1769472 | tf_op jit(solution)/shard_map/convert_element_type | solution.py:356
  87.9 1.6 %collective-permute-start.4 = (bf16[96,1536]{1,0:T(8,128)(2,1)S(1)}, bf16[96,1536]{1,0:T(8,128)(2,1)S(1)}, u32[]{:S(2)}, u32[]{:S(2)}) collective-permute-start(bf16[96,1536]{1,0:T(8,128)(2,1)S(1)} %get-tuple-element.46), channel_id=1, source_target_pairs={{0,1},{1,4},{4,5},{5,0},{2,3},{3,6},{6,7},{7,2},{8,9},{9,12},{12,1... | collective-permute-start | bytes 884744 | tf_op jit(solution)/shard_map/ppermute | solution.py:345
  89.5 1.7 %collective-permute-start.6 = (bf16[96,1536]{1,0:T(8,128)(2,1)S(1)}, bf16[96,1536]{1,0:T(8,128)(2,1)S(1)}, u32[]{:S(2)}, u32[]{:S(2)}) collective-permute-start(bf16[96,1536]{1,0:T(8,128)(2,1)S(1)} %get-tuple-element.47), channel_id=1, source_target_pairs={{0,5},{1,0},{4,1},{5,4},{2,7},{3,2},{6,3},{7,6},{8,13},{9,8},{12,9... | collective-permute-start | bytes 884744 | tf_op jit(solution)/shard_map/ppermute | solution.py:345
  91.2 0.0 copy-done
  91.2 1.2 fusion.4
  92.4 2.1 %collective-permute-start.2 = (bf16[96,1536]{1,0:T(8,128)(2,1)S(1)}, bf16[96,1536]{1,0:T(8,128)(2,1)S(1)}, u32[]{:S(2)}, u32[]{:S(2)}) collective-permute-start(bf16[96,1536]{1,0:T(8,128)(2,1)S(1)} %get-tuple-element.62), channel_id=1, source_target_pairs={{0,5},{1,0},{4,1},{5,4},{2,7},{3,2},{6,3},{7,6},{8,13},{9,8},{12,9... | collective-permute-start | bytes 884744 | tf_op jit(solution)/shard_map/ppermute | solution.py:345
  94.4 0.0 copy-start.1
  94.4 0.2 collective-permute-start.3
  94.7 1.2 broadcast_multiply_fusion.1
  95.9 2.6 %collective-permute-done.4 = bf16[96,1536]{1,0:T(8,128)(2,1)S(1)} collective-permute-done((bf16[96,1536]{1,0:T(8,128)(2,1)S(1)}, bf16[96,1536]{1,0:T(8,128)(2,1)S(1)}, u32[]{:S(2)}, u32[]{:S(2)}) %collective-permute-start.4) | collective-permute-done | bytes 294944 | tf_op jit(solution)/shard_map/ppermute | solution.py:345
  98.6 0.9 collective-permute-done.6
  99.4 0.0 copy-done.1
  99.4 1.3 fusion
  100.7 1.7 %collective-permute-start.5 = (bf16[96,1536]{1,0:T(8,128)(2,1)S(1)}, bf16[96,1536]{1,0:T(8,128)(2,1)S(1)}, u32[]{:S(2)}, u32[]{:S(2)}) collective-permute-start(bf16[96,1536]{1,0:T(8,128)(2,1)S(1)} %get-tuple-element.61), channel_id=1, source_target_pairs={{0,1},{1,4},{4,5},{5,0},{2,3},{3,6},{6,7},{7,2},{8,9},{9,12},{12,1... | collective-permute-start | bytes 884744 | tf_op jit(solution)/shard_map/ppermute | solution.py:345
  102.4 1.7 %collective-permute-start.7 = (bf16[96,1536]{1,0:T(8,128)(2,1)S(1)}, bf16[96,1536]{1,0:T(8,128)(2,1)S(1)}, u32[]{:S(2)}, u32[]{:S(2)}) collective-permute-start(bf16[96,1536]{1,0:T(8,128)(2,1)S(1)} %get-tuple-element.60), channel_id=1, source_target_pairs={{0,5},{1,0},{4,1},{5,4},{2,7},{3,2},{6,3},{7,6},{8,13},{9,8},{12,9... | collective-permute-start | bytes 884744 | tf_op jit(solution)/shard_map/ppermute | solution.py:345
  104.0 1.7 %collective-permute-done.2 = bf16[96,1536]{1,0:T(8,128)(2,1)S(1)} collective-permute-done((bf16[96,1536]{1,0:T(8,128)(2,1)S(1)}, bf16[96,1536]{1,0:T(8,128)(2,1)S(1)}, u32[]{:S(2)}, u32[]{:S(2)}) %collective-permute-start.2) | collective-permute-done | bytes 294944 | tf_op jit(solution)/shard_map/ppermute | solution.py:345
  105.8 0.0 collective-permute-done.3
  105.8 1.3 add_convert_fusion.1
  107.0 3.6 %all-to-all-done.3 = bf16[16,64,768]{2,1,0:T(8,128)(2,1)S(1)} async-done(((bf16[16,64,768]{2,1,0:T(8,128)(2,1)}), bf16[16,64,768]{2,1,0:T(8,128)(2,1)S(1)}, u32[]{:S(2)}, u32[]{:S(2)}) %all-to-all-start.3) | async-done | bytes 1572896 | tf_op jit(solution)/shard_map/all_to_all | solution.py:340
  110.6 0.0 collective-permute-done.5
  110.6 0.0 collective-permute-done.7
  110.6 0.1 add_convert_fusion
  110.8 0.1 constant_dynamic-slice_fusion.3
  110.8 0.1 copy.23
  111.0 3.2 %collective-permute-start.10 = (bf16[2,24,1536]{2,0,1:T(2,128)(2,1)S(1)}, bf16[2,24,1536]{2,0,1:T(2,128)(2,1)S(1)}, u32[]{:S(2)}, u32[]{:S(2)}) collective-permute-start(bf16[2,24,1536]{2,0,1:T(2,128)(2,1)S(1)} %bitcast.81), channel_id=1, source_target_pairs={{0,64},{2,18},{8,72},{10,26},{16,80},{18,2},{24,88},{26,10},{32,96... | collective-permute-start | bytes 442376 | tf_op jit(solution)/shard_map/ppermute | solution.py:385
  114.1 0.1 copy.25
  114.3 0.6 collective-permute-start.8
  114.9 0.1 copy.24
  115.0 2.7 %collective-permute-start.9 = (bf16[2,24,1536]{2,0,1:T(2,128)(2,1)S(1)}, bf16[2,24,1536]{2,0,1:T(2,128)(2,1)S(1)}, u32[]{:S(2)}, u32[]{:S(2)}) collective-permute-start(bf16[2,24,1536]{2,0,1:T(2,128)(2,1)S(1)} %bitcast.83), channel_id=1, source_target_pairs={{0,96},{2,26},{8,104},{10,2},{16,112},{18,10},{24,120},{26,18},{32... | collective-permute-start | bytes 442376 | tf_op jit(solution)/shard_map/ppermute | solution.py:385
  117.7 1.2 broadcast_multiply_fusion
  119.0 0.0 collective-permute-done.10
  119.0 1.7 %collective-permute-done.8 = bf16[2,24,1536]{2,0,1:T(2,128)(2,1)S(1)} collective-permute-done((bf16[2,24,1536]{2,0,1:T(2,128)(2,1)S(1)}, bf16[2,24,1536]{2,0,1:T(2,128)(2,1)S(1)}, u32[]{:S(2)}, u32[]{:S(2)}) %collective-permute-start.8) | collective-permute-done | bytes 147488 | tf_op jit(solution)/shard_map/ppermute | solution.py:385
  120.7 0.0 collective-permute-done.9
  120.7 0.3 fusion.10
  121.0 0.1 dynamic-slice_bitcast_fusion.2
  121.0 1.5 %collective-permute-start.11 = (bf16[2,6,1536]{2,0,1:T(2,128)(2,1)S(1)}, bf16[2,6,1536]{2,0,1:T(2,128)(2,1)S(1)}, u32[]{:S(2)}, u32[]{:S(2)}) collective-permute-start(bf16[2,6,1536]{2,0,1:T(2,128)(2,1)S(1)} %get-tuple-element.70), channel_id=1, source_target_pairs={{0,8},{2,34},{8,16},{10,42},{16,24},{18,50},{24,0},{26,58},{32,40}... | collective-permute-start | bytes 110600 | tf_op jit(solution)/shard_map/ppermute | solution.py:385
  122.6 1.8 %collective-permute-start.12 = (bf16[2,6,1536]{2,0,1:T(2,128)(2,1)S(1)}, bf16[2,6,1536]{2,0,1:T(2,128)(2,1)S(1)}, u32[]{:S(2)}, u32[]{:S(2)}) collective-permute-start(bf16[2,6,1536]{2,0,1:T(2,128)(2,1)S(1)} %get-tuple-element.72), channel_id=1, source_target_pairs={{0,24},{2,98},{8,0},{10,106},{16,8},{18,114},{24,16},{26,122},{32,... | collective-permute-start | bytes 110600 | tf_op jit(solution)/shard_map/ppermute | solution.py:385
  124.4 1.8 %collective-permute-start.13 = (bf16[2,6,1536]{2,0,1:T(2,128)(2,1)S(1)}, bf16[2,6,1536]{2,0,1:T(2,128)(2,1)S(1)}, u32[]{:S(2)}, u32[]{:S(2)}) collective-permute-start(bf16[2,6,1536]{2,0,1:T(2,128)(2,1)S(1)} %get-tuple-element.71), channel_id=1, source_target_pairs={{0,16},{2,66},{8,24},{10,74},{16,0},{18,82},{24,8},{26,90},{32,48}... | collective-permute-start | bytes 110600 | tf_op jit(solution)/shard_map/ppermute | solution.py:385
  126.1 0.2 collective-permute-done.11
  126.3 0.3 collective-permute-done.12
  126.5 3.3 %collective-permute-done.13 = bf16[2,6,1536]{2,0,1:T(2,128)(2,1)S(1)} collective-permute-done((bf16[2,6,1536]{2,0,1:T(2,128)(2,1)S(1)}, bf16[2,6,1536]{2,0,1:T(2,128)(2,1)S(1)}, u32[]{:S(2)}, u32[]{:S(2)}) %collective-permute-start.13) | collective-permute-done | bytes 36896 | tf_op jit(solution)/shard_map/ppermute | solution.py:385
  129.8 0.1 fusion.13
  129.9 0.1 reshape.83
  130.0 0.7 copy.13
  130.7 0.6 copy.26
  (2 shorter events, 0.0 us)
Async XLA Ops:
  31.2 26.4 %all-to-all-start = ((bf16[16,64,768]{2,1,0:T(8,128)(2,1)}), bf16[16,64,768]{2,1,0:T(8,128)(2,1)S(1)}, u32[]{:S(2)}, u32[]{:S(2)}) async-start(bf16[16,64,768]{2,1,0:T(8,128)(2,1)} %bitcast.72), calls=%async_computation | async-start | bytes 3145728 | tf_op jit(solution)/shard_map/all_to_all | solution.py:340
  57.5 24.4 %all-to-all-start.2 = ((bf16[16,64,768]{2,1,0:T(8,128)(2,1)}), bf16[16,64,768]{2,1,0:T(8,128)(2,1)S(1)}, u32[]{:S(2)}, u32[]{:S(2)}) async-start(bf16[16,64,768]{2,1,0:T(8,128)(2,1)} %bitcast.74), calls=%async_computation.2 | async-start | bytes 3145728 | tf_op jit(solution)/shard_map/all_to_all | solution.py:340
  78.8 7.6 %collective-permute-start = (bf16[4,96,1536]{2,1,0:T(8,128)(2,1)}, bf16[4,96,1536]{2,1,0:T(8,128)(2,1)}, u32[]{:S(2)}, u32[]{:S(2)}) collective-permute-start(bf16[4,96,1536]{2,1,0:T(8,128)(2,1)} %get-tuple-element.39), channel_id=1, source_target_pairs={{0,2},{2,0},{1,3},{3,1},{4,6},{6,4},{5,7},{7,5},{8,10},{10,8},{9,1... | collective-permute-start | bytes 3538952 | tf_op jit(solution)/shard_map/ppermute | solution.py:345
  78.9 7.5 %collective-permute-start.1 = (bf16[4,96,1536]{2,1,0:T(8,128)(2,1)}, bf16[4,96,1536]{2,1,0:T(8,128)(2,1)}, u32[]{:S(2)}, u32[]{:S(2)}) collective-permute-start(bf16[4,96,1536]{2,1,0:T(8,128)(2,1)} %get-tuple-element.40), channel_id=1, source_target_pairs={{0,2},{2,0},{1,3},{3,1},{4,6},{6,4},{5,7},{7,5},{8,10},{10,8},{9,1... | collective-permute-start | bytes 3538952 | tf_op jit(solution)/shard_map/ppermute | solution.py:345
  81.9 28.7 %all-to-all-start.3 = ((bf16[16,64,768]{2,1,0:T(8,128)(2,1)}), bf16[16,64,768]{2,1,0:T(8,128)(2,1)S(1)}, u32[]{:S(2)}, u32[]{:S(2)}) async-start(bf16[16,64,768]{2,1,0:T(8,128)(2,1)} %bitcast.73), calls=%async_computation.3 | async-start | bytes 3145728 | tf_op jit(solution)/shard_map/all_to_all | solution.py:340
  86.4 4.8 %copy-start = (bf16[4,96,1536]{2,1,0:T(8,128)(2,1)S(1)}, bf16[4,96,1536]{2,1,0:T(8,128)(2,1)}, u32[]{:S(2)}) copy-start(bf16[4,96,1536]{2,1,0:T(8,128)(2,1)} %get-tuple-element.43) | copy-start | bytes 3538948
  87.9 10.7 %collective-permute-start.4 = (bf16[96,1536]{1,0:T(8,128)(2,1)S(1)}, bf16[96,1536]{1,0:T(8,128)(2,1)S(1)}, u32[]{:S(2)}, u32[]{:S(2)}) collective-permute-start(bf16[96,1536]{1,0:T(8,128)(2,1)S(1)} %get-tuple-element.46), channel_id=1, source_target_pairs={{0,1},{1,4},{4,5},{5,0},{2,3},{3,6},{6,7},{7,2},{8,9},{9,12},{12,1... | collective-permute-start | bytes 884744 | tf_op jit(solution)/shard_map/ppermute | solution.py:345
  89.5 9.9 %collective-permute-start.6 = (bf16[96,1536]{1,0:T(8,128)(2,1)S(1)}, bf16[96,1536]{1,0:T(8,128)(2,1)S(1)}, u32[]{:S(2)}, u32[]{:S(2)}) collective-permute-start(bf16[96,1536]{1,0:T(8,128)(2,1)S(1)} %get-tuple-element.47), channel_id=1, source_target_pairs={{0,5},{1,0},{4,1},{5,4},{2,7},{3,2},{6,3},{7,6},{8,13},{9,8},{12,9... | collective-permute-start | bytes 884744 | tf_op jit(solution)/shard_map/ppermute | solution.py:345
  92.4 13.4 %collective-permute-start.2 = (bf16[96,1536]{1,0:T(8,128)(2,1)S(1)}, bf16[96,1536]{1,0:T(8,128)(2,1)S(1)}, u32[]{:S(2)}, u32[]{:S(2)}) collective-permute-start(bf16[96,1536]{1,0:T(8,128)(2,1)S(1)} %get-tuple-element.62), channel_id=1, source_target_pairs={{0,5},{1,0},{4,1},{5,4},{2,7},{3,2},{6,3},{7,6},{8,13},{9,8},{12,9... | collective-permute-start | bytes 884744 | tf_op jit(solution)/shard_map/ppermute | solution.py:345
  94.4 5.0 %copy-start.1 = (bf16[4,96,1536]{2,1,0:T(8,128)(2,1)S(1)}, bf16[4,96,1536]{2,1,0:T(8,128)(2,1)}, u32[]{:S(2)}) copy-start(bf16[4,96,1536]{2,1,0:T(8,128)(2,1)} %get-tuple-element.38) | copy-start | bytes 3538948
  94.4 11.3 %collective-permute-start.3 = (bf16[96,1536]{1,0:T(8,128)(2,1)S(1)}, bf16[96,1536]{1,0:T(8,128)(2,1)S(1)}, u32[]{:S(2)}, u32[]{:S(2)}) collective-permute-start(bf16[96,1536]{1,0:T(8,128)(2,1)S(1)} %get-tuple-element.63), channel_id=1, source_target_pairs={{0,1},{1,4},{4,5},{5,0},{2,3},{3,6},{6,7},{7,2},{8,9},{9,12},{12,1... | collective-permute-start | bytes 884744 | tf_op jit(solution)/shard_map/ppermute | solution.py:345
  100.7 9.9 %collective-permute-start.5 = (bf16[96,1536]{1,0:T(8,128)(2,1)S(1)}, bf16[96,1536]{1,0:T(8,128)(2,1)S(1)}, u32[]{:S(2)}, u32[]{:S(2)}) collective-permute-start(bf16[96,1536]{1,0:T(8,128)(2,1)S(1)} %get-tuple-element.61), channel_id=1, source_target_pairs={{0,1},{1,4},{4,5},{5,0},{2,3},{3,6},{6,7},{7,2},{8,9},{9,12},{12,1... | collective-permute-start | bytes 884744 | tf_op jit(solution)/shard_map/ppermute | solution.py:345
  102.4 8.3 %collective-permute-start.7 = (bf16[96,1536]{1,0:T(8,128)(2,1)S(1)}, bf16[96,1536]{1,0:T(8,128)(2,1)S(1)}, u32[]{:S(2)}, u32[]{:S(2)}) collective-permute-start(bf16[96,1536]{1,0:T(8,128)(2,1)S(1)} %get-tuple-element.60), channel_id=1, source_target_pairs={{0,5},{1,0},{4,1},{5,4},{2,7},{3,2},{6,3},{7,6},{8,13},{9,8},{12,9... | collective-permute-start | bytes 884744 | tf_op jit(solution)/shard_map/ppermute | solution.py:345
  111.0 8.0 %collective-permute-start.10 = (bf16[2,24,1536]{2,0,1:T(2,128)(2,1)S(1)}, bf16[2,24,1536]{2,0,1:T(2,128)(2,1)S(1)}, u32[]{:S(2)}, u32[]{:S(2)}) collective-permute-start(bf16[2,24,1536]{2,0,1:T(2,128)(2,1)S(1)} %bitcast.81), channel_id=1, source_target_pairs={{0,64},{2,18},{8,72},{10,26},{16,80},{18,2},{24,88},{26,10},{32,96... | collective-permute-start | bytes 442376 | tf_op jit(solution)/shard_map/ppermute | solution.py:385
  114.3 6.4 %collective-permute-start.8 = (bf16[2,24,1536]{2,0,1:T(2,128)(2,1)S(1)}, bf16[2,24,1536]{2,0,1:T(2,128)(2,1)S(1)}, u32[]{:S(2)}, u32[]{:S(2)}) collective-permute-start(bf16[2,24,1536]{2,0,1:T(2,128)(2,1)S(1)} %bitcast.82), channel_id=1, source_target_pairs={{0,32},{2,10},{8,40},{10,18},{16,48},{18,26},{24,56},{26,2},{32,64... | collective-permute-start | bytes 442376 | tf_op jit(solution)/shard_map/ppermute | solution.py:385
  115.0 5.7 %collective-permute-start.9 = (bf16[2,24,1536]{2,0,1:T(2,128)(2,1)S(1)}, bf16[2,24,1536]{2,0,1:T(2,128)(2,1)S(1)}, u32[]{:S(2)}, u32[]{:S(2)}) collective-permute-start(bf16[2,24,1536]{2,0,1:T(2,128)(2,1)S(1)} %bitcast.83), channel_id=1, source_target_pairs={{0,96},{2,26},{8,104},{10,2},{16,112},{18,10},{24,120},{26,18},{32... | collective-permute-start | bytes 442376 | tf_op jit(solution)/shard_map/ppermute | solution.py:385
  121.0 5.2 %collective-permute-start.11 = (bf16[2,6,1536]{2,0,1:T(2,128)(2,1)S(1)}, bf16[2,6,1536]{2,0,1:T(2,128)(2,1)S(1)}, u32[]{:S(2)}, u32[]{:S(2)}) collective-permute-start(bf16[2,6,1536]{2,0,1:T(2,128)(2,1)S(1)} %get-tuple-element.70), channel_id=1, source_target_pairs={{0,8},{2,34},{8,16},{10,42},{16,24},{18,50},{24,0},{26,58},{32,40}... | collective-permute-start | bytes 110600 | tf_op jit(solution)/shard_map/ppermute | solution.py:385
  122.6 4.0 %collective-permute-start.12 = (bf16[2,6,1536]{2,0,1:T(2,128)(2,1)S(1)}, bf16[2,6,1536]{2,0,1:T(2,128)(2,1)S(1)}, u32[]{:S(2)}, u32[]{:S(2)}) collective-permute-start(bf16[2,6,1536]{2,0,1:T(2,128)(2,1)S(1)} %get-tuple-element.72), channel_id=1, source_target_pairs={{0,24},{2,98},{8,0},{10,106},{16,8},{18,114},{24,16},{26,122},{32,... | collective-permute-start | bytes 110600 | tf_op jit(solution)/shard_map/ppermute | solution.py:385
  124.4 5.5 %collective-permute-start.13 = (bf16[2,6,1536]{2,0,1:T(2,128)(2,1)S(1)}, bf16[2,6,1536]{2,0,1:T(2,128)(2,1)S(1)}, u32[]{:S(2)}, u32[]{:S(2)}) collective-permute-start(bf16[2,6,1536]{2,0,1:T(2,128)(2,1)S(1)} %get-tuple-element.71), channel_id=1, source_target_pairs={{0,16},{2,66},{8,24},{10,74},{16,0},{18,82},{24,8},{26,90},{32,48}... | collective-permute-start | bytes 110600 | tf_op jit(solution)/shard_map/ppermute | solution.py:385
